TPU v7x, 32 devices: a whole 2x2x4 slice. The times are simulated.
32 devices in a mesh: dp: 8 (over z, core), mp: 4 (over y, x).
Axes of the slice: x: 2, y: 2, z: 4, core: 2. Of those that a mesh axis runs over, the one named last changes fastest.
Arguments:
- inputs: bfloat16 [4096, 2048], P(('dp', 'mp')), may hold values from -6 to 6
- cotangent: bfloat16 [4096, 2048], P(('dp', 'mp')), may hold values from -6 to 6
- segment_ids: int32 [8, 512], P('dp'), may hold values from 0 to 3, never falling along the last dimension, each value on 1 to 170 neighbouring positions
- norm_gain: bfloat16 [2048], replicated, may hold values from 0.099609375 to 1.8984375
- branch_weight: bfloat16 [2048, 2560], P(None, 'mp'), may hold values from -0.125 to 0.125
- stream_weight: bfloat16 [2048, 2560], P(None, 'mp'), may hold values from -0.125 to 0.125
- conv_weight: bfloat16 [4, 2560], P(None, 'mp'), may hold values from -3 to 3
- conv_bias: bfloat16 [2560], P('mp'), may hold values from -3 to 3
- recur_weight: float32 [16, 160, 160], P('mp'), may hold values from -0.5 to 0.5
- recur_bias: float32 [2560], P('mp'), may hold values from -4 to 4
- intake_weight: float32 [16, 160, 160], P('mp'), may hold values from -0.5 to 0.5
- intake_bias: float32 [2560], P('mp'), may hold values from -4 to 4
- decay_param: float32 [2560], P('mp'), may hold values from 2 to 7.5
- output_weight: bfloat16 [2560, 2048], P('mp'), may hold values from -0.3125 to 0.3125
- mlp_gain: bfloat16 [2048], replicated, may hold values from 0.099609375 to 1.8984375
- gate_weight: bfloat16 [2048, 6144], P(None, 'mp'), may hold values from -0.125 to 0.125
- up_weight: bfloat16 [2048, 6144], P(None, 'mp'), may hold values from -0.125 to 0.125
- down_weight: bfloat16 [6144, 2048], P('mp'), may hold values from -0.109375 to 0.109375
Outputs:
- block_out: bfloat16 [4096, 2048], P(('dp', 'mp'))
- inputs_grad: bfloat16 [4096, 2048], P(('dp', 'mp'))
- norm_gain_grad: float32 [2048], replicated
- branch_weight_grad: float32 [2048, 2560], P(None, 'mp')
- stream_weight_grad: float32 [2048, 2560], P(None, 'mp')
- conv_weight_grad: float32 [4, 2560], P(None, 'mp')
- conv_bias_grad: float32 [2560], P('mp')
- recur_weight_grad: float32 [16, 160, 160], P('mp')
- recur_bias_grad: float32 [2560], P('mp')
- intake_weight_grad: float32 [16, 160, 160], P('mp')
- intake_bias_grad: float32 [2560], P('mp')
- decay_param_grad: float32 [2560], P('mp')
- output_weight_grad: float32 [2560, 2048], P('mp')
- mlp_gain_grad: float32 [2048], replicated
- gate_weight_grad: float32 [2048, 6144], P(None, 'mp')
- up_weight_grad: float32 [2048, 6144], P(None, 'mp')
- down_weight_grad: float32 [6144, 2048], P('mp')
Inputs may be any that keep to these rules, and one draw needn't show every extreme that they name: `segment_ids`: along each packed row the ids never fall; each id names 1 to 170 consecutive tokens and some segment has exactly that many.
All inputs are finite; a program needn't handle non-finite values.
Results may differ from a plain program's by a relative error of at most 0.019.
Values may be sent and summed in bfloat16 or wider, within the bound.
No kernel may reach another device: no remote copies, remote signals or barrier semaphores. Data moves between devices by JAX's collectives and lax.ppermute only.
A program may use at most 256 MiB of HBM per device.

v0:
```python
import jax
import jax.numpy as jnp
from jax import lax
from jax.sharding import PartitionSpec as P

eps = 1e-06
decay_scale = 8.0
contract_rows = (((0,), (0,)), ((), ()))
contract_cols = (((1,), (1,)), ((), ()))


def rms_scale(values, gain):
    return values * lax.rsqrt(jnp.mean(values * values, axis=-1, keepdims=True) + eps) * gain


def combine(earlier, later):
    return (earlier[0] * later[0], later[0] * earlier[1] + later[1])


def recurrence(
    stream,
    seg_row,
    conv_weight,
    conv_bias,
    recur_weight,
    recur_bias,
    intake_weight,
    intake_bias,
    decay_param,
):
    length = stream.shape[0]
    channels = stream.shape[1]
    head_count = recur_weight.shape[0]
    head_size = recur_weight.shape[1]
    convolved = conv_bias[None, :] + conv_weight[0][None, :] * stream
    linked = jnp.zeros((length,), jnp.float32)
    for offset in range(1, conv_weight.shape[0]):
        earlier = jnp.concatenate([jnp.full((offset,), -1, jnp.int32), seg_row[:-offset]])
        joined = (seg_row == earlier).astype(jnp.float32)
        if offset == 1:
            linked = joined
        shifted = jnp.concatenate(
            [jnp.zeros((offset, channels), jnp.float32), stream[:-offset]], axis=0
        )
        convolved = convolved + conv_weight[offset][None, :] * shifted * joined[:, None]
    grouped = convolved.reshape(length, head_count, head_size)
    recur_gate = jax.nn.sigmoid(
        jnp.einsum("thi,hij->thj", grouped, recur_weight, precision=lax.Precision.HIGHEST).reshape(
            length, channels
        )
        + recur_bias[None, :]
    )
    intake_gate = jax.nn.sigmoid(
        jnp.einsum("thi,hij->thj", grouped, intake_weight, precision=lax.Precision.HIGHEST).reshape(
            length, channels
        )
        + intake_bias[None, :]
    )
    log_decay = -decay_scale * recur_gate * jax.nn.softplus(-decay_param)[None, :]
    link_col = linked[:, None]
    multiplier = link_col * jnp.sqrt(-jnp.expm1(2.0 * log_decay)) + (1.0 - link_col)
    carried = link_col * jnp.exp(log_decay)
    driven = multiplier * intake_gate * convolved
    products, state = lax.associative_scan(combine, (carried, driven), axis=0)
    return state


def gated_gelu(gate_pre, up_pre):
    return jax.nn.gelu(gate_pre) * up_pre


def local(
    inputs,
    cotangent,
    segment_ids,
    norm_gain,
    branch_weight,
    stream_weight,
    conv_weight,
    conv_bias,
    recur_weight,
    recur_bias,
    intake_weight,
    intake_bias,
    decay_param,
    output_weight,
    mlp_gain,
    gate_weight,
    up_weight,
    down_weight,
):
    seg_row = segment_ids[0]
    resid = inputs.astype(jnp.float32)
    normed, norm_back = jax.vjp(rms_scale, resid, norm_gain.astype(jnp.float32))
    normed_all = lax.all_gather(normed.astype(jnp.bfloat16), "mp", axis=0, tiled=True)
    branch_pre = jnp.dot(normed_all, branch_weight, preferred_element_type=jnp.float32)
    stream_pre = jnp.dot(normed_all, stream_weight, preferred_element_type=jnp.float32)
    small_params = (
        conv_weight.astype(jnp.float32),
        conv_bias.astype(jnp.float32),
        recur_weight,
        recur_bias,
        intake_weight,
        intake_bias,
        decay_param,
    )

    def gated_branch(branch_in, stream_in, weights):
        return jax.nn.gelu(branch_in) * recurrence(stream_in, seg_row, *weights)

    gated, gated_back = jax.vjp(gated_branch, branch_pre, stream_pre, small_params)
    gated_low = gated.astype(jnp.bfloat16)
    piece = gated_low
    mixer = lax.psum_scatter(
        jnp.dot(piece, output_weight, preferred_element_type=jnp.float32),
        "mp",
        scatter_dimension=0,
        tiled=True,
    )
    hidden_resid = resid + mixer
    normed_two, norm_two_back = jax.vjp(rms_scale, hidden_resid, mlp_gain.astype(jnp.float32))
    mlp_in = lax.all_gather(normed_two.astype(jnp.bfloat16), "mp", axis=0, tiled=True)
    gate_pre = jnp.dot(mlp_in, gate_weight, preferred_element_type=jnp.float32)
    up_pre = jnp.dot(mlp_in, up_weight, preferred_element_type=jnp.float32)
    activ, activ_back = jax.vjp(gated_gelu, gate_pre, up_pre)
    activ_low = activ.astype(jnp.bfloat16)
    piece = activ_low
    mlp_out = lax.psum_scatter(
        jnp.dot(piece, down_weight, preferred_element_type=jnp.float32).astype(jnp.bfloat16),
        "mp",
        scatter_dimension=0,
        tiled=True,
    ).astype(jnp.float32)
    block_out = (hidden_resid + mlp_out).astype(jnp.bfloat16)
    cot_all = lax.all_gather(cotangent, "mp", axis=0, tiled=True)
    activ_grad = lax.dot_general(
        cot_all, down_weight, contract_cols, preferred_element_type=jnp.float32
    )
    gate_grad, up_grad = activ_back(activ_grad)
    gate_low = gate_grad.astype(jnp.bfloat16)
    up_low = up_grad.astype(jnp.bfloat16)
    down_weight_grad = lax.dot_general(
        activ_low, cot_all, contract_rows, preferred_element_type=jnp.float32
    )
    gate_weight_grad = lax.dot_general(
        mlp_in, gate_low, contract_rows, preferred_element_type=jnp.float32
    )
    up_weight_grad = lax.dot_general(
        mlp_in, up_low, contract_rows, preferred_element_type=jnp.float32
    )
    normed_two_grad = lax.psum_scatter(
        (
            lax.dot_general(
                gate_low, gate_weight, contract_cols, preferred_element_type=jnp.float32
            )
            + lax.dot_general(up_low, up_weight, contract_cols, preferred_element_type=jnp.float32)
        ).astype(jnp.bfloat16),
        "mp",
        scatter_dimension=0,
        tiled=True,
    ).astype(jnp.float32)
    hidden_part, mlp_gain_grad = norm_two_back(normed_two_grad)
    resid_grad = cotangent.astype(jnp.float32) + hidden_part
    branch_cot = lax.all_gather(resid_grad.astype(jnp.bfloat16), "mp", axis=0, tiled=True)
    output_weight_grad = lax.dot_general(
        gated_low, branch_cot, contract_rows, preferred_element_type=jnp.float32
    )
    gated_grad = lax.dot_general(
        branch_cot, output_weight, contract_cols, preferred_element_type=jnp.float32
    )
    branch_grad, stream_grad, param_grads = gated_back(gated_grad)
    branch_low = branch_grad.astype(jnp.bfloat16)
    stream_low = stream_grad.astype(jnp.bfloat16)
    branch_weight_grad = lax.dot_general(
        normed_all, branch_low, contract_rows, preferred_element_type=jnp.float32
    )
    stream_weight_grad = lax.dot_general(
        normed_all, stream_low, contract_rows, preferred_element_type=jnp.float32
    )
    normed_grad = lax.psum_scatter(
        (
            lax.dot_general(
                branch_low, branch_weight, contract_cols, preferred_element_type=jnp.float32
            )
            + lax.dot_general(
                stream_low, stream_weight, contract_cols, preferred_element_type=jnp.float32
            )
        ).astype(jnp.bfloat16),
        "mp",
        scatter_dimension=0,
        tiled=True,
    ).astype(jnp.float32)
    input_part, norm_gain_grad = norm_back(normed_grad)
    inputs_grad = (resid_grad + input_part).astype(jnp.bfloat16)
    (
        conv_weight_grad,
        conv_bias_grad,
        recur_weight_grad,
        recur_bias_grad,
        intake_weight_grad,
        intake_bias_grad,
        decay_param_grad,
    ) = param_grads
    summed = (
        lax.psum(branch_weight_grad.astype(jnp.bfloat16), "dp").astype(jnp.float32),
        lax.psum(stream_weight_grad.astype(jnp.bfloat16), "dp").astype(jnp.float32),
        lax.psum(conv_weight_grad.astype(jnp.bfloat16), "dp").astype(jnp.float32),
        lax.psum(conv_bias_grad.astype(jnp.bfloat16), "dp").astype(jnp.float32),
        lax.psum(recur_weight_grad.astype(jnp.bfloat16), "dp").astype(jnp.float32),
        lax.psum(recur_bias_grad.astype(jnp.bfloat16), "dp").astype(jnp.float32),
        lax.psum(intake_weight_grad.astype(jnp.bfloat16), "dp").astype(jnp.float32),
        lax.psum(intake_bias_grad.astype(jnp.bfloat16), "dp").astype(jnp.float32),
        lax.psum(decay_param_grad.astype(jnp.bfloat16), "dp").astype(jnp.float32),
        lax.psum(output_weight_grad.astype(jnp.bfloat16), "dp").astype(jnp.float32),
        lax.psum(norm_gain_grad.astype(jnp.bfloat16), "dp").astype(jnp.float32),
        lax.psum(gate_weight_grad.astype(jnp.bfloat16), "dp").astype(jnp.float32),
        lax.psum(up_weight_grad.astype(jnp.bfloat16), "dp").astype(jnp.float32),
        lax.psum(down_weight_grad.astype(jnp.bfloat16), "dp").astype(jnp.float32),
        lax.psum(mlp_gain_grad.astype(jnp.bfloat16), "dp").astype(jnp.float32),
    )
    gain_totals = lax.psum((summed[10], summed[14]), "mp")
    return (
        block_out,
        inputs_grad,
        gain_totals[0],
        summed[0],
        summed[1],
        summed[2],
        summed[3],
        summed[4],
        summed[5],
        summed[6],
        summed[7],
        summed[8],
        summed[9],
        gain_totals[1],
        summed[11],
        summed[12],
        summed[13],
    )


def solution(mesh):
    placed = (
        P(("dp", "mp"), None),
        P(("dp", "mp"), None),
        P("dp", None),
        P(),
        P(None, "mp"),
        P(None, "mp"),
        P(None, "mp"),
        P("mp"),
        P("mp", None, None),
        P("mp"),
        P("mp", None, None),
        P("mp"),
        P("mp"),
        P("mp", None),
        P(),
        P(None, "mp"),
        P(None, "mp"),
        P("mp", None),
    )
    return jax.shard_map(
        local,
        mesh=mesh,
        in_specs=placed,
        out_specs=(
            P(("dp", "mp"), None),
            P(("dp", "mp"), None),
            P(),
            P(None, "mp"),
            P(None, "mp"),
            P(None, "mp"),
            P("mp"),
            P("mp", None, None),
            P("mp"),
            P("mp", None, None),
            P("mp"),
            P("mp"),
            P("mp", None),
            P(),
            P(None, "mp"),
            P(None, "mp"),
            P("mp", None),
        ),
        check_vma=False,
    )
```

profile of v0, /device:TPU:0, one launch (start us, length us, event | category | flops | bytes accessed | tf_op | source)
XLA Modules:
  0.0 1278.7 jit_solution(9425923390953606947)
XLA Ops:
  12.4 37.8 %all-gather.5.cloned.1.call-done = bf16[512,2048]{1,0:T(8,128)(2,1)} async-done(((bf16[128,2048]{1,0:T(8,128)(2,1)}), bf16[512,2048]{1,0:T(8,128)(2,1)}) %all-gather.5.cloned.1.call-update) | async-done | bytes 2097168 | tf_op jit(solution)/shard_map/all_gather | solution.py:95
  50.2 4.2 fusion.97
  57.4 2.8 copy.46
  60.2 4.2 fusion.99
  64.4 2.9 copy.50
  67.3 4.2 fusion.98
  71.5 2.8 copy.48
  74.4 4.9 exponential_multiply_fusion
  79.2 3.3 slice.325
  82.6 4.5 slice.329
  87.0 4.3 slice.324
  92.0 4.2 slice.326
  96.3 4.3 slice.389
  100.5 4.2 slice.327
  151.1 2.8 pad.373
  156.3 2.9 pad.374
  159.2 4.8 pad.375
  164.0 5.9 multiply_convert_fusion.2
  170.8 3.8 fusion.100
  175.3 52.2 %reduce-scatter.5.cloned.1.call-done = f32[128,2048]{1,0:T(8,128)} async-done(((f32[512,2048]{1,0:T(8,128)}), f32[128,2048]{1,0:T(8,128)}) %reduce-scatter.5.cloned.1.call-update) | async-done | bytes 1048592 | tf_op jit(solution)/shard_map/reduce_scatter | solution.py:114
  231.9 34.4 %all-gather.7.cloned.1.call-done = bf16[512,2048]{1,0:T(8,128)(2,1)} async-done(((bf16[128,2048]{1,0:T(8,128)(2,1)}), bf16[512,2048]{1,0:T(8,128)(2,1)}) %all-gather.7.cloned.1.call-update) | async-done | bytes 2097168 | tf_op jit(solution)/shard_map/all_gather | solution.py:122
  266.4 8.6 fusion.102
  275.0 8.2 fusion.101
  283.2 20.4 %all-gather.9.cloned.1.call-done = bf16[512,2048]{1,0:T(8,128)(2,1)} async-done(((bf16[128,2048]{1,0:T(8,128)(2,1)}), bf16[512,2048]{1,0:T(8,128)(2,1)}) %all-gather.9.cloned.1.call-update) | async-done | bytes 2097168 | tf_op jit(solution)/shard_map/all_gather | solution.py:135
  303.6 12.0 multiply_convert_fusion
  315.6 6.7 fusion.103
  322.4 4.6 add_convert_fusion.1
  327.1 35.3 %reduce-scatter.9.cloned.1.call-done = bf16[128,2048]{1,0:T(8,128)(2,1)} async-done(((bf16[512,2048]{1,0:T(8,128)(2,1)}), bf16[128,2048]{1,0:T(8,128)(2,1)}) %reduce-scatter.9.cloned.1.call-update) | async-done | bytes 524304 | tf_op jit(solution)/shard_map/reduce_scatter | solution.py:151
  367.4 35.2 %all-gather.11.cloned.1.call-done = bf16[512,2048]{1,0:T(8,128)(2,1)} async-done(((bf16[128,2048]{1,0:T(8,128)(2,1)}), bf16[512,2048]{1,0:T(8,128)(2,1)}) %all-gather.11.cloned.1.call-update) | async-done | bytes 2097168 | tf_op jit(solution)/shard_map/all_gather | solution.py:164
  402.6 6.5 fusion.30
  410.8 4.2 slice.390
  415.0 3.1 fusion.72
  418.1 4.2 slice.391
  532.0 2.8 pad.383
  544.9 4.0 multiply_add_fusion.4
  550.7 5.0 pad.434
  555.7 4.9 pad.378
  560.6 4.9 pad.459
  565.5 4.9 pad.435
  570.4 4.8 pad.460
  575.3 4.9 pad.436
  580.3 6.1 multiply_reduce_fusion
  586.5 3.3 fusion.66
  589.8 2.8 copy.52
  595.3 2.9 fusion.105
  600.7 2.8 copy.53
  603.6 4.6 multiply_reduce_fusion.4
  615.8 3.1 add_convert_fusion
  619.0 8.0 convolution_convert_fusion.6
  627.1 8.4 convolution_convert_fusion
  635.5 5.5 convolution_convert_fusion.1
  641.0 5.4 convolution_convert_fusion.2
  650.6 3.1 convolution_convert_fusion.3
  653.7 3.3 convolution_convert_fusion.5
  657.1 3.3 convolution_convert_fusion.4
  662.7 28.9 %all-reduce.98 = (bf16[2048]{0:T(1024)(128)(2,1)S(1)}, bf16[2048]{0:T(1024)(128)(2,1)S(1)}, bf16[4,640]{1,0:T(4,128)(2,1)S(1)}, bf16[640]{0:T(1024)(128)(2,1)S(1...) all-reduce(bf16[2048]{0:T(1024)(128)(2,1)S(1)} %get-tuple-element.2, ...), channel_id=1, replica_groups=mesh['dp'=8,'mp'=4] {'dp'}, use_global_device_ids=true, to_apply=%region_9.10 | all-reduce | flops 9216 | bytes 36864 | tf_op jit(solution)/shard_map/psum | solution.py:215
  694.6 15.6 %all-reduce.97 = (f32[2048]{0:T(1024)}, f32[2048]{0:T(1024)}) all-reduce(bf16[2048]{0:T(1024)(128)(2,1)S(1)} %get-tuple-element.29, bf16[2048]{0:T(1024)(128)(2,1)S(1)} %get-tuple-element.30), channel_id=1, replica_groups=mesh['dp'=8,'mp'=4] {'mp'}, use_global_device_ids=true, to_apply=%region_10.11 | all-reduce | flops 4096 | bytes 24576 | tf_op jit(solution)/shard_map/psum | solution.py:221
  710.4 3.4 fusion.26
  713.8 521.6 %all-reduce.102.cloned.1.call-done = (bf16[2048,640]{1,0:T(8,128)(2,1)}, bf16[2048,640]{1,0:T(8,128)(2,1)}, bf16[4,160,160]{2,1,0:T(8,128)(2,1)}, bf16[4,160,160...) async-done(((bf16[2048,640]{1,0:T(8,128)(2,1)}, ...) | async-done | bytes 27148304 | tf_op jit(solution)/shard_map/psum | solution.py:205
  1239.1 4.6 convert_element_type.204
  1246.5 3.1 convert_element_type.222
  1249.6 9.5 convert_element_type.226
  1259.1 6.6 convert_element_type.228
  1265.6 6.3 convert_element_type.230
  (570 shorter events, 219.6 us)
Async XLA Ops:
  7.2 156.8 %copy-start = (bf16[2048,640]{1,0:T(8,128)(2,1)S(1)}, bf16[2048,640]{1,0:T(8,128)(2,1)}, u32[]{:S(2)}) copy-start(bf16[2048,640]{1,0:T(8,128)(2,1)} %param.22) | copy-start | bytes 7864324
  7.2 43.0 %all-gather.5.cloned.1.call-start = ((), (), s32[]{:S(2)}) async-start(), calls=%async_computation.4 | async-start | bytes 2621440 | tf_op jit(solution)/shard_map/all_gather | solution.py:95
  12.0 215.4 %reduce-scatter.5.cloned.1.call-start = ((), (), s32[]{:S(2)}) async-start(), calls=%async_computation.5 | async-start | bytes 5242880 | tf_op jit(solution)/shard_map/reduce_scatter | solution.py:114
  12.2 42.2 %copy-start.104 = (f32[640]{0:T(1024)}, f32[640]{0:T(1024)S(1)}, u32[]{:S(2)}) copy-start(f32[640]{0:T(1024)S(1)} %get-tuple-element.23) | copy-start | bytes 7684
  12.2 42.2 %copy-start.106 = (f32[640]{0:T(1024)}, f32[640]{0:T(1024)S(1)}, u32[]{:S(2)}) copy-start(f32[640]{0:T(1024)S(1)} %get-tuple-element.26) | copy-start | bytes 7684
  12.2 42.2 %copy-start.108 = (f32[640]{0:T(1024)}, f32[640]{0:T(1024)S(1)}, u32[]{:S(2)}) copy-start(f32[640]{0:T(1024)S(1)} %get-tuple-element.25) | copy-start | bytes 7684
  12.2 42.2 %copy-start.110 = (f32[640]{0:T(1024)}, f32[640]{0:T(1024)S(1)}, u32[]{:S(2)}) copy-start(f32[640]{0:T(1024)S(1)} %get-tuple-element.24) | copy-start | bytes 7684
  12.3 42.1 %copy-start.115 = (f32[512]{0:T(512)}, f32[512]{0:T(512)S(1)}, u32[]{:S(2)}) copy-start(f32[512]{0:T(512)S(1)} %get-tuple-element.167) | copy-start | bytes 6148
  12.3 42.1 %copy-start.117 = (f32[512]{0:T(512)}, f32[512]{0:T(512)S(1)}, u32[]{:S(2)}) copy-start(f32[512]{0:T(512)S(1)} %get-tuple-element.168) | copy-start | bytes 6148
  12.4 61.9 %copy-start.87 = (f32[512]{0:T(512)}, f32[512]{0:T(512)S(1)}, u32[]{:S(2)}) copy-start(f32[512]{0:T(512)S(1)} %get-tuple-element.79) | copy-start | bytes 6148
  12.4 61.9 %copy-start.112 = (f32[512]{0:T(512)}, f32[512]{0:T(512)S(1)}, u32[]{:S(2)}) copy-start(f32[512]{0:T(512)S(1)} %get-tuple-element.78) | copy-start | bytes 6148
  12.4 61.9 %copy-start.85 = (f32[640]{0:T(1024)}, f32[640]{0:T(1024)S(1)}, u32[]{:S(2)}) copy-start(f32[640]{0:T(1024)S(1)} %broadcast_multiply_fusion.3) | copy-start | bytes 7684
  82.6 22.2 %copy-start.14 = (f32[256,640]{1,0:T(8,128)}, f32[256,640]{1,0:T(8,128)S(1)}, u32[]{:S(2)}) copy-start(f32[256,640]{1,0:T(8,128)S(1)} %slice.325) | copy-start | bytes 1966084
  109.5 14.2 %copy-start.23 = (f32[128,640]{1,0:T(8,128)}, f32[128,640]{1,0:T(8,128)S(1)}, u32[]{:S(2)}) copy-start(f32[128,640]{1,0:T(8,128)S(1)} %slice.331) | copy-start | bytes 983044
  111.6 12.0 copy-start.27
  126.7 7.1 copy-start.30
  135.3 8.2 copy-start.56
  135.4 8.1 copy-start.67
  136.0 7.5 copy-start.52
  136.8 7.5 copy-start.76
  137.5 7.8 copy-start.89
  139.1 7.0 copy-start.43
  139.1 7.0 copy-start.58
  164.0 6.8 copy-start.134
  174.6 52.9 %copy-start.9 = (bf16[128,2048]{1,0:T(8,128)(2,1)S(1)}, bf16[128,2048]{1,0:T(8,128)(2,1)}, u32[]{:S(2)}) copy-start(bf16[128,2048]{1,0:T(8,128)(2,1)} %param.18) | copy-start | bytes 1572868
  174.6 91.7 %all-gather.7.cloned.1.call-start = ((), (), s32[]{:S(2)}) async-start(), calls=%async_computation.6 | async-start | bytes 2621440 | tf_op jit(solution)/shard_map/all_gather | solution.py:122
  175.3 189.6 %copy-start.74 = (f32[2048]{0:T(1024)}, f32[2048]{0:T(1024)S(1)}, u32[]{:S(2)}) copy-start(f32[2048]{0:T(1024)S(1)} %convert_element_type.184) | copy-start | bytes 24580
  228.9 135.9 %copy-start.123 = (f32[128]{0:T(128)}, f32[128]{0:T(128)S(1)}, u32[]{:S(2)}) copy-start(f32[128]{0:T(128)S(1)} %fusion.53) | copy-start | bytes 1540
  230.9 72.7 %all-gather.9.cloned.1.call-start = ((), (), s32[]{:S(2)}) async-start(), calls=%async_computation.8 | async-start | bytes 2621440 | tf_op jit(solution)/shard_map/all_gather | solution.py:135
  231.5 130.9 %reduce-scatter.9.cloned.1.call-start = ((), (), s32[]{:S(2)}) async-start(), calls=%async_computation.9 | async-start | bytes 2621440 | tf_op jit(solution)/shard_map/reduce_scatter | solution.py:151
  266.4 8.6 copy-start.137
  303.6 18.8 %slice-start.7 = ((s8[6291456]{0:T(1024)(128)(4,1)}), s8[2097152]{0:T(1024)(128)(4,1)S(1)}, s32[]{:S(2)}) async-start(s8[6291456]{0:T(1024)(128)(4,1)} %bitcast.100), calls=%async_computation.20 | async-start | bytes 4194304
  315.6 6.8 copy-start.144
  315.6 6.8 copy-start.146
  315.6 6.8 slice-start.8
  327.1 75.6 %all-gather.11.cloned.1.call-start = ((), (), s32[]{:S(2)}) async-start(), calls=%async_computation.10 | async-start | bytes 2621440 | tf_op jit(solution)/shard_map/all_gather | solution.py:164
  367.2 293.4 %reduce-scatter.11.cloned.1.call-start = ((), (), s32[]{:S(2)}) async-start(), calls=%async_computation.11 | async-start | bytes 2621440 | tf_op jit(solution)/shard_map/reduce_scatter | solution.py:180
  439.5 9.7 copy-start.60
  439.5 9.7 copy-start.62
  444.4 8.5 copy-start.69
  444.4 8.6 copy-start.71
  444.4 8.6 copy-start.77
  445.8 29.3 %copy-start.73 = (f32[8,640]{1,0:T(8,128)S(1)}, f32[8,640]{1,0:T(8,128)}, u32[]{:S(2)}) copy-start(f32[8,640]{1,0:T(8,128)} %copy-done.72) | copy-start | bytes 61444
  448.3 35.2 %copy-start.57 = (f32[16,640]{1,0:T(8,128)S(1)}, f32[16,640]{1,0:T(8,128)}, u32[]{:S(2)}) copy-start(f32[16,640]{1,0:T(8,128)} %copy-done.56) | copy-start | bytes 122884
  448.3 35.2 %copy-start.64 = (f32[16,640]{1,0:T(8,128)S(1)}, f32[16,640]{1,0:T(8,128)}, u32[]{:S(2)}) copy-start(f32[16,640]{1,0:T(8,128)} %copy-done.63) | copy-start | bytes 122884
  448.3 35.2 %copy-start.66 = (f32[16,640]{1,0:T(8,128)S(1)}, f32[16,640]{1,0:T(8,128)}, u32[]{:S(2)}) copy-start(f32[16,640]{1,0:T(8,128)} %copy-done.65) | copy-start | bytes 122884
  453.6 24.1 %copy-start.92 = (f32[7,640]{1,0:T(8,128)S(1)}, f32[7,640]{1,0:T(8,128)}, u32[]{:S(2)}) copy-start(f32[7,640]{1,0:T(8,128)} %get-tuple-element.138) | copy-start | bytes 53764
  456.3 38.7 %copy-start.50 = (f32[32,640]{1,0:T(8,128)S(1)}, f32[32,640]{1,0:T(8,128)}, u32[]{:S(2)}) copy-start(f32[32,640]{1,0:T(8,128)} %copy-done.49) | copy-start | bytes 245764
  495.0 13.6 %copy-start.31 = (f32[64,640]{1,0:T(8,128)S(1)}, f32[64,640]{1,0:T(8,128)}, u32[]{:S(2)}) copy-start(f32[64,640]{1,0:T(8,128)} %copy-done.30) | copy-start | bytes 491524
  513.0 12.1 copy-start.24
  513.0 12.1 slice-start.6
  534.9 8.2 copy-start.44
  537.6 7.3 slice-start.5
  618.9 91.4 %reduce-scatter.7.cloned.1.call-start = ((), (), s32[]{:S(2)}) async-start(), calls=%async_computation.7 | async-start | bytes 2621440 | tf_op jit(solution)/shard_map/reduce_scatter | solution.py:128
  627.0 608.3 %all-reduce.102.cloned.1.call-start = ((), (), s32[]{:S(2)}) async-start(), calls=%async_computation.12 | async-start | bytes 54788096 | tf_op jit(solution)/shard_map/psum | solution.py:205
  627.1 8.4 copy-start.138
  627.1 8.4 copy-start.147
  660.4 49.9 %copy-start.133 = (f32[128]{0:T(128)S(1)}, f32[128]{0:T(128)}, u32[]{:S(2)}) copy-start(f32[128]{0:T(128)} %copy-done.132) | copy-start | bytes 1540
  660.4 49.9 %copy-start.75 = (f32[2048]{0:T(1024)S(1)}, f32[2048]{0:T(1024)}, u32[]{:S(2)}) copy-start(f32[2048]{0:T(1024)} %copy-done.74) | copy-start | bytes 24580
  660.4 49.9 %copy-start.124 = (f32[128]{0:T(128)S(1)}, f32[128]{0:T(128)}, u32[]{:S(2)}) copy-start(f32[128]{0:T(128)} %copy-done.123) | copy-start | bytes 1540
  660.4 49.9 %copy-start.130 = (f32[128]{0:T(128)S(1)}, f32[128]{0:T(128)}, u32[]{:S(2)}) copy-start(f32[128]{0:T(128)} %copy-done.129) | copy-start | bytes 1540
  1246.5 12.6 slice-start.2
  1249.6 9.5 slice-start.3
  1249.6 16.1 %slice-start = ((s8[6291456]{0:T(1024)(128)(4,1)}), s8[4194304]{0:T(1024)(128)(4,1)S(1)}, s32[]{:S(2)}) async-start(s8[6291456]{0:T(1024)(128)(4,1)} %bitcast.88), calls=%async_computation.13 | async-start | bytes 8388608
  (102 other events, 288.9 us)
Sparse Core Ops, SparseCore 0:
  12.2 38.0 all-gather.4
  174.7 52.6 reduce-scatter.4
  231.0 35.2 all-gather.6
  268.2 35.2 all-gather.8
  327.2 35.1 reduce-scatter.8
  367.3 35.2 all-gather.10
  619.1 35.1 reduce-scatter.10
  657.5 35.2 reduce-scatter.6
  698.0 537.3 all-reduce.101
where the time goes:
time: 1290 us; the launch traced here: 1280 us
  waiting for transfers between devices  738 us (57%)
  local copies, waits for them, and re-layouts  226 us (18%)
  other arithmetic  133 us (10%)
  matrix products  121 us (9%)
  blocking collectives  44.6 us (3%)
  between operations  15.9 us (1%)
    psum x1, waiting for transfers between devices, local(): lax.psum(branch_weight_grad.astype(jnp.bfloat16), 'dp').astype(jnp.float32)  522 us
    pad x70, local copies, waits for them, and re-layouts, recurrence(): products, state = lax.associative_scan(combine, (carried, driven), axis=0)  120 us
    slice x69, local copies, waits for them, and re-layouts, recurrence(): products, state = lax.associative_scan(combine, (carried, driven), axis=0)  74 us
    reduce_scatter x1, waiting for transfers between devices, local(): lax.psum_scatter(jnp.dot(piece, output_weight, preferred_element_type=jnp...  52.2 us
    all_gather x1, waiting for transfers between devices, local(): lax.all_gather(normed.astype(jnp.bfloat16), 'mp', axis=0, tiled=True)  37.8 us
    reduce_scatter x1, waiting for transfers between devices, local(): lax.psum_scatter((lax.dot_general(gate_low, gate_weight, contract_cols, p...  35.3 us
    all_gather x1, waiting for transfers between devices, local(): lax.all_gather(resid_grad.astype(jnp.bfloat16), 'mp', axis=0, tiled=True)  35.2 us
    all_gather x1, waiting for transfers between devices, local(): lax.all_gather(normed_two.astype(jnp.bfloat16), 'mp', axis=0, tiled=True)  34.4 us
  transfers between devices with their start and end apart: 9, of which 7 were waited for; matrix products, arithmetic and copies ran while one was open for 5% of the time, Pallas kernels for 0%

commit v1 on v0

v1 whole, which is shorter than its diff:
```python
import functools

import jax
import jax.numpy as jnp
from jax import lax
from jax.experimental import pallas as pl
from jax.experimental.pallas import tpu as pltpu
from jax.sharding import Mesh
from jax.sharding import PartitionSpec as P

eps = 1e-06
decay_scale = 8.0
contract_rows = (((0,), (0,)), ((), ()))
contract_cols = (((1,), (1,)), ((), ()))
f32 = jnp.float32
bf16 = jnp.bfloat16
swap = [(0, 1), (1, 0)]
ALL = ("z", "core", "y", "x")
STEP = 16
root_two_over_pi = 0.7978845608028654


def gather_row(part, square):
    if not square:
        return lax.all_gather(part, ("y", "x"), axis=0, tiled=True)
    half = part.shape[0] // 2
    from_x = lax.ppermute(part, "x", swap)
    from_y = lax.ppermute(part, "y", swap)
    diag_a = lax.ppermute(from_x[:half], "y", swap)
    diag_b = lax.ppermute(from_y[half:], "x", swap)
    return jnp.concatenate([part, from_x, from_y, diag_a, diag_b], axis=0)


def scatter_row(partial, square):
    if not square:
        return lax.psum_scatter(partial, ("y", "x"), scatter_dimension=0, tiled=True).astype(f32)
    rows = partial.shape[0] // 4
    cut = partial.shape[1] // 2
    blocks = [partial[k * rows : (k + 1) * rows] for k in range(4)]
    got_x = lax.ppermute(
        jnp.concatenate([blocks[1][:, :cut], blocks[3][:, :cut]], axis=0), "x", swap
    )
    got_y = lax.ppermute(
        jnp.concatenate([blocks[2][:, cut:], blocks[3][:, cut:]], axis=0), "y", swap
    )
    send_y = (blocks[2][:, :cut].astype(f32) + got_x[rows:].astype(f32)).astype(bf16)
    send_x = (blocks[1][:, cut:].astype(f32) + got_y[rows:].astype(f32)).astype(bf16)
    last_y = lax.ppermute(send_y, "y", swap)
    last_x = lax.ppermute(send_x, "x", swap)
    left = blocks[0][:, :cut].astype(f32) + got_x[:rows].astype(f32) + last_y.astype(f32)
    right = blocks[0][:, cut:].astype(f32) + got_y[:rows].astype(f32) + last_x.astype(f32)
    return jnp.concatenate([left, right], axis=1)


def sibling(value):
    return lax.ppermute(value, "core", swap)


def half_of(value, which, axis):
    size = value.shape[axis] // 2
    return lax.dynamic_slice_in_dim(value, which * size, size, axis=axis)


def join(own, other, core, axis):
    first = jnp.where(core == 0, own, other)
    second = jnp.where(core == 0, other, own)
    return jnp.concatenate([first, second], axis=axis).astype(f32)


def line_sums(pieces, depth):
    if depth != 4:
        return [lax.psum(piece, "z") for piece in pieces]
    place = lax.axis_index("z")
    inner = (place == 1) | (place == 2)
    totals = []
    for piece in pieces:
        kind = piece.dtype
        inward = lax.ppermute(piece, "z", [(0, 1), (3, 2)])
        side = (piece.astype(f32) + inward.astype(f32)).astype(kind)
        across = lax.ppermute(side, "z", [(1, 2), (2, 1)])
        total = (side.astype(f32) + across.astype(f32)).astype(kind)
        outward = lax.ppermute(total, "z", [(1, 0), (2, 3)])
        totals.append(jnp.where(inner, total, outward))
    return totals


def tile_span(first, last, head, width):
    low = (first // head) * head // 128 * 128
    high = min(width, -(-(((last - 1) // head + 1) * head) // 128) * 128)
    return low, high


def tiles(width):
    return [(n, min(n + 256, width)) for n in range(0, width, 256)]


def sigmoid(x):
    return 1.0 / (1.0 + jnp.exp(-x))


def decay_terms(gate, soft, link):
    log_decay = gate * soft
    decay = jnp.exp(log_decay)
    square = decay * decay
    x = 2.0 * log_decay
    series = 1.0 + x * (1.0 / 6.0) * (1.0 + x * (1.0 / 7.0))
    series = 1.0 + x * (1.0 / 4.0) * (1.0 + x * (1.0 / 5.0) * series)
    series = -x * (1.0 + x * (1.0 / 2.0) * (1.0 + x * (1.0 / 3.0) * series))
    gap = jnp.where(x > -0.3, series, 1.0 - square)
    root = jnp.sqrt(gap)
    return link * decay, square, root, link * root + (1.0 - link)


def gelu_terms(x):
    inner = jnp.tanh(root_two_over_pi * (x + 0.044715 * x * x * x))
    value = 0.5 * x * (1.0 + inner)
    slope = 0.5 * (1.0 + inner) + 0.5 * x * (1.0 - inner * inner) * root_two_over_pi * (
        1.0 + 3.0 * 0.044715 * x * x
    )
    return value, slope


def widen(mask, width):
    return jnp.concatenate([mask] * (-(-width // 128)), axis=1)[:, :width]


def forward_kernel(
    spot_ref,
    branch_ref,
    stream_ref,
    joined_ref,
    taps_ref,
    bias_ref,
    high_ref,
    low_ref,
    gate_bias_ref,
    soft_ref,
    gated_ref,
    conv_ref,
    recur_ref,
    intake_ref,
    state_ref,
    part_high,
    part_low,
    *,
    head,
):
    length, width = branch_ref.shape
    block = length // 4
    per_block = block // STEP
    steps = length // STEP
    spot = spot_ref[0]

    def offset(step):
        turn = lax.bitwise_xor(step // per_block, spot)
        return pl.multiple_of(turn * block + lax.rem(step, per_block) * STEP, STEP)

    def convolve(step, before):
        at = offset(step)
        here = pl.multiple_of(step * STEP, STEP)
        now = stream_ref[pl.ds(at, STEP), :]
        both = jnp.concatenate([before, now], axis=0)
        total = bias_ref[0:1, :] + taps_ref[0:1, :] * now
        for k in range(1, 4):
            mask = widen(joined_ref[k - 1, pl.ds(here, STEP), :], width)
            total = total + taps_ref[k : k + 1, :] * both[8 - k : 8 - k + STEP] * mask
        conv_ref[pl.ds(at, STEP), :] = total
        high = total.astype(bf16)
        part_high[pl.ds(here, STEP), :] = high
        part_low[pl.ds(here, STEP), :] = (total - high.astype(f32)).astype(bf16)
        return now[STEP - 8 :]

    lax.fori_loop(0, steps, convolve, jnp.zeros((8, width), f32))

    for which, out_ref in ((0, recur_ref), (1, intake_ref)):
        for first, last in tiles(width):
            low, high = tile_span(first, last, head, width)
            span, cols = slice(low, high), slice(first, last)
            high_part, low_part = high_ref[which, span, cols], low_ref[which, span, cols]
            pre = (
                jnp.dot(part_high[:, span], high_part, preferred_element_type=f32)
                + jnp.dot(part_low[:, span], high_part, preferred_element_type=f32)
                + jnp.dot(part_high[:, span], low_part, preferred_element_type=f32)
            )
            out_ref[:, cols] = pre + gate_bias_ref[which : which + 1, cols]

    rows = lax.broadcasted_iota(jnp.int32, (8, width), 0)
    soft = soft_ref[0:1, :]

    def advance(step, last_state):
        at = offset(step)
        here = pl.multiple_of(step * STEP, STEP)
        link = widen(joined_ref[0, pl.ds(here, STEP), :], width)
        conv = conv_ref[pl.ds(at, STEP), :]
        recur = sigmoid(recur_ref[pl.ds(here, STEP), :])
        intake = sigmoid(intake_ref[pl.ds(here, STEP), :])
        recur_ref[pl.ds(here, STEP), :] = recur
        intake_ref[pl.ds(here, STEP), :] = intake
        carried, square, root, multiplier = decay_terms(recur, soft, link)
        driven = multiplier * intake * conv
        found = []
        for part in range(STEP // 8):
            a = carried[8 * part : 8 * part + 8]
            b = driven[8 * part : 8 * part + 8]
            for shift in (1, 2, 4):
                a_before = jnp.where(rows >= shift, pltpu.roll(a, shift, 0), 1.0)
                b_before = jnp.where(rows >= shift, pltpu.roll(b, shift, 0), 0.0)
                b = b + a * b_before
                a = a * a_before
            state = b + a * last_state
            last_state = state[7:8]
            found.append(state)
        state = jnp.concatenate(found, axis=0)
        state_ref[pl.ds(at, STEP), :] = state
        value, slope = gelu_terms(branch_ref[pl.ds(at, STEP), :])
        gated_ref[pl.ds(at, STEP), :] = (value * state).astype(bf16)
        return last_state

    lax.fori_loop(0, steps, advance, jnp.zeros((1, width), f32))


def backward_kernel(
    spot_ref,
    grad_ref,
    stream_ref,
    joined_ref,
    conv_ref,
    recur_ref,
    intake_ref,
    state_ref,
    taps_ref,
    back_ref,
    soft_ref,
    stream_grad_ref,
    gates_ref,
    sums_ref,
    pre_ref,
    conv_low,
    conv_grad,
    *,
    head,
):
    length, width = grad_ref.shape
    block = length // 4
    per_block = block // STEP
    steps = length // STEP
    spot = spot_ref[0]

    def offset(step):
        turn = lax.bitwise_xor(step // per_block, spot)
        return pl.multiple_of(turn * block + lax.rem(step, per_block) * STEP, STEP)

    rows = lax.broadcasted_iota(jnp.int32, (8, width), 0)
    soft = soft_ref[0:1, :]
    count = STEP // 8

    def fold(value):
        total = value[0:8]
        for part in range(1, count):
            total = total + value[8 * part : 8 * part + 8]
        return total

    def retreat(turn, kept):
        after_carried, after_adjoint, decay_sum, recur_sum, intake_sum = kept
        step = steps - 1 - turn
        at = offset(step)
        at_before = offset(jnp.maximum(step - 1, 0))
        here = pl.multiple_of(step * STEP, STEP)
        link = widen(joined_ref[0, pl.ds(here, STEP), :], width)
        conv = conv_ref[pl.ds(at, STEP), :]
        recur = recur_ref[pl.ds(here, STEP), :]
        intake = intake_ref[pl.ds(here, STEP), :]
        carried, square, root, multiplier = decay_terms(recur, soft, link)
        grad = grad_ref[pl.ds(at, STEP), :]
        found = []
        for part in reversed(range(count)):
            own = carried[8 * part : 8 * part + 8]
            a = jnp.where(rows < 7, pltpu.roll(own, 7, 0), after_carried)
            b = grad[8 * part : 8 * part + 8]
            for shift in (1, 2, 4):
                a_after = jnp.where(rows < 8 - shift, pltpu.roll(a, 8 - shift, 0), 1.0)
                b_after = jnp.where(rows < 8 - shift, pltpu.roll(b, 8 - shift, 0), 0.0)
                b = b + a * b_after
                a = a * a_after
            adjoint = b + a * after_adjoint
            after_adjoint = adjoint[0:1]
            after_carried = own[0:1]
            found.append(adjoint)
        adjoint = jnp.concatenate(found[::-1], axis=0)
        state = state_ref[pl.ds(at, STEP), :]
        tail = state_ref[pl.ds(at_before + (STEP - 8), 8), :]
        earlier = jnp.concatenate([tail, state], axis=0)[7 : 7 + STEP]
        driven_part = adjoint * intake
        log_grad = adjoint * earlier * carried - driven_part * conv * link * square / root
        recur_grad = log_grad * soft * recur * (1.0 - recur)
        spread = driven_part * multiplier
        intake_grad = spread * conv * (1.0 - intake)
        pre_ref[0, pl.ds(here, STEP), :] = recur_grad.astype(bf16)
        pre_ref[1, pl.ds(here, STEP), :] = intake_grad.astype(bf16)
        conv_low[pl.ds(here, STEP), :] = conv.astype(bf16)
        conv_grad[pl.ds(here, STEP), :] = spread
        return (
            after_carried,
            after_adjoint,
            decay_sum + fold(log_grad * recur),
            recur_sum + fold(recur_grad),
            intake_sum + fold(intake_grad),
        )

    line = jnp.zeros((1, width), f32)
    eight = jnp.zeros((8, width), f32)
    kept = lax.fori_loop(0, steps, retreat, (line, line, eight, eight, eight))
    sums_ref[5:6, :] = jnp.sum(kept[3], axis=0, keepdims=True)
    sums_ref[6:7, :] = jnp.sum(kept[4], axis=0, keepdims=True)
    sums_ref[7:8, :] = jnp.sum(kept[2], axis=0, keepdims=True)

    conv_grad[length : length + 8, :] = eight
    for first, last in tiles(width):
        low, high = tile_span(first, last, head, width)
        span, cols = slice(low, high), slice(first, last)
        total = conv_grad[0:length, cols]
        for which in range(2):
            total = total + jnp.dot(
                pre_ref[which, :, span], back_ref[which, span, cols], preferred_element_type=f32
            )
            gates_ref[which, span, cols] = lax.dot_general(
                conv_low[:, span], pre_ref[which, :, cols], contract_rows, preferred_element_type=f32
            )
        conv_grad[0:length, cols] = total

    def unwind(step, kept):
        at = offset(step)
        here = pl.multiple_of(step * STEP, STEP)
        ahead = conv_grad[pl.ds(here, STEP + 8), :]
        now = stream_ref[pl.ds(at, STEP), :]
        total = taps_ref[0:1, :] * ahead[0:STEP]
        sums = [kept[0] + fold(ahead[0:STEP] * now)]
        for k in range(1, 4):
            mask = widen(joined_ref[k - 1, pl.ds(here, STEP + 8), :], width)
            moved = (ahead * mask)[k : k + STEP]
            total = total + taps_ref[k : k + 1, :] * moved
            sums.append(kept[k] + fold(moved * now))
        stream_grad_ref[pl.ds(at, STEP), :] = total.astype(bf16)
        return (*sums, kept[4] + fold(ahead[0:STEP]))

    kept = lax.fori_loop(0, steps, unwind, (eight,) * 5)
    for k in range(5):
        sums_ref[k : k + 1, :] = jnp.sum(kept[k], axis=0, keepdims=True)


def call(body, outs, scratch, args):
    vmem = pl.BlockSpec(memory_space=pltpu.VMEM)
    return pl.pallas_call(
        body,
        out_shape=outs,
        in_specs=[pl.BlockSpec(memory_space=pltpu.SMEM)] + [vmem] * (len(args) - 1),
        out_specs=[vmem] * len(outs),
        scratch_shapes=scratch,
        compiler_params=pltpu.CompilerParams(vmem_limit_bytes=48 * 1024 * 1024),
    )(*args)


def spread_heads(weight):
    count, size = weight.shape[0], weight.shape[1]
    rows = []
    for h in range(count):
        rows.append(jnp.pad(weight[h], ((0, 0), (h * size, (count - 1 - h) * size))))
    return jnp.concatenate(rows, axis=0)


def take_heads(wide, count, size):
    return jnp.stack([wide[h * size : (h + 1) * size, h * size : (h + 1) * size] for h in range(count)])


def local(
    inputs,
    cotangent,
    segment_ids,
    norm_gain,
    branch_weight,
    stream_weight,
    conv_weight,
    conv_bias,
    recur_weight,
    recur_bias,
    intake_weight,
    intake_bias,
    decay_param,
    output_weight,
    mlp_gain,
    gate_weight,
    up_weight,
    down_weight,
    *,
    depth,
    square,
):
    core = lax.axis_index("core")
    spot = jnp.zeros((1,), jnp.int32)
    if square:
        spot = spot + (2 * lax.axis_index("y") + lax.axis_index("x")).astype(jnp.int32)
    heads, head = recur_weight.shape[0], recur_weight.shape[1]
    width = heads * head
    length = segment_ids.shape[1]

    seg_row = segment_ids[0]
    masks = []
    for k in range(1, 4):
        earlier = jnp.concatenate([jnp.full((k,), -1, jnp.int32), seg_row[:-k]])
        masks.append((seg_row == earlier).astype(f32))
    joined = jnp.pad(jnp.stack(masks), ((0, 0), (0, 8)))
    joined = jnp.broadcast_to(joined[:, :, None], (3, length + 8, 128))
    wide = jnp.stack([spread_heads(recur_weight), spread_heads(intake_weight)])
    wide_high = wide.astype(bf16)
    wide_low = (wide - wide_high.astype(f32)).astype(bf16)
    wide_back = jnp.swapaxes(wide_high, 1, 2)
    gate_bias = jnp.stack([recur_bias, intake_bias])
    soft = (-decay_scale * jax.nn.softplus(-decay_param))[None, :]
    taps = conv_weight.astype(f32)

    resid = inputs.astype(f32)
    scale_one = lax.rsqrt(jnp.mean(resid * resid, axis=-1, keepdims=True) + eps)
    gain_one = norm_gain.astype(f32)[None, :]
    normed = gather_row((resid * scale_one * gain_one).astype(bf16), square)
    cot_all = lax.all_gather(cotangent, ALL, axis=0, tiled=True)

    branch_pre = jnp.dot(normed, branch_weight, preferred_element_type=f32)
    stream_pre = jnp.dot(normed, stream_weight, preferred_element_type=f32)
    token = jax.ShapeDtypeStruct((length, width), f32)
    gated, convolved, recur_gate, intake_gate, state = call(
        functools.partial(forward_kernel, head=head),
        [jax.ShapeDtypeStruct((length, width), bf16), token, token, token, token],
        [pltpu.VMEM((length, width), bf16), pltpu.VMEM((length, width), bf16)],
        (
            spot,
            branch_pre,
            stream_pre,
            joined,
            taps,
            conv_bias.astype(f32)[None, :],
            wide_high,
            wide_low,
            gate_bias,
            soft,
        ),
    )
    mixer = scatter_row(jnp.dot(gated, output_weight, preferred_element_type=f32).astype(bf16), square)

    hidden = resid + mixer
    scale_two = lax.rsqrt(jnp.mean(hidden * hidden, axis=-1, keepdims=True) + eps)
    gain_two = mlp_gain.astype(f32)[None, :]
    hat_two = hidden * scale_two
    normed_two = (hat_two * gain_two).astype(bf16)
    mlp_in = gather_row(normed_two, square)
    mlp_all = lax.all_gather(normed_two, ALL, axis=0, tiled=True)
    cot_row = gather_row(cotangent, square)

    def mlp_grads(tokens, cots, gate, up, down):
        gate_pre = jnp.dot(tokens, gate, preferred_element_type=f32)
        up_pre = jnp.dot(tokens, up, preferred_element_type=f32)
        activ_grad = lax.dot_general(cots, down, contract_cols, preferred_element_type=f32)
        value, slope = gelu_terms(gate_pre)
        return (
            (value * up_pre).astype(bf16),
            (activ_grad * up_pre * slope).astype(bf16),
            (activ_grad * value).astype(bf16),
        )

    activ, gate_low, up_low = mlp_grads(mlp_in, cot_row, gate_weight, up_weight, down_weight)
    two_grad = scatter_row(
        (
            lax.dot_general(gate_low, gate_weight, contract_cols, preferred_element_type=f32)
            + lax.dot_general(up_low, up_weight, contract_cols, preferred_element_type=f32)
        ).astype(bf16),
        square,
    )
    mlp_out = scatter_row(jnp.dot(activ, down_weight, preferred_element_type=f32).astype(bf16), square)
    block_out = (hidden + mlp_out).astype(bf16)

    mlp_gain_part = jnp.sum(two_grad * hat_two, axis=0)
    scaled = two_grad * gain_two
    resid_grad = cotangent.astype(f32) + scale_two * (
        scaled - hat_two * jnp.mean(scaled * hat_two, axis=-1, keepdims=True)
    )
    branch_cot = gather_row(resid_grad.astype(bf16), square)

    gated_grad = lax.dot_general(branch_cot, output_weight, contract_cols, preferred_element_type=f32)
    value, slope = gelu_terms(branch_pre)
    state_grad = gated_grad * value
    branch_low = (gated_grad * state * slope).astype(bf16)
    stream_low, wide_grad, sums = call(
        functools.partial(backward_kernel, head=head),
        [
            jax.ShapeDtypeStruct((length, width), bf16),
            jax.ShapeDtypeStruct((2, width, width), f32),
            jax.ShapeDtypeStruct((8, width), f32),
        ],
        [
            pltpu.VMEM((2, length, width), bf16),
            pltpu.VMEM((length, width), bf16),
            pltpu.VMEM((length + 8, width), f32),
        ],
        (
            spot,
            state_grad,
            stream_pre,
            joined,
            convolved,
            recur_gate,
            intake_gate,
            state,
            taps,
            wide_back,
            soft,
        ),
    )
    one_grad = scatter_row(
        (
            lax.dot_general(branch_low, branch_weight, contract_cols, preferred_element_type=f32)
            + lax.dot_general(stream_low, stream_weight, contract_cols, preferred_element_type=f32)
        ).astype(bf16),
        square,
    )
    hat_one = resid * scale_one
    norm_gain_part = jnp.sum(one_grad * hat_one, axis=0)
    scaled = one_grad * gain_one
    inputs_grad = (
        resid_grad
        + scale_one * (scaled - hat_one * jnp.mean(scaled * hat_one, axis=-1, keepdims=True))
    ).astype(bf16)

    def both(value):
        return jnp.concatenate([value, sibling(value)], axis=0)

    def both_halves(value):
        return jnp.concatenate(
            [half_of(value, core, 1), sibling(half_of(value, 1 - core, 1))], axis=0
        )

    normed_half = both_halves(normed)
    output_half = lax.dot_general(
        both(gated), both_halves(branch_cot), contract_rows, preferred_element_type=f32
    ).astype(bf16)
    branch_half = lax.dot_general(
        normed_half, both(branch_low), contract_rows, preferred_element_type=f32
    ).astype(bf16)
    stream_half = lax.dot_general(
        normed_half, both(stream_low), contract_rows, preferred_element_type=f32
    ).astype(bf16)
    recur_part = take_heads(wide_grad[0], heads, head).astype(bf16)
    intake_part = take_heads(wide_grad[1], heads, head).astype(bf16)
    gate_half = (
        jnp.where(core == 0, recur_part, intake_part).astype(f32)
        + sibling(jnp.where(core == 0, intake_part, recur_part)).astype(f32)
    ).astype(bf16)
    gains = jnp.concatenate([norm_gain_part, mlp_gain_part])
    if square:
        gains = gains + lax.ppermute(gains, "x", swap)
        gains = gains + lax.ppermute(gains, "y", swap)
    else:
        gains = lax.psum(gains, ("y", "x"))
    small = jnp.concatenate([sums.reshape(-1), gains]).reshape(-1, 128)
    small = small + sibling(small)
    output_sum, branch_sum, stream_sum, gate_sum, small_sum = line_sums(
        [output_half, branch_half, stream_half, gate_half, small], depth
    )

    gate_part = half_of(gate_weight, core, 1)
    up_part = half_of(up_weight, core, 1)
    down_part = half_of(down_weight, core, 0)
    activ_all, gate_all, up_all = mlp_grads(mlp_all, cot_all, gate_part, up_part, down_part)
    down_half = lax.dot_general(activ_all, cot_all, contract_rows, preferred_element_type=f32).astype(bf16)
    gate_w_half = lax.dot_general(mlp_all, gate_all, contract_rows, preferred_element_type=f32).astype(bf16)
    up_w_half = lax.dot_general(mlp_all, up_all, contract_rows, preferred_element_type=f32).astype(bf16)

    def whole(own, axis):
        return join(own, sibling(own), core, axis)

    gate_other = sibling(gate_sum)
    small_flat = small_sum.reshape(-1)
    sums = small_flat[: 8 * width].reshape(8, width)
    gains = small_flat[8 * width :].reshape(2, -1)
    return (
        block_out,
        inputs_grad,
        gains[0],
        whole(branch_sum, 0),
        whole(stream_sum, 0),
        sums[0:4],
        sums[4],
        jnp.where(core == 0, gate_sum, gate_other).astype(f32),
        sums[5],
        jnp.where(core == 0, gate_other, gate_sum).astype(f32),
        sums[6],
        sums[7] * decay_scale * jax.nn.sigmoid(-decay_param),
        whole(output_sum, 1),
        gains[1],
        whole(gate_w_half, 1),
        whole(up_w_half, 1),
        whole(down_half, 0),
    )


def solution(mesh):
    depth = mesh.shape["dp"] // 2
    across = mesh.shape["mp"] // 2
    fine = Mesh(mesh.devices.reshape(depth, 2, 2, across), ALL)
    dp, mp = ("z", "core"), ("y", "x")
    cols, vec, blocks, rows = P(None, mp), P(mp), P(mp, None, None), P(mp, None)
    tokens = P(ALL, None)
    return jax.shard_map(
        functools.partial(local, depth=depth, square=across == 2),
        mesh=fine,
        in_specs=(
            tokens,
            tokens,
            P(dp, None),
            P(),
            cols,
            cols,
            cols,
            vec,
            blocks,
            vec,
            blocks,
            vec,
            vec,
            rows,
            P(),
            cols,
            cols,
            rows,
        ),
        out_specs=(
            tokens,
            tokens,
            P(),
            cols,
            cols,
            cols,
            vec,
            blocks,
            vec,
            blocks,
            vec,
            vec,
            rows,
            P(),
            cols,
            cols,
            rows,
        ),
        check_vma=False,
    )
```

time: 1290 us -> 785 us (0.61)
  waiting for transfers between devices: 738 us -> 312 us
  local copies, waits for them, and re-layouts: 226 us -> 78.7 us
  matrix products: 121 us -> 211 us
  starting transfers between devices: 0.95 us -> 62.4 us
  other arithmetic: 133 us -> 72.8 us
  blocking collectives: 44.6 us -> 0 us
  Pallas kernels: 0 us -> 24.9 us
    psum x1 -> x0, waiting for transfers between devices: 522 us -> none  [local(): lax.psum(branch_weight_grad.astype(jnp.bfloat16), 'dp').astype(jnp.float32)]
    ppermute x0 -> x63, waiting for transfers between devices: none -> 311 us  [the longest x5 82.9 us: line_sums(): outward = lax.ppermute(total, 'z', [(1, 0), (2, 3)])]
    all_gather x4 -> x2, waiting for transfers between devices: 128 us -> 0.01 us  [the longest x1 0.01 us: local(): cot_all = lax.all_gather(cotangent, ALL, axis=0, tiled=True)]
    pad x70 -> x0, local copies, waits for them, and re-layouts: 120 us -> none  [recurrence(): products, state = lax.associative_scan(combine, (carried, driven), axis=0)]
    reduce_scatter x4 -> x0, waiting for transfers between devices: 87.5 us -> none  [the longest x1 52.2 us: local(): lax.psum_scatter(jnp.dot(piece, output_weight, preferred_element_type=jnp...]
    dot_general x19 -> x16, matrix products: 97.8 us -> 183 us  [the longest x1 32 us: local(): lax.dot_general(mlp_all, gate_all, contract_rows, preferred_element_type=...]
    slice x70 -> x16, local copies, waits for them, and re-layouts: 74 us -> 7.74 us  [the longest x2 3.99 us: spread_heads(): weight[h]]
    ppermute x0 -> x63, starting transfers between devices: none -> 62.4 us  [the longest x5 12 us: line_sums(): inward = lax.ppermute(piece, 'z', [(0, 1), (3, 2)])]
  transfers between devices with their start and end apart: 9 -> 65, of which waited for: 7 -> 32; matrix products, arithmetic and copies ran while one was open for 5% -> 39% of each run, Pallas kernels for 0% -> 3%
where the time goes in v1:
time: 785 us; the launch traced here: 777 us
  waiting for transfers between devices  312 us (40%)
  matrix products  211 us (27%)
  local copies, waits for them, and re-layouts  78.7 us (10%)
  other arithmetic  72.8 us (9%)
  starting transfers between devices  62.4 us (8%)
  Pallas kernels  24.9 us (3%)
  between operations  16 us (2%)
    ppermute x5, waiting for transfers between devices, line_sums(): outward = lax.ppermute(total, 'z', [(1, 0), (2, 3)])  82.9 us
    ppermute x5, waiting for transfers between devices, line_sums(): inward = lax.ppermute(piece, 'z', [(0, 1), (3, 2)])  64.9 us
    unnamed x129, local copies, waits for them, and re-layouts  51.8 us
    ppermute x4, waiting for transfers between devices, scatter_row(): last_y = lax.ppermute(send_y, 'y', swap)  37.4 us
    dot_general x1, matrix products, local(): lax.dot_general(mlp_all, gate_all, contract_rows, preferred_element_type=...  32 us
    ppermute x4, waiting for transfers between devices, scatter_row(): lax.ppermute(jnp.concatenate([blocks[1][:, :cut], blocks[3][:, :cut]], ax...  31 us
    dot_general x2, matrix products, mlp_grads(): lax.dot_general(cots, down, contract_cols, preferred_element_type=f32)  29.4 us
    convert_element_type x6, other arithmetic, join(): return jnp.concatenate([first, second], axis=axis).astype(f32)  27.6 us
  transfers between devices with their start and end apart: 65, of which 32 were waited for; matrix products, arithmetic and copies ran while one was open for 39% of the time, Pallas kernels for 3%

profile of v1, /device:TPU:0, one launch (start us, length us, event | category | flops | bytes accessed | tf_op | source)
XLA Modules:
  0.0 777.2 jit_solution(2601569495000196003)
XLA Ops:
  12.2 3.0 collective-permute-start.1
  38.7 3.5 copy.44.low_ref
  42.2 3.9 fusion.115
  46.2 3.5 copy.43.high_ref
  54.5 5.9 collective-permute-done.2
  61.1 3.0 collective-permute-done.3
  64.9 4.6 fusion.124.stream_ref
  69.5 3.0 fusion.123.branch_ref
  72.8 11.8 %shard_map.305 = (bf16[512,640]{1,0:T(8,128)(2,1)S(1)}, f32[512,640]{1,0:T(8,128)S(1)}, f32[512,640]{1,0:T(8,128)S(1)}, f32[512,640]{1,0:T(8,128)S(1)}, f32[512,640]{1,0:T(8,128)}) custom-call(s32[1]{0:T(128)} %bitcast.spot_ref, f32[512,640]{1,0:T(8,128)} %fusion.123.branch_ref, f32[512,640]{1,0:T(8,128)} %fusion.124.stream_ref, ...), custom_call_target="tpu_custom_call" | custom-call | tf_op jit(solution)/shard_map/pallas_call | solution.py:353
  88.5 23.8 %collective-permute-done.4 = bf16[256,1024]{1,0:T(8,128)(2,1)S(1)} collective-permute-done((bf16[256,1024]{1,0:T(8,128)(2,1)S(1)}, bf16[256,1024]{1,0:T(8,128)(2,1)S(1)}, u32[]{:S(2)}, u32[]{:S(2)}) %collective-permute-start.4) | collective-permute-done | bytes 524320 | tf_op jit(solution)/shard_map/ppermute | solution.py:40
  113.5 13.0 %collective-permute-done.5 = bf16[128,1024]{1,0:T(8,128)(2,1)S(1)} collective-permute-done((bf16[128,1024]{1,0:T(8,128)(2,1)S(1)}, bf16[128,1024]{1,0:T(8,128)(2,1)S(1)}, u32[]{:S(2)}, u32[]{:S(2)}) %collective-permute-start.5) | collective-permute-done | bytes 262176 | tf_op jit(solution)/shard_map/ppermute | solution.py:48
  127.6 5.6 collective-permute-done.7
  137.8 9.9 %collective-permute-done.17 = bf16[128,2048]{1,0:T(8,128)(2,1)S(1)} collective-permute-done((bf16[128,2048]{1,0:T(8,128)(2,1)}, bf16[128,2048]{1,0:T(8,128)(2,1)S(1)}, u32[]{:S(2)}, u32[]{:S(2)}) %collective-permute-start.17) | collective-permute-done | bytes 524320 | tf_op jit(solution)/shard_map/ppermute | solution.py:28
  148.2 3.1 collective-permute-start.18
  151.4 6.8 collective-permute-done.18
  160.7 8.4 %fusion.127 = f32[512,1536]{1,0:T(8,128)} fusion(bf16[512,2048]{1,0:T(8,128)(2,1)S(1)} %constant_dynamic-update-slice_fusion.10, bf16[1536,2048]{1,0:T(8,128)(2,1)} %param.35), kind=kOutput, calls=%fused_computation.273 | convolution fusion | flops 3221225472 | bytes 11534336 | tf_op jit(solution)/shard_map/dot_general | solution.py:461
  169.1 5.3 collective-permute-done.9
  176.7 5.7 collective-permute-done.10
  182.6 3.4 fusion.125
  186.0 3.4 fusion.126
  189.5 4.9 convolution_convert_fusion
  195.0 10.5 %fusion.49 = f32[512,2048]{1,0:T(8,128)} fusion(bf16[2048,1536]{1,0:T(8,128)(2,1)S(1)} %bitcast.116, f32[512,1536]{1,0:T(8,128)} %copy-done.45, f32[512,1536]{1,0:T(8,128)} %fusion.127, f32[512,1536]{1,0:T(8,128)} %copy-done.46), kind=kOutput, calls=%fused_computation.98 | convolution fusion | flops 3236954112 | bytes 19922944 | tf_op jit(solution)/shard_map/dot_general | solution.py:472
  205.5 9.7 %add_convert_fusion.1 = bf16[512,2048]{1,0:T(8,128)(2,1)S(1)} fusion(f32[512,2048]{1,0:T(8,128)} %fusion.49, bf16[2048,1536]{1,0:T(8,128)(2,1)} %param.34, f32[512,1536]{1,0:T(8,128)} %fusion.127, f32[512,1536]{1,0:T(8,128)} %copy-done.45), kind=kOutput, calls=%fused_computation.23 | convolution fusion | flops 3231186944 | bytes 18874368 | tf_op jit(solution)/shard_map/dot_general | solution.py:473
  219.8 6.5 collective-permute-done.20
  228.2 3.6 collective-permute-done.14
  231.8 9.5 %collective-permute-done.13 = bf16[128,1024]{1,0:T(8,128)(2,1)S(1)} collective-permute-done((bf16[128,1024]{1,0:T(8,128)(2,1)S(1)}, bf16[128,1024]{1,0:T(8,128)(2,1)S(1)}, u32[]{:S(2)}, u32[]{:S(2)}) %collective-permute-start.13) | collective-permute-done | bytes 262176 | tf_op jit(solution)/shard_map/ppermute | solution.py:48
  241.7 16.4 %collective-permute-done.22 = bf16[256,1024]{1,0:T(8,128)(2,1)S(1)} collective-permute-done((bf16[256,1024]{1,0:T(8,128)(2,1)S(1)}, bf16[256,1024]{1,0:T(8,128)(2,1)S(1)}, u32[]{:S(2)}, u32[]{:S(2)}) %collective-permute-start.22) | collective-permute-done | bytes 524320 | tf_op jit(solution)/shard_map/ppermute | solution.py:43
  258.2 10.4 %collective-permute-done.21 = bf16[128,1024]{1,0:T(8,128)(2,1)S(1)} collective-permute-done((bf16[128,1024]{1,0:T(8,128)(2,1)S(1)}, bf16[128,1024]{1,0:T(8,128)(2,1)S(1)}, u32[]{:S(2)}, u32[]{:S(2)}) %collective-permute-start.21) | collective-permute-done | bytes 262176 | tf_op jit(solution)/shard_map/ppermute | solution.py:48
  269.4 6.8 collective-permute-done.23
  281.7 10.3 %collective-permute-done.25 = bf16[128,2048]{1,0:T(8,128)(2,1)} collective-permute-done((bf16[128,2048]{1,0:T(8,128)(2,1)}, bf16[128,2048]{1,0:T(8,128)(2,1)}, u32[]{:S(2)}, u32[]{:S(2)}) %collective-permute-start.25) | collective-permute-done | bytes 524320 | tf_op jit(solution)/shard_map/ppermute | solution.py:28
  302.2 4.2 multiply_multiply_fusion.6
  306.5 13.2 %shard_map.306 = (bf16[512,640]{1,0:T(8,128)(2,1)S(1)}, f32[2,640,640]{2,1,0:T(8,128)}, f32[8,640]{1,0:T(8,128)S(1)}) custom-call(s32[1]{0:T(128)} %bitcast.spot_ref, f32[512,640]{1,0:T(8,128)S(1)} %get-tuple-element.79.grad_ref, f32[512,640]{1,0:T(8,128)S(1)} %copy-done.2, f32[3,520,128]{2,1,0:T(8,128)S(1)} %broadcast_in_dim.8.joined_ref, ...), custom_call_target="tpu_custom_call" | custom-call | tf_op jit(solution)/shard_map/pallas_call | solution.py:353
  329.6 3.4 collective-permute-start.50
  333.1 3.0 constant_dynamic-slice_fusion.3
  346.6 7.1 collective-permute-done.30
  353.7 4.5 collective-permute-done.29
  362.4 3.6 convolution_convert_fusion.2
  366.1 3.6 collective-permute-done.31
  369.7 4.4 collective-permute-start.45
  377.2 3.1 convolution_convert_fusion.3
  390.6 12.6 %collective-permute-done.45 = bf16[1024,640]{1,0:T(8,128)(2,1)S(1)} collective-permute-done((bf16[1024,640]{1,0:T(8,128)(2,1)S(1)}, bf16[1024,640]{1,0:T(8,128)(2,1)S(1)}, u32[]{:S(2)}, u32[]{:S(2)}) %collective-permute-start.45) | collective-permute-done | bytes 1310752 | tf_op jit(solution)/shard_map/ppermute | solution.py:78
  404.3 27.0 %collective-permute-done.40 = bf16[1024,640]{1,0:T(8,128)(2,1)S(1)} collective-permute-done((bf16[1024,640]{1,0:T(8,128)(2,1)S(1)}, bf16[1024,640]{1,0:T(8,128)(2,1)S(1)}, u32[]{:S(2)}, u32[]{:S(2)}) %collective-permute-start.40) | collective-permute-done | bytes 1310752 | tf_op jit(solution)/shard_map/ppermute | solution.py:78
  433.5 25.0 %collective-permute-done.35 = f32[72,128]{1,0:T(8,128)S(1)} collective-permute-done((f32[72,128]{1,0:T(8,128)S(1)}, f32[72,128]{1,0:T(8,128)S(1)}, u32[]{:S(2)}, u32[]{:S(2)}) %collective-permute-start.35) | collective-permute-done | bytes 36896 | tf_op jit(solution)/shard_map/ppermute | solution.py:78
  466.5 3.5 collective-permute-done.37
  473.0 30.7 %collective-permute-done.47 = bf16[1024,640]{1,0:T(8,128)(2,1)S(1)} collective-permute-done((bf16[1024,640]{1,0:T(8,128)(2,1)S(1)}, bf16[1024,640]{1,0:T(8,128)(2,1)S(1)}, u32[]{:S(2)}, u32[]{:S(2)}) %collective-permute-start.47) | collective-permute-done | bytes 1310752 | tf_op jit(solution)/shard_map/ppermute | solution.py:82
  504.5 27.2 %collective-permute-done.42 = bf16[1024,640]{1,0:T(8,128)(2,1)S(1)} collective-permute-done((bf16[1024,640]{1,0:T(8,128)(2,1)S(1)}, bf16[1024,640]{1,0:T(8,128)(2,1)S(1)}, u32[]{:S(2)}, u32[]{:S(2)}) %collective-permute-start.42) | collective-permute-done | bytes 1310752 | tf_op jit(solution)/shard_map/ppermute | solution.py:82
  534.8 21.4 %collective-permute-done.58 = bf16[640,1024]{1,0:T(8,128)(2,1)} collective-permute-done((bf16[640,1024]{1,0:T(8,128)(2,1)}, bf16[640,1024]{1,0:T(8,128)(2,1)}, u32[]{:S(2)}, u32[]{:S(2)}) %collective-permute-start.58) | collective-permute-done | bytes 1310752 | tf_op jit(solution)/shard_map/ppermute | solution.py:82
  559.4 2.7 maximum_convert_fusion.4
  564.0 2.7 maximum_convert_fusion.3
  566.9 3.0 maximum_convert_fusion.5
  570.0 21.0 %fusion.31 = f32[768,4096]{1,0:T(8,128)} fusion(bf16[4096,2048]{1,0:T(8,128)(2,1)} %all-gather.5.cloned.1.call-done, bf16[1536,2048]{1,0:T(8,128)(2,1)} %param.35, s32[]{:T(128)S(6)} %select_n.157), kind=kOutput, calls=%fused_computation.40 | convolution fusion | flops 12884901888 | bytes 32505860 | tf_op jit(solution)/shard_map/dot_general | solution.py:461
  590.9 20.5 %fusion.27 = f32[4096,768]{0,1:T(8,128)} fusion(bf16[4096,2048]{1,0:T(8,128)(2,1)} %all-gather.3.cloned.1.call-done, bf16[2048,1536]{1,0:T(8,128)(2,1)} %param.33, s32[]{:T(128)S(6)} %select_n.157), kind=kOutput, calls=%fused_computation.36 | convolution fusion | flops 12884901888 | bytes 32505860 | tf_op jit(solution)/shard_map/dot_general | solution.py:459
  611.4 25.4 %fusion.16 = bf16[2048,768]{0,1:T(8,128)(2,1)} fusion(bf16[4096,2048]{1,0:T(8,128)(2,1)} %all-gather.3.cloned.1.call-done, f32[768,4096]{1,0:T(8,128)} %fusion.31, f32[4096,768]{0,1:T(8,128)} %fusion.27), kind=kOutput, calls=%fused_computation.25 | convolution fusion | flops 12917932032 | bytes 45088768 | tf_op jit(solution)/shard_map/dot_general | solution.py:574
  637.2 20.5 %fusion.29 = f32[4096,768]{0,1:T(8,128)} fusion(bf16[4096,2048]{1,0:T(8,128)(2,1)} %all-gather.3.cloned.1.call-done, bf16[2048,1536]{1,0:T(8,128)(2,1)} %param.34, s32[]{:T(128)S(6)} %select_n.157), kind=kOutput, calls=%fused_computation.38 | convolution fusion | flops 12884901888 | bytes 32505860 | tf_op jit(solution)/shard_map/dot_general | solution.py:460
  657.7 32.0 %fusion.13 = bf16[2048,768]{0,1:T(8,128)(2,1)} fusion(bf16[4096,2048]{1,0:T(8,128)(2,1)} %all-gather.3.cloned.1.call-done, f32[4096,768]{0,1:T(8,128)} %fusion.27, f32[4096,768]{0,1:T(8,128)} %fusion.29, f32[768,4096]{1,0:T(8,128)} %fusion.31), kind=kOutput, calls=%fused_computation.24 | convolution fusion | flops 12949389312 | bytes 57671680 | tf_op jit(solution)/shard_map/dot_general | solution.py:573
  689.8 25.5 %fusion.19 = bf16[768,2048]{1,0:T(8,128)(2,1)} fusion(bf16[4096,2048]{1,0:T(8,128)(2,1)} %all-gather.5.cloned.1.call-done, f32[4096,768]{0,1:T(8,128)} %fusion.29, f32[4096,768]{0,1:T(8,128)} %fusion.27), kind=kOutput, calls=%fused_computation.26 | convolution fusion | flops 12917932032 | bytes 45088768 | tf_op jit(solution)/shard_map/dot_general | solution.py:572
  715.7 3.3 broadcast_select_fusion.5
  719.0 6.4 maximum_convert_fusion
  725.4 12.6 %copy.54 = f32[2048,1536]{1,0:T(8,128)} copy(f32[2048,1536]{0,1:T(8,128)} %maximum_convert_fusion) | data formatting | bytes 25165824
  738.0 3.3 broadcast_select_fusion.3
  741.2 6.4 maximum_convert_fusion.1
  747.6 12.6 %copy.55 = f32[2048,1536]{1,0:T(8,128)} copy(f32[2048,1536]{0,1:T(8,128)} %maximum_convert_fusion.1) | data formatting | bytes 25165824
  760.2 3.3 broadcast_select_fusion.1
  763.5 6.4 maximum_convert_fusion.2
  (340 shorter events, 137.0 us)
Async XLA Ops:
  7.3 562.7 %all-gather.5.cloned.1.call-start = ((), (), s32[]{:S(2)}) async-start(), calls=%async_computation.1 | async-start | bytes 17301504 | tf_op jit(solution)/shard_map/all_gather | solution.py:425
  8.0 582.9 %all-gather.3.cloned.1.call-start = ((), (), s32[]{:S(2)}) async-start(), calls=%async_computation | async-start | bytes 17301504 | tf_op jit(solution)/shard_map/all_gather | solution.py:455
  12.2 37.6 %collective-permute-start.1 = (bf16[128,2048]{1,0:T(8,128)(2,1)}, bf16[128,2048]{1,0:T(8,128)(2,1)S(1)}, u32[]{:S(2)}, u32[]{:S(2)}) collective-permute-start(bf16[128,2048]{1,0:T(8,128)(2,1)} %get-tuple-element.62), channel_id=1, source_target_pairs={{0,2},{2,0},{1,3},{3,1},{4,6},{6,4},{5,7},{7,5},{8,10},{10,8},{9,1... | collective-permute-start | bytes 1572872 | tf_op jit(solution)/shard_map/ppermute | solution.py:28
  15.2 35.4 %collective-permute-start = (bf16[128,2048]{1,0:T(8,128)(2,1)}, bf16[128,2048]{1,0:T(8,128)(2,1)}, u32[]{:S(2)}, u32[]{:S(2)}) collective-permute-start(bf16[128,2048]{1,0:T(8,128)(2,1)} %get-tuple-element.62), channel_id=1, source_target_pairs={{0,1},{1,0},{2,3},{3,2},{4,5},{5,4},{6,7},{7,6},{8,9},{9,8},{10,11... | collective-permute-start | bytes 1572872 | tf_op jit(solution)/shard_map/ppermute | solution.py:27
  49.9 14.3 %collective-permute-start.3 = (bf16[64,2048]{1,0:T(8,128)(2,1)S(1)}, bf16[64,2048]{1,0:T(8,128)(2,1)S(1)}, u32[]{:S(2)}, u32[]{:S(2)}) collective-permute-start(bf16[64,2048]{1,0:T(8,128)(2,1)S(1)} %slice.403), channel_id=1, source_target_pairs={{0,1},{1,0},{2,3},{3,2},{4,5},{5,4},{6,7},{7,6},{8,9},{9,8},{10,11... | collective-permute-start | bytes 786440 | tf_op jit(solution)/shard_map/ppermute | solution.py:30
  51.6 8.8 %collective-permute-start.2 = (bf16[64,2048]{1,0:T(8,128)(2,1)S(1)}, bf16[64,2048]{1,0:T(8,128)(2,1)S(1)}, u32[]{:S(2)}, u32[]{:S(2)}) collective-permute-start(bf16[64,2048]{1,0:T(8,128)(2,1)S(1)} %slice.402), channel_id=1, source_target_pairs={{0,2},{2,0},{1,3},{3,1},{4,6},{6,4},{5,7},{7,5},{8,10},{10,8},{9,1... | collective-permute-start | bytes 786440 | tf_op jit(solution)/shard_map/ppermute | solution.py:29
  86.8 25.6 %collective-permute-start.4 = (bf16[256,1024]{1,0:T(8,128)(2,1)S(1)}, bf16[256,1024]{1,0:T(8,128)(2,1)S(1)}, u32[]{:S(2)}, u32[]{:S(2)}) collective-permute-start(bf16[256,1024]{1,0:T(8,128)(2,1)S(1)} %pad_maximum_fusion.6), channel_id=1, source_target_pairs={{0,1},{1,0},{2,3},{3,2},{4,5},{5,4},{6,7},{7,6},{8,9},{9,8},{10,11... | collective-permute-start | bytes 1572872 | tf_op jit(solution)/shard_map/ppermute | solution.py:40
  88.4 25.1 %collective-permute-start.6 = (bf16[256,1024]{1,0:T(8,128)(2,1)S(1)}, bf16[256,1024]{1,0:T(8,128)(2,1)S(1)}, u32[]{:S(2)}, u32[]{:S(2)}) collective-permute-start(bf16[256,1024]{1,0:T(8,128)(2,1)S(1)} %concatenate.137), channel_id=1, source_target_pairs={{0,2},{2,0},{1,3},{3,1},{4,6},{6,4},{5,7},{7,5},{8,10},{10,8},{9,1... | collective-permute-start | bytes 1572872 | tf_op jit(solution)/shard_map/ppermute | solution.py:43
  112.4 14.1 %collective-permute-start.5 = (bf16[128,1024]{1,0:T(8,128)(2,1)S(1)}, bf16[128,1024]{1,0:T(8,128)(2,1)S(1)}, u32[]{:S(2)}, u32[]{:S(2)}) collective-permute-start(bf16[128,1024]{1,0:T(8,128)(2,1)S(1)} %add_convert_fusion.18), channel_id=1, source_target_pairs={{0,2},{2,0},{1,3},{3,1},{4,6},{6,4},{5,7},{7,5},{8,10},{10,8},{9,1... | collective-permute-start | bytes 786440 | tf_op jit(solution)/shard_map/ppermute | solution.py:48
  126.7 6.4 collective-permute-start.7
  135.7 12.1 %collective-permute-start.17 = (bf16[128,2048]{1,0:T(8,128)(2,1)}, bf16[128,2048]{1,0:T(8,128)(2,1)S(1)}, u32[]{:S(2)}, u32[]{:S(2)}) collective-permute-start(bf16[128,2048]{1,0:T(8,128)(2,1)} %param.19), channel_id=1, source_target_pairs={{0,2},{2,0},{1,3},{3,1},{4,6},{6,4},{5,7},{7,5},{8,10},{10,8},{9,1... | collective-permute-start | bytes 1572872 | tf_op jit(solution)/shard_map/ppermute | solution.py:28
  136.5 11.7 %collective-permute-start.16 = (bf16[128,2048]{1,0:T(8,128)(2,1)}, bf16[128,2048]{1,0:T(8,128)(2,1)S(1)}, u32[]{:S(2)}, u32[]{:S(2)}) collective-permute-start(bf16[128,2048]{1,0:T(8,128)(2,1)} %param.19), channel_id=1, source_target_pairs={{0,1},{1,0},{2,3},{3,2},{4,5},{5,4},{6,7},{7,6},{8,9},{9,8},{10,11... | collective-permute-start | bytes 1572872 | tf_op jit(solution)/shard_map/ppermute | solution.py:27
  147.8 10.5 %collective-permute-start.19 = (bf16[64,2048]{1,0:T(8,128)(2,1)S(1)}, bf16[64,2048]{1,0:T(8,128)(2,1)S(1)}, u32[]{:S(2)}, u32[]{:S(2)}) collective-permute-start(bf16[64,2048]{1,0:T(8,128)(2,1)S(1)} %slice.427), channel_id=1, source_target_pairs={{0,1},{1,0},{2,3},{3,2},{4,5},{5,4},{6,7},{7,6},{8,9},{9,8},{10,11... | collective-permute-start | bytes 786440 | tf_op jit(solution)/shard_map/ppermute | solution.py:30
  148.2 10.1 %collective-permute-start.18 = (bf16[64,2048]{1,0:T(8,128)(2,1)S(1)}, bf16[64,2048]{1,0:T(8,128)(2,1)S(1)}, u32[]{:S(2)}, u32[]{:S(2)}) collective-permute-start(bf16[64,2048]{1,0:T(8,128)(2,1)S(1)} %slice.426), channel_id=1, source_target_pairs={{0,2},{2,0},{1,3},{3,1},{4,6},{6,4},{5,7},{7,5},{8,10},{10,8},{9,1... | collective-permute-start | bytes 786440 | tf_op jit(solution)/shard_map/ppermute | solution.py:29
  158.4 16.0 %collective-permute-start.9 = (bf16[128,2048]{1,0:T(8,128)(2,1)S(1)}, bf16[128,2048]{1,0:T(8,128)(2,1)S(1)}, u32[]{:S(2)}, u32[]{:S(2)}) collective-permute-start(bf16[128,2048]{1,0:T(8,128)(2,1)S(1)} %copy-done.19), channel_id=1, source_target_pairs={{0,2},{2,0},{1,3},{3,1},{4,6},{6,4},{5,7},{7,5},{8,10},{10,8},{9,1... | collective-permute-start | bytes 1572872 | tf_op jit(solution)/shard_map/ppermute | solution.py:28
  160.7 15.3 %collective-permute-start.8 = (bf16[128,2048]{1,0:T(8,128)(2,1)S(1)}, bf16[128,2048]{1,0:T(8,128)(2,1)S(1)}, u32[]{:S(2)}, u32[]{:S(2)}) collective-permute-start(bf16[128,2048]{1,0:T(8,128)(2,1)S(1)} %copy-done.19), channel_id=1, source_target_pairs={{0,1},{1,0},{2,3},{3,2},{4,5},{5,4},{6,7},{7,6},{8,9},{9,8},{10,11... | collective-permute-start | bytes 1572872 | tf_op jit(solution)/shard_map/ppermute | solution.py:27
  174.4 8.0 %collective-permute-start.11 = (bf16[64,2048]{1,0:T(8,128)(2,1)S(1)}, bf16[64,2048]{1,0:T(8,128)(2,1)S(1)}, u32[]{:S(2)}, u32[]{:S(2)}) collective-permute-start(bf16[64,2048]{1,0:T(8,128)(2,1)S(1)} %slice.415), channel_id=1, source_target_pairs={{0,1},{1,0},{2,3},{3,2},{4,5},{5,4},{6,7},{7,6},{8,9},{9,8},{10,11... | collective-permute-start | bytes 786440 | tf_op jit(solution)/shard_map/ppermute | solution.py:30
  176.0 6.4 collective-permute-start.10
  194.4 23.1 %collective-permute-start.12 = (bf16[256,1024]{1,0:T(8,128)(2,1)S(1)}, bf16[256,1024]{1,0:T(8,128)(2,1)S(1)}, u32[]{:S(2)}, u32[]{:S(2)}) collective-permute-start(bf16[256,1024]{1,0:T(8,128)(2,1)S(1)} %pad_maximum_fusion.7), channel_id=1, source_target_pairs={{0,1},{1,0},{2,3},{3,2},{4,5},{5,4},{6,7},{7,6},{8,9},{9,8},{10,11... | collective-permute-start | bytes 1572872 | tf_op jit(solution)/shard_map/ppermute | solution.py:40
  215.3 11.0 %collective-permute-start.20 = (bf16[256,1024]{1,0:T(8,128)(2,1)S(1)}, bf16[256,1024]{1,0:T(8,128)(2,1)S(1)}, u32[]{:S(2)}, u32[]{:S(2)}) collective-permute-start(bf16[256,1024]{1,0:T(8,128)(2,1)S(1)} %pad_maximum_fusion.8), channel_id=1, source_target_pairs={{0,1},{1,0},{2,3},{3,2},{4,5},{5,4},{6,7},{7,6},{8,9},{9,8},{10,11... | collective-permute-start | bytes 1572872 | tf_op jit(solution)/shard_map/ppermute | solution.py:40
  216.9 14.9 %collective-permute-start.14 = (bf16[256,1024]{1,0:T(8,128)(2,1)S(1)}, bf16[256,1024]{1,0:T(8,128)(2,1)S(1)}, u32[]{:S(2)}, u32[]{:S(2)}) collective-permute-start(bf16[256,1024]{1,0:T(8,128)(2,1)S(1)} %concatenate.138), channel_id=1, source_target_pairs={{0,2},{2,0},{1,3},{3,1},{4,6},{6,4},{5,7},{7,5},{8,10},{10,8},{9,1... | collective-permute-start | bytes 1572872 | tf_op jit(solution)/shard_map/ppermute | solution.py:43
  217.6 23.7 %collective-permute-start.13 = (bf16[128,1024]{1,0:T(8,128)(2,1)S(1)}, bf16[128,1024]{1,0:T(8,128)(2,1)S(1)}, u32[]{:S(2)}, u32[]{:S(2)}) collective-permute-start(bf16[128,1024]{1,0:T(8,128)(2,1)S(1)} %add_convert_fusion.16), channel_id=1, source_target_pairs={{0,2},{2,0},{1,3},{3,1},{4,6},{6,4},{5,7},{7,5},{8,10},{10,8},{9,1... | collective-permute-start | bytes 786440 | tf_op jit(solution)/shard_map/ppermute | solution.py:48
  219.2 39.0 %collective-permute-start.22 = (bf16[256,1024]{1,0:T(8,128)(2,1)S(1)}, bf16[256,1024]{1,0:T(8,128)(2,1)S(1)}, u32[]{:S(2)}, u32[]{:S(2)}) collective-permute-start(bf16[256,1024]{1,0:T(8,128)(2,1)S(1)} %concatenate.139), channel_id=1, source_target_pairs={{0,2},{2,0},{1,3},{3,1},{4,6},{6,4},{5,7},{7,5},{8,10},{10,8},{9,1... | collective-permute-start | bytes 1572872 | tf_op jit(solution)/shard_map/ppermute | solution.py:43
  226.3 42.3 %collective-permute-start.21 = (bf16[128,1024]{1,0:T(8,128)(2,1)S(1)}, bf16[128,1024]{1,0:T(8,128)(2,1)S(1)}, u32[]{:S(2)}, u32[]{:S(2)}) collective-permute-start(bf16[128,1024]{1,0:T(8,128)(2,1)S(1)} %add_convert_fusion.14), channel_id=1, source_target_pairs={{0,2},{2,0},{1,3},{3,1},{4,6},{6,4},{5,7},{7,5},{8,10},{10,8},{9,1... | collective-permute-start | bytes 786440 | tf_op jit(solution)/shard_map/ppermute | solution.py:48
  241.5 27.7 %collective-permute-start.15 = (bf16[128,1024]{1,0:T(8,128)(2,1)S(1)}, bf16[128,1024]{1,0:T(8,128)(2,1)S(1)}, u32[]{:S(2)}, u32[]{:S(2)}) collective-permute-start(bf16[128,1024]{1,0:T(8,128)(2,1)S(1)} %get-tuple-element.94), channel_id=1, source_target_pairs={{0,1},{1,0},{2,3},{3,2},{4,5},{5,4},{6,7},{7,6},{8,9},{9,8},{10,11... | collective-permute-start | bytes 786440 | tf_op jit(solution)/shard_map/ppermute | solution.py:49
  268.8 7.3 collective-permute-start.23
  279.7 12.3 %collective-permute-start.25 = (bf16[128,2048]{1,0:T(8,128)(2,1)}, bf16[128,2048]{1,0:T(8,128)(2,1)}, u32[]{:S(2)}, u32[]{:S(2)}) collective-permute-start(bf16[128,2048]{1,0:T(8,128)(2,1)} %get-tuple-element.55), channel_id=1, source_target_pairs={{0,2},{2,0},{1,3},{3,1},{4,6},{6,4},{5,7},{7,5},{8,10},{10,8},{9,1... | collective-permute-start | bytes 1572872 | tf_op jit(solution)/shard_map/ppermute | solution.py:28
  281.2 12.2 %collective-permute-start.24 = (bf16[128,2048]{1,0:T(8,128)(2,1)}, bf16[128,2048]{1,0:T(8,128)(2,1)}, u32[]{:S(2)}, u32[]{:S(2)}) collective-permute-start(bf16[128,2048]{1,0:T(8,128)(2,1)} %get-tuple-element.55), channel_id=1, source_target_pairs={{0,1},{1,0},{2,3},{3,2},{4,5},{5,4},{6,7},{7,6},{8,9},{9,8},{10,11... | collective-permute-start | bytes 1572872 | tf_op jit(solution)/shard_map/ppermute | solution.py:27
  293.0 8.5 %collective-permute-start.27 = (bf16[64,2048]{1,0:T(8,128)(2,1)S(1)}, bf16[64,2048]{1,0:T(8,128)(2,1)S(1)}, u32[]{:S(2)}, u32[]{:S(2)}) collective-permute-start(bf16[64,2048]{1,0:T(8,128)(2,1)S(1)} %slice.439), channel_id=1, source_target_pairs={{0,1},{1,0},{2,3},{3,2},{4,5},{5,4},{6,7},{7,6},{8,9},{9,8},{10,11... | collective-permute-start | bytes 786440 | tf_op jit(solution)/shard_map/ppermute | solution.py:30
  294.3 6.4 collective-permute-start.26
  322.4 7.0 collective-permute-start.49
  327.6 14.5 %collective-permute-start.28 = (bf16[256,1024]{1,0:T(8,128)(2,1)S(1)}, bf16[256,1024]{1,0:T(8,128)(2,1)}, u32[]{:S(2)}, u32[]{:S(2)}) collective-permute-start(bf16[256,1024]{1,0:T(8,128)(2,1)S(1)} %pad_maximum_fusion.9), channel_id=1, source_target_pairs={{0,1},{1,0},{2,3},{3,2},{4,5},{5,4},{6,7},{7,6},{8,9},{9,8},{10,11... | collective-permute-start | bytes 1572872 | tf_op jit(solution)/shard_map/ppermute | solution.py:40
  329.6 10.7 %collective-permute-start.50 = (bf16[4,160,160]{2,1,0:T(8,128)(2,1)S(1)}, bf16[4,160,160]{2,1,0:T(8,128)(2,1)S(1)}, u32[]{:S(2)}, u32[]{:S(2)}) collective-permute-start(bf16[4,160,160]{2,1,0:T(8,128)(2,1)S(1)} %add_convert_fusion.10), channel_id=1, source_target_pairs={{0,8},{24,16},{1,9},{25,17},{2,10},{26,18},{3,11},{27,19},{4,12},{... | collective-permute-start | bytes 614408 | tf_op jit(solution)/shard_map/ppermute | solution.py:78
  336.1 23.5 %collective-permute-start.38 = (bf16[512,1024]{1,0:T(8,128)(2,1)}, bf16[512,1024]{1,0:T(8,128)(2,1)}, u32[]{:S(2)}, u32[]{:S(2)}) collective-permute-start(bf16[512,1024]{1,0:T(8,128)(2,1)} %get-tuple-element.84), channel_id=1, source_target_pairs={{0,4},{4,0},{1,5},{5,1},{2,6},{6,2},{3,7},{7,3},{8,12},{12,8},{9,1... | collective-permute-start | bytes 3145736 | tf_op jit(solution)/shard_map/ppermute | solution.py:56
  336.1 24.8 %collective-permute-start.44 = (bf16[512,640]{1,0:T(8,128)(2,1)S(1)}, bf16[512,640]{1,0:T(8,128)(2,1)}, u32[]{:S(2)}, u32[]{:S(2)}) collective-permute-start(bf16[512,640]{1,0:T(8,128)(2,1)S(1)} %get-tuple-element.30), channel_id=1, source_target_pairs={{0,4},{4,0},{1,5},{5,1},{2,6},{6,2},{3,7},{7,3},{8,12},{12,8},{9,1... | collective-permute-start | bytes 1966088 | tf_op jit(solution)/shard_map/ppermute | solution.py:56
  338.6 15.1 %collective-permute-start.30 = (bf16[256,1024]{1,0:T(8,128)(2,1)}, bf16[256,1024]{1,0:T(8,128)(2,1)}, u32[]{:S(2)}, u32[]{:S(2)}) collective-permute-start(bf16[256,1024]{1,0:T(8,128)(2,1)} %concatenate.140), channel_id=1, source_target_pairs={{0,2},{2,0},{1,3},{3,1},{4,6},{6,4},{5,7},{7,5},{8,10},{10,8},{9,1... | collective-permute-start | bytes 1572872 | tf_op jit(solution)/shard_map/ppermute | solution.py:43
  340.5 5.9 collective-permute-start.51
  343.2 15.0 %collective-permute-start.29 = (bf16[128,1024]{1,0:T(8,128)(2,1)S(1)}, bf16[128,1024]{1,0:T(8,128)(2,1)S(1)}, u32[]{:S(2)}, u32[]{:S(2)}) collective-permute-start(bf16[128,1024]{1,0:T(8,128)(2,1)S(1)} %add_convert_fusion.12), channel_id=1, source_target_pairs={{0,2},{2,0},{1,3},{3,1},{4,6},{6,4},{5,7},{7,5},{8,10},{10,8},{9,1... | collective-permute-start | bytes 786440 | tf_op jit(solution)/shard_map/ppermute | solution.py:48
  346.5 39.3 %collective-permute-start.54 = (bf16[512,640]{1,0:T(8,128)(2,1)S(1)}, bf16[512,640]{1,0:T(8,128)(2,1)S(1)}, u32[]{:S(2)}, u32[]{:S(2)}) collective-permute-start(bf16[512,640]{1,0:T(8,128)(2,1)S(1)} %copy-done.8), channel_id=1, source_target_pairs={{0,4},{4,0},{1,5},{5,1},{2,6},{6,2},{3,7},{7,3},{8,12},{12,8},{9,1... | collective-permute-start | bytes 1966088 | tf_op jit(solution)/shard_map/ppermute | solution.py:56
  353.7 21.9 %collective-permute-start.39 = (bf16[512,640]{1,0:T(8,128)(2,1)}, bf16[512,640]{1,0:T(8,128)(2,1)S(1)}, u32[]{:S(2)}, u32[]{:S(2)}) collective-permute-start(bf16[512,640]{1,0:T(8,128)(2,1)} %copy-done.43), channel_id=1, source_target_pairs={{0,4},{4,0},{1,5},{5,1},{2,6},{6,2},{3,7},{7,3},{8,12},{12,8},{9,1... | collective-permute-start | bytes 1966088 | tf_op jit(solution)/shard_map/ppermute | solution.py:56
  358.2 28.1 %collective-permute-start.55 = (bf16[512,1024]{1,0:T(8,128)(2,1)}, bf16[512,1024]{1,0:T(8,128)(2,1)S(1)}, u32[]{:S(2)}, u32[]{:S(2)}) collective-permute-start(bf16[512,1024]{1,0:T(8,128)(2,1)} %get-tuple-element.82), channel_id=1, source_target_pairs={{0,4},{4,0},{1,5},{5,1},{2,6},{6,2},{3,7},{7,3},{8,12},{12,8},{9,1... | collective-permute-start | bytes 3145736 | tf_op jit(solution)/shard_map/ppermute | solution.py:56
  359.6 22.3 %collective-permute-start.52 = (bf16[4,160,160]{2,1,0:T(8,128)(2,1)S(1)}, bf16[4,160,160]{2,1,0:T(8,128)(2,1)S(1)}, u32[]{:S(2)}, u32[]{:S(2)}) collective-permute-start(bf16[4,160,160]{2,1,0:T(8,128)(2,1)S(1)} %add_convert_fusion.8), channel_id=1, source_target_pairs={{8,0},{16,24},{9,1},{17,25},{10,2},{18,26},{11,3},{19,27},{12,4},{... | collective-permute-start | bytes 614408 | tf_op jit(solution)/shard_map/ppermute | solution.py:82
  360.9 8.8 %collective-permute-start.31 = (bf16[128,1024]{1,0:T(8,128)(2,1)S(1)}, bf16[128,1024]{1,0:T(8,128)(2,1)S(1)}, u32[]{:S(2)}, u32[]{:S(2)}) collective-permute-start(bf16[128,1024]{1,0:T(8,128)(2,1)S(1)} %get-tuple-element.86), channel_id=1, source_target_pairs={{0,1},{1,0},{2,3},{3,2},{4,5},{5,4},{6,7},{7,6},{8,9},{9,8},{10,11... | collective-permute-start | bytes 786440 | tf_op jit(solution)/shard_map/ppermute | solution.py:49
  369.7 33.5 %collective-permute-start.45 = (bf16[1024,640]{1,0:T(8,128)(2,1)S(1)}, bf16[1024,640]{1,0:T(8,128)(2,1)S(1)}, u32[]{:S(2)}, u32[]{:S(2)}) collective-permute-start(bf16[1024,640]{1,0:T(8,128)(2,1)S(1)} %convolution_convert_fusion.2), channel_id=1, source_target_pairs={{0,8},{24,16},{1,9},{25,17},{2,10},{26,18},{3,11},{27,19},{4,12},{... | collective-permute-start | bytes 3932168 | tf_op jit(solution)/shard_map/ppermute | solution.py:78
  375.7 4.6 collective-permute-start.32
  380.3 51.0 %collective-permute-start.40 = (bf16[1024,640]{1,0:T(8,128)(2,1)S(1)}, bf16[1024,640]{1,0:T(8,128)(2,1)S(1)}, u32[]{:S(2)}, u32[]{:S(2)}) collective-permute-start(bf16[1024,640]{1,0:T(8,128)(2,1)S(1)} %convolution_convert_fusion.3), channel_id=1, source_target_pairs={{0,8},{24,16},{1,9},{25,17},{2,10},{26,18},{3,11},{27,19},{4,12},{... | collective-permute-start | bytes 3932168 | tf_op jit(solution)/shard_map/ppermute | solution.py:78
  381.9 3.8 collective-permute-start.33
  385.7 46.7 %collective-permute-start.53 = (bf16[4,160,160]{2,1,0:T(8,128)(2,1)S(1)}, bf16[4,160,160]{2,1,0:T(8,128)(2,1)S(1)}, u32[]{:S(2)}, u32[]{:S(2)}) collective-permute-start(bf16[4,160,160]{2,1,0:T(8,128)(2,1)S(1)} %broadcast_select_fusion.15), channel_id=1, source_target_pairs={{0,4},{4,0},{1,5},{5,1},{2,6},{6,2},{3,7},{7,3},{8,12},{12,8},{9,1... | collective-permute-start | bytes 614408 | tf_op jit(solution)/shard_map/ppermute | solution.py:56
  385.7 3.5 collective-permute-start.34
  387.9 72.7 %collective-permute-start.56 = (bf16[640,1024]{1,0:T(8,128)(2,1)S(1)}, bf16[640,1024]{1,0:T(8,128)(2,1)S(1)}, u32[]{:S(2)}, u32[]{:S(2)}) collective-permute-start(bf16[640,1024]{1,0:T(8,128)(2,1)S(1)} %fusion.42), channel_id=1, source_target_pairs={{0,8},{24,16},{1,9},{25,17},{2,10},{26,18},{3,11},{27,19},{4,12},{... | collective-permute-start | bytes 3932168 | tf_op jit(solution)/shard_map/ppermute | solution.py:78
  389.3 69.3 %collective-permute-start.35 = (f32[72,128]{1,0:T(8,128)S(1)}, f32[72,128]{1,0:T(8,128)S(1)}, u32[]{:S(2)}, u32[]{:S(2)}) collective-permute-start(f32[72,128]{1,0:T(8,128)S(1)} %fusion.114), channel_id=1, source_target_pairs={{0,8},{24,16},{1,9},{25,17},{2,10},{26,18},{3,11},{27,19},{4,12},{... | collective-permute-start | bytes 110600 | tf_op jit(solution)/shard_map/ppermute | solution.py:78
  403.5 58.3 %collective-permute-start.46 = (bf16[1024,640]{1,0:T(8,128)(2,1)S(1)}, bf16[1024,640]{1,0:T(8,128)(2,1)S(1)}, u32[]{:S(2)}, u32[]{:S(2)}) collective-permute-start(bf16[1024,640]{1,0:T(8,128)(2,1)S(1)} %add_convert_fusion.5), channel_id=1, source_target_pairs={{8,16},{16,8},{9,17},{17,9},{10,18},{18,10},{11,19},{19,11},{12,20... | collective-permute-start | bytes 3932168 | tf_op jit(solution)/shard_map/ppermute | solution.py:80
  431.6 32.0 %collective-permute-start.41 = (bf16[1024,640]{1,0:T(8,128)(2,1)S(1)}, bf16[1024,640]{1,0:T(8,128)(2,1)S(1)}, u32[]{:S(2)}, u32[]{:S(2)}) collective-permute-start(bf16[1024,640]{1,0:T(8,128)(2,1)S(1)} %add_convert_fusion.7), channel_id=1, source_target_pairs={{8,16},{16,8},{9,17},{17,9},{10,18},{18,10},{11,19},{19,11},{12,20... | collective-permute-start | bytes 3932168 | tf_op jit(solution)/shard_map/ppermute | solution.py:80
  459.3 10.8 %collective-permute-start.37 = (f32[72,128]{1,0:T(8,128)S(1)}, f32[72,128]{1,0:T(8,128)S(1)}, u32[]{:S(2)}, u32[]{:S(2)}) collective-permute-start(f32[72,128]{1,0:T(8,128)S(1)} %add.280), channel_id=1, source_target_pairs={{8,0},{16,24},{9,1},{17,25},{10,2},{18,26},{11,3},{19,27},{12,4},{... | collective-permute-start | bytes 110600 | tf_op jit(solution)/shard_map/ppermute | solution.py:82
  461.1 9.0 %collective-permute-start.57 = (bf16[640,1024]{1,0:T(8,128)(2,1)S(1)}, bf16[640,1024]{1,0:T(8,128)(2,1)S(1)}, u32[]{:S(2)}, u32[]{:S(2)}) collective-permute-start(bf16[640,1024]{1,0:T(8,128)(2,1)S(1)} %add_convert_fusion.3), channel_id=1, source_target_pairs={{8,16},{16,8},{9,17},{17,9},{10,18},{18,10},{11,19},{19,11},{12,20... | collective-permute-start | bytes 3932168 | tf_op jit(solution)/shard_map/ppermute | solution.py:80
  462.2 41.4 %collective-permute-start.47 = (bf16[1024,640]{1,0:T(8,128)(2,1)S(1)}, bf16[1024,640]{1,0:T(8,128)(2,1)S(1)}, u32[]{:S(2)}, u32[]{:S(2)}) collective-permute-start(bf16[1024,640]{1,0:T(8,128)(2,1)S(1)} %add_convert_fusion.4), channel_id=1, source_target_pairs={{8,0},{16,24},{9,1},{17,25},{10,2},{18,26},{11,3},{19,27},{12,4},{... | collective-permute-start | bytes 3932168 | tf_op jit(solution)/shard_map/ppermute | solution.py:82
  464.0 67.7 %collective-permute-start.42 = (bf16[1024,640]{1,0:T(8,128)(2,1)S(1)}, bf16[1024,640]{1,0:T(8,128)(2,1)S(1)}, u32[]{:S(2)}, u32[]{:S(2)}) collective-permute-start(bf16[1024,640]{1,0:T(8,128)(2,1)S(1)} %add_convert_fusion.6), channel_id=1, source_target_pairs={{8,0},{16,24},{9,1},{17,25},{10,2},{18,26},{11,3},{19,27},{12,4},{... | collective-permute-start | bytes 3932168 | tf_op jit(solution)/shard_map/ppermute | solution.py:82
  471.7 84.6 %collective-permute-start.58 = (bf16[640,1024]{1,0:T(8,128)(2,1)}, bf16[640,1024]{1,0:T(8,128)(2,1)}, u32[]{:S(2)}, u32[]{:S(2)}) collective-permute-start(bf16[640,1024]{1,0:T(8,128)(2,1)} %add_convert_fusion.2), channel_id=1, source_target_pairs={{8,0},{16,24},{9,1},{17,25},{10,2},{18,26},{11,3},{19,27},{12,4},{... | collective-permute-start | bytes 3932168 | tf_op jit(solution)/shard_map/ppermute | solution.py:82
  503.8 54.0 %collective-permute-start.48 = (bf16[1024,640]{1,0:T(8,128)(2,1)S(1)}, bf16[1024,640]{1,0:T(8,128)(2,1)}, u32[]{:S(2)}, u32[]{:S(2)}) collective-permute-start(bf16[1024,640]{1,0:T(8,128)(2,1)S(1)} %broadcast_select_fusion.9), channel_id=1, source_target_pairs={{0,4},{4,0},{1,5},{5,1},{2,6},{6,2},{3,7},{7,3},{8,12},{12,8},{9,1... | collective-permute-start | bytes 3932168 | tf_op jit(solution)/shard_map/ppermute | solution.py:56
  533.0 29.1 %collective-permute-start.43 = (bf16[1024,640]{1,0:T(8,128)(2,1)}, bf16[1024,640]{1,0:T(8,128)(2,1)}, u32[]{:S(2)}, u32[]{:S(2)}) collective-permute-start(bf16[1024,640]{1,0:T(8,128)(2,1)} %broadcast_select_fusion.10), channel_id=1, source_target_pairs={{0,4},{4,0},{1,5},{5,1},{2,6},{6,2},{3,7},{7,3},{8,12},{12,8},{9,1... | collective-permute-start | bytes 3932168 | tf_op jit(solution)/shard_map/ppermute | solution.py:56
  557.7 9.0 %collective-permute-start.59 = (bf16[640,1024]{1,0:T(8,128)(2,1)S(1)}, bf16[640,1024]{1,0:T(8,128)(2,1)S(1)}, u32[]{:S(2)}, u32[]{:S(2)}) collective-permute-start(bf16[640,1024]{1,0:T(8,128)(2,1)S(1)} %broadcast_select_fusion.6), channel_id=1, source_target_pairs={{0,4},{4,0},{1,5},{5,1},{2,6},{6,2},{3,7},{7,3},{8,12},{12,8},{9,1... | collective-permute-start | bytes 3932168 | tf_op jit(solution)/shard_map/ppermute | solution.py:56
  636.8 101.2 %collective-permute-start.61 = (bf16[2048,768]{0,1:T(8,128)(2,1)}, bf16[2048,768]{0,1:T(8,128)(2,1)}, u32[]{:S(2)}, u32[]{:S(2)}) collective-permute-start(bf16[2048,768]{0,1:T(8,128)(2,1)} %fusion.16), channel_id=1, source_target_pairs={{0,4},{4,0},{1,5},{5,1},{2,6},{6,2},{3,7},{7,3},{8,12},{12,8},{9,1... | collective-permute-start | bytes 9437192 | tf_op jit(solution)/shard_map/ppermute | solution.py:56
  689.7 26.1 %collective-permute-start.60 = (bf16[2048,768]{0,1:T(8,128)(2,1)}, bf16[2048,768]{0,1:T(8,128)(2,1)}, u32[]{:S(2)}, u32[]{:S(2)}) collective-permute-start(bf16[2048,768]{0,1:T(8,128)(2,1)} %fusion.13), channel_id=1, source_target_pairs={{0,4},{4,0},{1,5},{5,1},{2,6},{6,2},{3,7},{7,3},{8,12},{12,8},{9,1... | collective-permute-start | bytes 9437192 | tf_op jit(solution)/shard_map/ppermute | solution.py:56
  715.3 44.9 %collective-permute-start.62 = (bf16[768,2048]{1,0:T(8,128)(2,1)}, bf16[768,2048]{1,0:T(8,128)(2,1)}, u32[]{:S(2)}, u32[]{:S(2)}) collective-permute-start(bf16[768,2048]{1,0:T(8,128)(2,1)} %fusion.19), channel_id=1, source_target_pairs={{0,4},{4,0},{1,5},{5,1},{2,6},{6,2},{3,7},{7,3},{8,12},{12,8},{9,1... | collective-permute-start | bytes 9437192 | tf_op jit(solution)/shard_map/ppermute | solution.py:56
  (54 other events, 639.1 us)
Sparse Core Ops, SparseCore 0:
  11.0 142.0 all-gather.4
  156.0 145.6 all-gather.2

commit v2 on v1

--- a/solution.py
+++ b/solution.py
@@ -15,41 +15,61 @@
 f32 = jnp.float32
 bf16 = jnp.bfloat16
 swap = [(0, 1), (1, 0)]
+brief = pl.CostEstimate(flops=1, bytes_accessed=1, transcendentals=0)
+large = pltpu.CompilerParams(vmem_limit_bytes=48 * 1024 * 1024)
 ALL = ("z", "core", "y", "x")
 STEP = 16
 root_two_over_pi = 0.7978845608028654
 
 
-def gather_row(part, square):
+def pass_kernel(*refs):
+    pass
+
+
+def held(values, after):
+    values, after = list(values), list(after)
+    anywhere = pl.BlockSpec(memory_space=pl.ANY)
+    return pl.pallas_call(
+        pass_kernel,
+        in_specs=[anywhere] * (len(values) + len(after)),
+        out_specs=[anywhere] * len(values),
+        out_shape=[jax.ShapeDtypeStruct(value.shape, value.dtype) for value in values],
+        input_output_aliases={n: n for n in range(len(values))},
+        cost_estimate=brief,
+    )(*values, *after)
+
+
+def gather_row(halves, square, beside=()):
     if not square:
-        return lax.all_gather(part, ("y", "x"), axis=0, tiled=True)
-    half = part.shape[0] // 2
-    from_x = lax.ppermute(part, "x", swap)
-    from_y = lax.ppermute(part, "y", swap)
-    diag_a = lax.ppermute(from_x[:half], "y", swap)
-    diag_b = lax.ppermute(from_y[half:], "x", swap)
-    return jnp.concatenate([part, from_x, from_y, diag_a, diag_b], axis=0)
-
-
-def scatter_row(partial, square):
+        return [lax.all_gather(jnp.concatenate(halves, axis=0), ("y", "x"), axis=0, tiled=True)]
+    one, two = halves
+    one_x = lax.ppermute(one, "x", swap)
+    two_y = lax.ppermute(two, "y", swap)
+    two_x = lax.ppermute(two, "x", swap)
+    one_y = lax.ppermute(one, "y", swap)
+    if beside:
+        one_x, two_y = held((one_x, two_y), beside)
+    one_d = lax.ppermute(one_x, "y", swap)
+    two_d = lax.ppermute(two_y, "x", swap)
+    return [one, one_x, one_y, one_d, two, two_x, two_y, two_d]
+
+
+def scatter_row(sends, square, beside=()):
     if not square:
-        return lax.psum_scatter(partial, ("y", "x"), scatter_dimension=0, tiled=True).astype(f32)
-    rows = partial.shape[0] // 4
-    cut = partial.shape[1] // 2
-    blocks = [partial[k * rows : (k + 1) * rows] for k in range(4)]
-    got_x = lax.ppermute(
-        jnp.concatenate([blocks[1][:, :cut], blocks[3][:, :cut]], axis=0), "x", swap
-    )
-    got_y = lax.ppermute(
-        jnp.concatenate([blocks[2][:, cut:], blocks[3][:, cut:]], axis=0), "y", swap
-    )
-    send_y = (blocks[2][:, :cut].astype(f32) + got_x[rows:].astype(f32)).astype(bf16)
-    send_x = (blocks[1][:, cut:].astype(f32) + got_y[rows:].astype(f32)).astype(bf16)
+        return [lax.psum_scatter(sends[0], ("y", "x"), scatter_dimension=0, tiled=True)]
+    to_x, to_y, keep_x, keep_y, own = sends
+    got_x = lax.ppermute(to_x, "x", swap)
+    got_y = lax.ppermute(to_y, "y", swap)
+    if beside:
+        got_x, got_y = held((got_x, got_y), beside)
+    send_y, send_x = pl.pallas_call(
+        middle_kernel,
+        out_shape=[jax.ShapeDtypeStruct(keep_x.shape, bf16)] * 2,
+        cost_estimate=brief,
+    )(got_x, got_y, keep_x, keep_y)
     last_y = lax.ppermute(send_y, "y", swap)
     last_x = lax.ppermute(send_x, "x", swap)
-    left = blocks[0][:, :cut].astype(f32) + got_x[:rows].astype(f32) + last_y.astype(f32)
-    right = blocks[0][:, cut:].astype(f32) + got_y[:rows].astype(f32) + last_x.astype(f32)
-    return jnp.concatenate([left, right], axis=1)
+    return [own, got_x, got_y, last_y, last_x]
 
 
 def sibling(value):
@@ -67,21 +87,188 @@
     return jnp.concatenate([first, second], axis=axis).astype(f32)
 
 
-def line_sums(pieces, depth):
-    if depth != 4:
-        return [lax.psum(piece, "z") for piece in pieces]
+def line_sums(groups, beside):
     place = lax.axis_index("z")
     inner = (place == 1) | (place == 2)
-    totals = []
+    pairs = [[(0, 1), (3, 2)], [(1, 2), (2, 1)], [(1, 0), (2, 3)]]
+    groups = [list(group) for group in groups]
+    for step in range(len(groups) + 2):
+        moves = [(step - stage, stage) for stage in range(3) if 0 <= step - stage < len(groups)]
+        got = [lax.ppermute(piece, "z", pairs[stage]) for n, stage in moves for piece in groups[n]]
+        if beside[step]:
+            got = held(got, beside[step])
+        got = list(got)
+        for n, stage in moves:
+            for k, piece in enumerate(groups[n]):
+                other = got.pop(0)
+                if stage < 2:
+                    groups[n][k] = (piece.astype(f32) + other.astype(f32)).astype(piece.dtype)
+                else:
+                    groups[n][k] = jnp.where(inner, piece, other)
+    return groups
+
+
+def assemble(pieces, out_ref):
+    at = 0
     for piece in pieces:
-        kind = piece.dtype
-        inward = lax.ppermute(piece, "z", [(0, 1), (3, 2)])
-        side = (piece.astype(f32) + inward.astype(f32)).astype(kind)
-        across = lax.ppermute(side, "z", [(1, 2), (2, 1)])
-        total = (side.astype(f32) + across.astype(f32)).astype(kind)
-        outward = lax.ppermute(total, "z", [(1, 0), (2, 3)])
-        totals.append(jnp.where(inner, total, outward))
-    return totals
+        out_ref[at : at + piece.shape[0], :] = piece[...]
+        at += piece.shape[0]
+
+
+def send_shapes(length, width, plain):
+    if plain:
+        return [jax.ShapeDtypeStruct((length, width), bf16)]
+    block, cut = length // 4, width // 2
+    return (
+        [jax.ShapeDtypeStruct((2 * block, cut), bf16)] * 2
+        + [jax.ShapeDtypeStruct((block, cut), bf16)] * 2
+        + [jax.ShapeDtypeStruct((block, width), f32)]
+    )
+
+
+def emit(value, first, width, sends, plain):
+    last = first + value.shape[1]
+    if plain:
+        sends[0][:, first:last] = value.astype(bf16)
+        return
+    to_x, to_y, keep_x, keep_y, own = sends
+    cut = width // 2
+    half = value.shape[0] // 8
+
+    def put(ref, at, block, cols, kind):
+        for n in range(2):
+            rows = slice(n * 4 * half + block * half, n * 4 * half + (block + 1) * half)
+            ref[at + n * half : at + (n + 1) * half, cols] = value[rows].astype(kind)
+
+    put(own, 0, 0, slice(first, last), f32)
+    if last <= cut:
+        cols = slice(first, last)
+        put(to_x, 0, 1, cols, bf16)
+        put(to_x, 2 * half, 3, cols, bf16)
+        put(keep_y, 0, 2, cols, bf16)
+    else:
+        cols = slice(first - cut, last - cut)
+        put(to_y, 0, 2, cols, bf16)
+        put(to_y, 2 * half, 3, cols, bf16)
+        put(keep_x, 0, 1, cols, bf16)
+
+
+def middle_kernel(got_x, got_y, keep_x, keep_y, send_y, send_x):
+    block = keep_x.shape[0]
+    send_y[...] = (keep_y[...].astype(f32) + got_x[block:].astype(f32)).astype(bf16)
+    send_x[...] = (keep_x[...].astype(f32) + got_y[block:].astype(f32)).astype(bf16)
+
+
+def finish(refs):
+    if len(refs) == 1:
+        return refs[0][...].astype(f32)
+    own, got_x, got_y, last_y, last_x = refs
+    block, cut = last_y.shape
+    left = own[:, :cut] + got_x[:block].astype(f32) + last_y[...].astype(f32)
+    right = own[:, cut:] + got_y[:block].astype(f32) + last_x[...].astype(f32)
+    return jnp.concatenate([left, right], axis=1)
+
+
+def mean_of(x):
+    return jnp.mean(x, axis=-1, keepdims=True)
+
+
+def norm_kernel(input_ref, gain_ref, one_ref, two_ref):
+    values = input_ref[...].astype(f32)
+    normed = (values * lax.rsqrt(mean_of(values * values) + eps) * gain_ref[...]).astype(bf16)
+    half = normed.shape[0] // 2
+    one_ref[...] = normed[:half]
+    two_ref[...] = normed[half:]
+
+
+def second_norm_kernel(input_ref, gain_ref, *refs, cuts):
+    hidden_ref, one_ref, two_ref, *parts = refs[-3 - len(cuts) + 1 :]
+    addends = refs[: -3 - len(cuts) + 1]
+    hidden = input_ref[...].astype(f32) + finish(addends)
+    hidden_ref[...] = hidden
+    normed = (hidden * lax.rsqrt(mean_of(hidden * hidden) + eps) * gain_ref[...]).astype(bf16)
+    half = normed.shape[0] // 2
+    one_ref[...] = normed[:half]
+    two_ref[...] = normed[half:]
+    for ref, first, last in zip(parts, cuts[:-1], cuts[1:], strict=True):
+        ref[...] = normed[first:last]
+
+
+def norm_back_kernel(value_ref, before_ref, gain_ref, *refs, final):
+    outs = 2 if final else 4
+    addends, outs = refs[:-outs], refs[-outs:]
+    values = value_ref[...].astype(f32)
+    scale = lax.rsqrt(mean_of(values * values) + eps)
+    hat = values * scale
+    grad = finish(addends)
+    outs[0][...] = jnp.sum(grad * hat, axis=0, keepdims=True)
+    scaled = grad * gain_ref[...]
+    total = before_ref[...].astype(f32) + scale * (scaled - hat * mean_of(scaled * hat))
+    if final:
+        outs[1][...] = total.astype(bf16)
+        return
+    outs[1][...] = total
+    low = total.astype(bf16)
+    half = low.shape[0] // 2
+    outs[2][...] = low[:half]
+    outs[3][...] = low[half:]
+
+
+def add_kernel(value_ref, *refs):
+    refs[-1][...] = (value_ref[...] + finish(refs[:-1])).astype(bf16)
+
+
+def mlp_kernel(*refs, count, plain, keep):
+    pieces, (grad_ref, gate_w, up_w), refs = refs[:count], refs[count : count + 3], refs[count + 3 :]
+    *outs, token_ref, total_ref = refs
+    token_out, activ_ref, *outs = outs
+    step = pl.program_id(0)
+
+    @pl.when(step == 0)
+    def _():
+        assemble(pieces, token_ref)
+        token_out[...] = token_ref[...]
+
+    tokens = token_ref[...]
+    gate_pre = jnp.dot(tokens, gate_w[...], preferred_element_type=f32)
+    up_pre = jnp.dot(tokens, up_w[...], preferred_element_type=f32)
+    activ_grad = grad_ref[...]
+    value, slope = gelu_terms(gate_pre)
+    activ_ref[...] = (value * up_pre).astype(bf16)
+    gate_low = (activ_grad * up_pre * slope).astype(bf16)
+    up_low = (activ_grad * value).astype(bf16)
+    if keep:
+        outs[0][...] = gate_low
+        outs[1][...] = up_low
+        outs = outs[2:]
+    width = total_ref.shape[1]
+    last = step == pl.num_programs(0) - 1
+    for first in range(0, width, 512):
+        cols = slice(first, first + 512)
+        part = lax.dot_general(
+            gate_low, gate_w[cols, :], contract_cols, preferred_element_type=f32
+        ) + lax.dot_general(up_low, up_w[cols, :], contract_cols, preferred_element_type=f32)
+
+        @pl.when(step == 0)
+        def _(part=part, cols=cols):
+            total_ref[:, cols] = part
+
+        @pl.when(step > 0)
+        def _(part=part, cols=cols):
+            total_ref[:, cols] += part
+
+    @pl.when(last)
+    def _():
+        for first in range(0, width, 512):
+            emit(total_ref[:, first : first + 512], first, width, outs, plain)
+
+
+def down_kernel(activ_ref, weight_ref, *sends, plain):
+    width = weight_ref.shape[1]
+    for first in range(0, width, 512):
+        cols = slice(first, first + 512)
+        value = jnp.dot(activ_ref[...], weight_ref[:, cols], preferred_element_type=f32)
+        emit(value, first, width, sends, plain)
 
 
 def tile_span(first, last, head, width):
@@ -124,36 +311,57 @@
     return jnp.concatenate([mask] * (-(-width // 128)), axis=1)[:, :width]
 
 
-def forward_kernel(
-    spot_ref,
-    branch_ref,
-    stream_ref,
-    joined_ref,
-    taps_ref,
-    bias_ref,
-    high_ref,
-    low_ref,
-    gate_bias_ref,
-    soft_ref,
-    gated_ref,
-    conv_ref,
-    recur_ref,
-    intake_ref,
-    state_ref,
-    part_high,
-    part_low,
-    *,
-    head,
-):
+def token_place(length, spot, plain):
+    block, half = length // 4, length // 8
+    per_block = block // STEP
+    per_half = half // STEP
+
+    def offset(step):
+        if plain:
+            return pl.multiple_of(step * STEP, STEP)
+        turn = lax.bitwise_xor(step // per_block, spot)
+        inside = lax.rem(step, per_block)
+        at = (inside // per_half) * (length // 2) + turn * half + lax.rem(inside, per_half) * STEP
+        return pl.multiple_of(at, STEP)
+
+    return offset
+
+
+def prep_kernel(recur_ref, intake_ref, high_ref, low_ref):
+    count, size, _ = recur_ref.shape
+    for which, ref in ((0, recur_ref), (1, intake_ref)):
+        for h in range(count):
+            parts = [ref[h]]
+            if h:
+                parts.insert(0, jnp.zeros((size, h * size), f32))
+            if h < count - 1:
+                parts.append(jnp.zeros((size, (count - 1 - h) * size), f32))
+            row = jnp.concatenate(parts, axis=1)
+            high = row.astype(bf16)
+            rows = slice(h * size, (h + 1) * size)
+            high_ref[which, rows, :] = high
+            low_ref[which, rows, :] = (row - high.astype(f32)).astype(bf16)
+
+
+def forward_kernel(spot_ref, *refs, count, head, plain):
+    pieces, refs = refs[:count], refs[count:]
+    (branch_w, stream_w, output_w, joined_ref, taps_ref, bias_ref, high_ref, low_ref, gate_bias_ref, soft_ref), refs = (
+        refs[:10],
+        refs[10:],
+    )
+    (normed_ref, branch_ref, stream_ref, gated_ref, conv_ref, recur_ref, intake_ref, state_ref), refs = (
+        refs[:8],
+        refs[8:],
+    )
+    *sends, part_high, part_low = refs
+    assemble(pieces, normed_ref)
+    for first, last in tiles(branch_ref.shape[1]):
+        cols = slice(first, last)
+        branch_ref[:, cols] = jnp.dot(normed_ref[...], branch_w[:, cols], preferred_element_type=f32)
+        stream_ref[:, cols] = jnp.dot(normed_ref[...], stream_w[:, cols], preferred_element_type=f32)
     length, width = branch_ref.shape
-    block = length // 4
-    per_block = block // STEP
     steps = length // STEP
-    spot = spot_ref[0]
-
-    def offset(step):
-        turn = lax.bitwise_xor(step // per_block, spot)
-        return pl.multiple_of(turn * block + lax.rem(step, per_block) * STEP, STEP)
+    offset = token_place(length, spot_ref[0], plain)
 
     def convolve(step, before):
         at = offset(step)
@@ -217,38 +425,41 @@
         return last_state
 
     lax.fori_loop(0, steps, advance, jnp.zeros((1, width), f32))
-
-
-def backward_kernel(
-    spot_ref,
-    grad_ref,
-    stream_ref,
-    joined_ref,
-    conv_ref,
-    recur_ref,
-    intake_ref,
-    state_ref,
-    taps_ref,
-    back_ref,
-    soft_ref,
-    stream_grad_ref,
-    gates_ref,
-    sums_ref,
-    pre_ref,
-    conv_low,
-    conv_grad,
-    *,
-    head,
-):
+    step_cols = 512
+    for first in range(0, output_w.shape[1], step_cols):
+        cols = slice(first, first + step_cols)
+        value = jnp.dot(gated_ref[...], output_w[:, cols], preferred_element_type=f32)
+        emit(value, first, output_w.shape[1], sends, plain)
+
+
+def backward_kernel(spot_ref, *refs, count, head, plain):
+    pieces, refs = refs[:count], refs[count:]
+    (
+        output_w,
+        branch_w,
+        stream_w,
+        branch_ref,
+        stream_ref,
+        joined_ref,
+        conv_ref,
+        recur_ref,
+        intake_ref,
+        state_ref,
+        taps_ref,
+        high_ref,
+        soft_ref,
+    ), refs = refs[:13], refs[13:]
+    (cot_ref, branch_grad_ref, stream_grad_ref, gates_ref, sums_ref), refs = refs[:5], refs[5:]
+    *sends, grad_ref, pre_ref, conv_low, conv_grad = refs
+    assemble(pieces, cot_ref)
+    for first, last in tiles(branch_ref.shape[1]):
+        cols = slice(first, last)
+        grad_ref[:, cols] = lax.dot_general(
+            cot_ref[...], output_w[cols, :], contract_cols, preferred_element_type=f32
+        )
     length, width = grad_ref.shape
-    block = length // 4
-    per_block = block // STEP
     steps = length // STEP
-    spot = spot_ref[0]
-
-    def offset(step):
-        turn = lax.bitwise_xor(step // per_block, spot)
-        return pl.multiple_of(turn * block + lax.rem(step, per_block) * STEP, STEP)
+    offset = token_place(length, spot_ref[0], plain)
 
     rows = lax.broadcasted_iota(jnp.int32, (8, width), 0)
     soft = soft_ref[0:1, :]
@@ -271,7 +482,9 @@
         recur = recur_ref[pl.ds(here, STEP), :]
         intake = intake_ref[pl.ds(here, STEP), :]
         carried, square, root, multiplier = decay_terms(recur, soft, link)
-        grad = grad_ref[pl.ds(at, STEP), :]
+        value, slope = gelu_terms(branch_ref[pl.ds(at, STEP), :])
+        gated_grad = grad_ref[pl.ds(at, STEP), :]
+        grad = gated_grad * value
         found = []
         for part in reversed(range(count)):
             own = carried[8 * part : 8 * part + 8]
@@ -288,6 +501,7 @@
             found.append(adjoint)
         adjoint = jnp.concatenate(found[::-1], axis=0)
         state = state_ref[pl.ds(at, STEP), :]
+        branch_grad_ref[pl.ds(at, STEP), :] = (gated_grad * state * slope).astype(bf16)
         tail = state_ref[pl.ds(at_before + (STEP - 8), 8), :]
         earlier = jnp.concatenate([tail, state], axis=0)[7 : 7 + STEP]
         driven_part = adjoint * intake
@@ -320,8 +534,8 @@
         span, cols = slice(low, high), slice(first, last)
         total = conv_grad[0:length, cols]
         for which in range(2):
-            total = total + jnp.dot(
-                pre_ref[which, :, span], back_ref[which, span, cols], preferred_element_type=f32
+            total = total + lax.dot_general(
+                pre_ref[which, :, span], high_ref[which, cols, span], contract_cols, preferred_element_type=f32
             )
             gates_ref[which, span, cols] = lax.dot_general(
                 conv_low[:, span], pre_ref[which, :, cols], contract_rows, preferred_element_type=f32
@@ -346,26 +560,162 @@
     kept = lax.fori_loop(0, steps, unwind, (eight,) * 5)
     for k in range(5):
         sums_ref[k : k + 1, :] = jnp.sum(kept[k], axis=0, keepdims=True)
-
-
-def call(body, outs, scratch, args):
-    vmem = pl.BlockSpec(memory_space=pltpu.VMEM)
+    step_cols = 512
+    for first in range(0, branch_w.shape[0], step_cols):
+        cols = slice(first, first + step_cols)
+        value = lax.dot_general(
+            branch_grad_ref[...], branch_w[cols, :], contract_cols, preferred_element_type=f32
+        ) + lax.dot_general(
+            stream_grad_ref[...], stream_w[cols, :], contract_cols, preferred_element_type=f32
+        )
+        emit(value, first, branch_w.shape[0], sends, plain)
+
+
+def rows_kernel(core_ref, token_ref, cot_ref, gate_ref, up_ref, down_ref, *rest):
+    activ_ref, gate_out, up_out = rest[-3:]
+    tokens, cots = token_ref[...], cot_ref[...]
+    hidden = gate_ref.shape[0]
+    part = hidden // 3
+    for n in range(3):
+        rows = slice(n * part, (n + 1) * part)
+        gate_pre = lax.dot_general(gate_ref[rows], tokens, contract_cols, preferred_element_type=f32)
+        up_pre = lax.dot_general(up_ref[rows], tokens, contract_cols, preferred_element_type=f32)
+        activ_grad = lax.dot_general(down_ref[rows], cots, contract_cols, preferred_element_type=f32)
+        value, slope = gelu_terms(gate_pre)
+        activ_ref[rows] = (value * up_pre).astype(bf16)
+        gate_out[rows] = (activ_grad * up_pre * slope).astype(bf16)
+        up_out[rows] = (activ_grad * value).astype(bf16)
+
+
+def mlp_rows(core, tokens, cots, gate, up, down, after):
+    count, width = tokens.shape
+    hidden = gate.shape[0]
+    tile = 256
+    rows = pl.BlockSpec((tile, width), lambda i, core: (i, 0))
+    tall = pl.BlockSpec((hidden, tile), lambda i, core: (0, i))
+    weight = pl.BlockSpec((hidden, width), lambda i, core: (0, 0))
+    return pl.pallas_call(
+        rows_kernel,
+        grid_spec=pltpu.PrefetchScalarGridSpec(
+            num_scalar_prefetch=1,
+            grid=(count // tile,),
+            in_specs=[rows, rows, weight, weight]
+            + [pl.BlockSpec((hidden, width), lambda i, core: (core[0], 0))]
+            + [pl.BlockSpec(memory_space=pl.ANY)] * len(after),
+            out_specs=[tall, tall, tall],
+        ),
+        out_shape=[jax.ShapeDtypeStruct((hidden, count), bf16)] * 3,
+        cost_estimate=brief,
+        compiler_params=large,
+    )(core, tokens, cots, gate, up, down, *after)
+
+
+def product(left, right, added=(), after=()):
+    rows, depth = left.shape
+    cols = right.shape[1]
+    kind = bf16 if added else f32
+
+    def body(left_ref, right_ref, *rest):
+        total = jnp.dot(left_ref[...], right_ref[...], preferred_element_type=f32)
+        if added:
+            total = total + rest[0][...]
+        rest[-1][...] = total.astype(kind)
+
+    column = pl.BlockSpec((rows, 256), lambda n: (0, n))
     return pl.pallas_call(
         body,
+        grid=(cols // 256,),
+        in_specs=[
+            pl.BlockSpec((rows, depth), lambda n: (0, 0)),
+            pl.BlockSpec((depth, 256), lambda n: (0, n)),
+        ]
+        + [column] * len(added)
+        + [pl.BlockSpec(memory_space=pl.ANY)] * len(after),
+        out_specs=column,
+        out_shape=jax.ShapeDtypeStruct((rows, cols), kind),
+        cost_estimate=brief,
+        compiler_params=pltpu.CompilerParams(vmem_limit_bytes=48 * 1024 * 1024),
+    )(left, right, *added, *after)
+
+
+def flip_kernel(core_ref, one_ref, two_ref, *rest):
+    rest[-2][...] = one_ref[...].astype(f32).T.astype(bf16)
+    rest[-1][...] = two_ref[...].astype(f32).T.astype(bf16)
+
+
+def flipped(one, two, core, after):
+    width, hidden = one.shape[0], one.shape[1] // 2
+    tile = 256
+    source = pl.BlockSpec((tile, hidden), lambda n, core: (n, core[0]))
+    result = pl.BlockSpec((hidden, tile), lambda n, core: (0, n))
+    return pl.pallas_call(
+        flip_kernel,
+        grid_spec=pltpu.PrefetchScalarGridSpec(
+            num_scalar_prefetch=1,
+            grid=(width // tile,),
+            in_specs=[source, source] + [pl.BlockSpec(memory_space=pl.ANY)] * len(after),
+            out_specs=[result, result],
+        ),
+        out_shape=[jax.ShapeDtypeStruct((hidden, width), bf16)] * 2,
+        cost_estimate=brief,
+    )(core.astype(jnp.int32).reshape((1,)), one, two, *after)
+
+
+def turn_kernel(core_ref, own_ref, other_ref, out_ref):
+    mine = pl.program_id(0) == core_ref[0]
+
+    @pl.when(mine)
+    def _():
+        out_ref[...] = own_ref[...].astype(f32).T
+
+    @pl.when(jnp.logical_not(mine))
+    def _():
+        out_ref[...] = other_ref[...].astype(f32).T
+
+
+def turned(own, other, core):
+    hidden, width = own.shape
+    tile = 256
+
+    def chosen(h, n, core):
+        return (0, jnp.where(h == core[0], n, 0))
+
+    def unchosen(h, n, core):
+        return (0, jnp.where(h == core[0], 0, n))
+
+    return pl.pallas_call(
+        turn_kernel,
+        grid_spec=pltpu.PrefetchScalarGridSpec(
+            num_scalar_prefetch=1,
+            grid=(2, width // tile),
+            in_specs=[pl.BlockSpec((hidden, tile), chosen), pl.BlockSpec((hidden, tile), unchosen)],
+            out_specs=pl.BlockSpec((tile, hidden), lambda h, n, core: (n, h)),
+        ),
+        out_shape=jax.ShapeDtypeStruct((width, 2 * hidden), f32),
+        cost_estimate=brief,
+        compiler_params=pltpu.CompilerParams(vmem_limit_bytes=48 * 1024 * 1024),
+    )(core.astype(jnp.int32).reshape((1,)), own, other)
+
+
+def run(body, outs, args, scratch=(), after=(), scalar=False):
+    vmem = pl.BlockSpec(memory_space=pltpu.VMEM)
+    specs = [vmem] * len(args)
+    if scalar:
+        specs[0] = pl.BlockSpec(memory_space=pltpu.SMEM)
+    count = len(args)
+
+    def whole(*refs):
+        body(*refs[:count], *refs[count + len(after) :])
+
+    return pl.pallas_call(
+        whole,
         out_shape=outs,
-        in_specs=[pl.BlockSpec(memory_space=pltpu.SMEM)] + [vmem] * (len(args) - 1),
+        in_specs=specs + [pl.BlockSpec(memory_space=pl.ANY)] * len(after),
         out_specs=[vmem] * len(outs),
         scratch_shapes=scratch,
-        compiler_params=pltpu.CompilerParams(vmem_limit_bytes=48 * 1024 * 1024),
-    )(*args)
-
-
-def spread_heads(weight):
-    count, size = weight.shape[0], weight.shape[1]
-    rows = []
-    for h in range(count):
-        rows.append(jnp.pad(weight[h], ((0, 0), (h * size, (count - 1 - h) * size))))
-    return jnp.concatenate(rows, axis=0)
+        cost_estimate=brief,
+        compiler_params=large,
+    )(*args, *after)
 
 
 def take_heads(wide, count, size):
@@ -395,13 +745,24 @@
     depth,
     square,
 ):
+    line = square and depth == 4
+    plain = not square
     core = lax.axis_index("core")
+    core_id = core.astype(jnp.int32).reshape((1,))
     spot = jnp.zeros((1,), jnp.int32)
     if square:
         spot = spot + (2 * lax.axis_index("y") + lax.axis_index("x")).astype(jnp.int32)
     heads, head = recur_weight.shape[0], recur_weight.shape[1]
     width = heads * head
     length = segment_ids.shape[1]
+    block, features = inputs.shape
+    hidden_units = gate_weight.shape[1]
+    shape = jax.ShapeDtypeStruct
+    halves = [shape((block // 2, features), bf16)] * 2
+
+    gain_one = norm_gain.astype(f32)[None, :]
+    gain_two = mlp_gain.astype(f32)[None, :]
+    normed_own = run(norm_kernel, halves, (inputs, gain_one))
 
     seg_row = segment_ids[0]
     masks = []
@@ -410,31 +771,33 @@
         masks.append((seg_row == earlier).astype(f32))
     joined = jnp.pad(jnp.stack(masks), ((0, 0), (0, 8)))
     joined = jnp.broadcast_to(joined[:, :, None], (3, length + 8, 128))
-    wide = jnp.stack([spread_heads(recur_weight), spread_heads(intake_weight)])
-    wide_high = wide.astype(bf16)
-    wide_low = (wide - wide_high.astype(f32)).astype(bf16)
-    wide_back = jnp.swapaxes(wide_high, 1, 2)
+    square_low = shape((2, width, width), bf16)
+    wide_high, wide_low = pl.pallas_call(
+        prep_kernel, out_shape=[square_low, square_low], cost_estimate=brief
+    )(recur_weight, intake_weight)
     gate_bias = jnp.stack([recur_bias, intake_bias])
     soft = (-decay_scale * jax.nn.softplus(-decay_param))[None, :]
     taps = conv_weight.astype(f32)
 
-    resid = inputs.astype(f32)
-    scale_one = lax.rsqrt(jnp.mean(resid * resid, axis=-1, keepdims=True) + eps)
-    gain_one = norm_gain.astype(f32)[None, :]
-    normed = gather_row((resid * scale_one * gain_one).astype(bf16), square)
-    cot_all = lax.all_gather(cotangent, ALL, axis=0, tiled=True)
-
-    branch_pre = jnp.dot(normed, branch_weight, preferred_element_type=f32)
-    stream_pre = jnp.dot(normed, stream_weight, preferred_element_type=f32)
-    token = jax.ShapeDtypeStruct((length, width), f32)
-    gated, convolved, recur_gate, intake_gate, state = call(
-        functools.partial(forward_kernel, head=head),
-        [jax.ShapeDtypeStruct((length, width), bf16), token, token, token, token],
-        [pltpu.VMEM((length, width), bf16), pltpu.VMEM((length, width), bf16)],
+    cuts = (0, block * 3 // 4, block)
+    spans = list(zip(cuts[:-1], cuts[1:], strict=True))
+    if line:
+        cots = [lax.all_gather(cotangent[a:b], ALL, axis=0, tiled=True) for a, b in spans]
+
+    normed_pieces = gather_row(normed_own, square, (wide_high,) if square else ())
+    token = shape((length, width), f32)
+    token_low = shape((length, width), bf16)
+    row_low = shape((length, features), bf16)
+    row_sends = send_shapes(length, features, plain)
+    normed, branch_pre, stream_pre, gated, convolved, recur_gate, intake_gate, state, *sends = run(
+        functools.partial(forward_kernel, count=len(normed_pieces), head=head, plain=plain),
+        [row_low, token, token, token_low, token, token, token, token, *row_sends],
         (
             spot,
-            branch_pre,
-            stream_pre,
+            *normed_pieces,
+            branch_weight,
+            stream_weight,
+            output_weight,
             joined,
             taps,
             conv_bias.astype(f32)[None, :],
@@ -443,66 +806,67 @@
             gate_bias,
             soft,
         ),
+        [pltpu.VMEM((length, width), bf16)] * 2,
+        scalar=True,
     )
-    mixer = scatter_row(jnp.dot(gated, output_weight, preferred_element_type=f32).astype(bf16), square)
-
-    hidden = resid + mixer
-    scale_two = lax.rsqrt(jnp.mean(hidden * hidden, axis=-1, keepdims=True) + eps)
-    gain_two = mlp_gain.astype(f32)[None, :]
-    hat_two = hidden * scale_two
-    normed_two = (hat_two * gain_two).astype(bf16)
-    mlp_in = gather_row(normed_two, square)
-    mlp_all = lax.all_gather(normed_two, ALL, axis=0, tiled=True)
-    cot_row = gather_row(cotangent, square)
-
-    def mlp_grads(tokens, cots, gate, up, down):
-        gate_pre = jnp.dot(tokens, gate, preferred_element_type=f32)
-        up_pre = jnp.dot(tokens, up, preferred_element_type=f32)
-        activ_grad = lax.dot_general(cots, down, contract_cols, preferred_element_type=f32)
-        value, slope = gelu_terms(gate_pre)
-        return (
-            (value * up_pre).astype(bf16),
-            (activ_grad * up_pre * slope).astype(bf16),
-            (activ_grad * value).astype(bf16),
-        )
-
-    activ, gate_low, up_low = mlp_grads(mlp_in, cot_row, gate_weight, up_weight, down_weight)
-    two_grad = scatter_row(
-        (
-            lax.dot_general(gate_low, gate_weight, contract_cols, preferred_element_type=f32)
-            + lax.dot_general(up_low, up_weight, contract_cols, preferred_element_type=f32)
-        ).astype(bf16),
-        square,
+    cot_own = (cotangent[: block // 2], cotangent[block // 2 :])
+    if square:
+        cot_own = held(cot_own, (normed_pieces[-1],))
+    cot_row = jnp.concatenate(gather_row(cot_own, square), axis=0)
+    activ_grad = lax.dot_general(cot_row, down_weight, contract_cols, preferred_element_type=f32)
+    addends = scatter_row(sends, square)
+
+    parts = [shape((b - a, features), bf16) for a, b in spans]
+    hidden, one, two, *token_parts = run(
+        functools.partial(second_norm_kernel, cuts=cuts),
+        [shape((block, features), f32), *halves, *parts],
+        (inputs, gain_two, *addends),
     )
-    mlp_out = scatter_row(jnp.dot(activ, down_weight, preferred_element_type=f32).astype(bf16), square)
-    block_out = (hidden + mlp_out).astype(bf16)
-
-    mlp_gain_part = jnp.sum(two_grad * hat_two, axis=0)
-    scaled = two_grad * gain_two
-    resid_grad = cotangent.astype(f32) + scale_two * (
-        scaled - hat_two * jnp.mean(scaled * hat_two, axis=-1, keepdims=True)
+    if line:
+        tokens = [lax.all_gather(part, ALL, axis=0, tiled=True) for part in token_parts]
+        gate_turned, up_turned = flipped(gate_weight, up_weight, core, (gated,))
+    mlp_pieces = gather_row((one, two), square, (gate_turned,) if line else ())
+    tile = min(512, hidden_units)
+    fixed = [pl.BlockSpec(piece.shape, lambda i: (0, 0)) for piece in mlp_pieces]
+    column = pl.BlockSpec((length, tile), lambda i: (0, i))
+    weight_column = pl.BlockSpec((features, tile), lambda i: (0, i))
+    low_units = shape((length, hidden_units), bf16)
+    kept = [] if line else [low_units, low_units]
+    mlp_in, activ, *sends = pl.pallas_call(
+        functools.partial(mlp_kernel, count=len(mlp_pieces), plain=plain, keep=not line),
+        grid=(hidden_units // tile,),
+        in_specs=[*fixed, column, weight_column, weight_column],
+        out_specs=[pl.BlockSpec(row_low.shape, lambda i: (0, 0)), column]
+        + [column] * len(kept)
+        + [pl.BlockSpec(send.shape, lambda i: (0, 0)) for send in row_sends],
+        out_shape=[row_low, low_units, *kept, *row_sends],
+        scratch_shapes=[pltpu.VMEM((length, features), bf16), pltpu.VMEM((length, features), f32)],
+        cost_estimate=brief,
+        compiler_params=pltpu.CompilerParams(vmem_limit_bytes=56 * 1024 * 1024),
+    )(*mlp_pieces, activ_grad, gate_weight, up_weight)
+    kept, sends = sends[: len(kept)], sends[len(kept) :]
+    out_sends = run(functools.partial(down_kernel, plain=plain), row_sends, (activ, down_weight))
+    addends = scatter_row(sends, square, (out_sends[0],) if square else ())
+
+    mlp_gain_part, resid_grad, one, two = run(
+        functools.partial(norm_back_kernel, final=False),
+        [shape((1, features), f32), shape((block, features), f32), *halves],
+        (hidden, cotangent, gain_two, *addends),
     )
-    branch_cot = gather_row(resid_grad.astype(bf16), square)
-
-    gated_grad = lax.dot_general(branch_cot, output_weight, contract_cols, preferred_element_type=f32)
-    value, slope = gelu_terms(branch_pre)
-    state_grad = gated_grad * value
-    branch_low = (gated_grad * state * slope).astype(bf16)
-    stream_low, wide_grad, sums = call(
-        functools.partial(backward_kernel, head=head),
-        [
-            jax.ShapeDtypeStruct((length, width), bf16),
-            jax.ShapeDtypeStruct((2, width, width), f32),
-            jax.ShapeDtypeStruct((8, width), f32),
-        ],
-        [
-            pltpu.VMEM((2, length, width), bf16),
-            pltpu.VMEM((length, width), bf16),
-            pltpu.VMEM((length + 8, width), f32),
-        ],
+    if line:
+        kept_a = mlp_rows(core_id, tokens[0], cots[0], gate_turned, up_turned, down_weight, (one,))
+    cot_pieces = gather_row((one, two), square)
+
+    branch_cot, branch_low, stream_low, wide_grad, sums, *sends = run(
+        functools.partial(backward_kernel, count=len(cot_pieces), head=head, plain=plain),
+        [row_low, token_low, token_low, shape((2, width, width), f32), shape((8, width), f32), *row_sends],
         (
             spot,
-            state_grad,
+            *cot_pieces,
+            output_weight,
+            branch_weight,
+            stream_weight,
+            branch_pre,
             stream_pre,
             joined,
             convolved,
@@ -510,24 +874,27 @@
             intake_gate,
             state,
             taps,
-            wide_back,
+            wide_high,
             soft,
         ),
+        [
+            pltpu.VMEM((length, width), f32),
+            pltpu.VMEM((2, length, width), bf16),
+            pltpu.VMEM((length, width), bf16),
+            pltpu.VMEM((length + 8, width), f32),
+        ],
+        scalar=True,
     )
-    one_grad = scatter_row(
-        (
-            lax.dot_general(branch_low, branch_weight, contract_cols, preferred_element_type=f32)
-            + lax.dot_general(stream_low, stream_weight, contract_cols, preferred_element_type=f32)
-        ).astype(bf16),
-        square,
+    addends = scatter_row(sends, square)
+    norm_gain_part, inputs_grad = run(
+        functools.partial(norm_back_kernel, final=True),
+        [shape((1, features), f32), shape((block, features), bf16)],
+        (inputs, resid_grad, gain_one, *addends),
     )
-    hat_one = resid * scale_one
-    norm_gain_part = jnp.sum(one_grad * hat_one, axis=0)
-    scaled = one_grad * gain_one
-    inputs_grad = (
-        resid_grad
-        + scale_one * (scaled - hat_one * jnp.mean(scaled * hat_one, axis=-1, keepdims=True))
-    ).astype(bf16)
+    if square:
+        out_sends = held(out_sends, (inputs_grad,))
+    addends = scatter_row(out_sends, square)
+    (block_out,) = run(add_kernel, [shape((block, features), bf16)], (hidden, *addends))
 
     def both(value):
         return jnp.concatenate([value, sibling(value)], axis=0)
@@ -553,25 +920,44 @@
         jnp.where(core == 0, recur_part, intake_part).astype(f32)
         + sibling(jnp.where(core == 0, intake_part, recur_part)).astype(f32)
     ).astype(bf16)
-    gains = jnp.concatenate([norm_gain_part, mlp_gain_part])
+    gains = jnp.concatenate([norm_gain_part, mlp_gain_part], axis=1)
     if square:
         gains = gains + lax.ppermute(gains, "x", swap)
         gains = gains + lax.ppermute(gains, "y", swap)
     else:
         gains = lax.psum(gains, ("y", "x"))
-    small = jnp.concatenate([sums.reshape(-1), gains]).reshape(-1, 128)
+    small = jnp.concatenate([sums.reshape(-1), gains.reshape(-1)]).reshape(-1, 128)
     small = small + sibling(small)
-    output_sum, branch_sum, stream_sum, gate_sum, small_sum = line_sums(
-        [output_half, branch_half, stream_half, gate_half, small], depth
-    )
-
-    gate_part = half_of(gate_weight, core, 1)
-    up_part = half_of(up_weight, core, 1)
-    down_part = half_of(down_weight, core, 0)
-    activ_all, gate_all, up_all = mlp_grads(mlp_all, cot_all, gate_part, up_part, down_part)
-    down_half = lax.dot_general(activ_all, cot_all, contract_rows, preferred_element_type=f32).astype(bf16)
-    gate_w_half = lax.dot_general(mlp_all, gate_all, contract_rows, preferred_element_type=f32).astype(bf16)
-    up_w_half = lax.dot_general(mlp_all, up_all, contract_rows, preferred_element_type=f32).astype(bf16)
+
+    if line:
+        first = [product(part, right, (), (stream_half,)) for part, right in zip(kept_a, (cots[0], tokens[0], tokens[0]), strict=True)]
+        kept_b = mlp_rows(
+            core_id, tokens[1], cots[1], gate_turned, up_turned, down_weight, (stream_half, *first)
+        )
+        down_half, gate_half_w, up_half_w = (
+            product(part, right, (before,))
+            for part, right, before in zip(kept_b, (cots[1], tokens[1], tokens[1]), first, strict=True)
+        )
+        groups = line_sums(
+            [(output_half,), (branch_half,), (stream_half,), (gate_half, small)],
+            ((first[0],), (first[2],), (kept_b[0],), (down_half,), (up_half_w,), ()),
+        )
+        (output_sum,), (branch_sum,), (stream_sum,), (gate_sum, small_sum) = groups
+        down_w_grad = join(down_half, sibling(down_half), core, 0)
+        gate_w_grad = turned(gate_half_w, sibling(gate_half_w), core)
+        up_w_grad = turned(up_half_w, sibling(up_half_w), core)
+    else:
+        output_sum, branch_sum, stream_sum, gate_sum, small_sum = (
+            lax.psum(part, "z") for part in (output_half, branch_half, stream_half, gate_half, small)
+        )
+
+        def over_rows(left, right):
+            part = lax.dot_general(left, right, contract_rows, preferred_element_type=f32)
+            return lax.psum(part.astype(bf16), ("z", "core")).astype(f32)
+
+        gate_w_grad = over_rows(mlp_in, kept[0])
+        up_w_grad = over_rows(mlp_in, kept[1])
+        down_w_grad = over_rows(activ, cot_row)
 
     def whole(own, axis):
         return join(own, sibling(own), core, axis)
@@ -595,9 +981,9 @@
         sums[7] * decay_scale * jax.nn.sigmoid(-decay_param),
         whole(output_sum, 1),
         gains[1],
-        whole(gate_w_half, 1),
-        whole(up_w_half, 1),
-        whole(down_half, 0),
+        gate_w_grad,
+        up_w_grad,
+        down_w_grad,
     )
 
 

time: 785 us -> 658 us (0.84)
  Pallas kernels: 24.9 us -> 254 us
  matrix products: 211 us -> 19.4 us
  waiting for transfers between devices: 312 us -> 143 us
  starting transfers between devices: 62.4 us -> 94.3 us
  other arithmetic: 72.8 us -> 56 us
  local copies, waits for them, and re-layouts: 78.7 us -> 65.5 us
    pallas_call x2 -> x35, Pallas kernels: 24.9 us -> 254 us  [the longest x6 73.2 us: product(): pl.pallas_call(body, grid=(cols // 256,), in_specs=[pl.BlockSpec((rows, d...]
    dot_general x18 -> x1, matrix products: 202 us -> 8.53 us  [local(): lax.dot_general(cot_row, down_weight, contract_cols, preferred_element_ty...]
    ppermute x39 -> x47, waiting for transfers between devices: 256 us -> 113 us  [the longest x4 35.4 us: scatter_row(): got_x = lax.ppermute(to_x, 'x', swap)]
    ppermute x39 -> x47, starting transfers between devices: 47.5 us -> 81.8 us  [the longest x15 49.7 us: line_sums(): lax.ppermute(piece, 'z', pairs[stage])]
    ppermute x4, waiting for transfers between devices: 37.4 us -> 22.8 us  [scatter_row(): last_y = lax.ppermute(send_y, 'y', swap)]
    ppermute x4, waiting for transfers between devices: 16 us -> 1.72 us  [scatter_row(): last_x = lax.ppermute(send_x, 'x', swap)]
    convert_element_type x6 -> x4, other arithmetic: 27.6 us -> 14.8 us  [join(): return jnp.concatenate([first, second], axis=axis).astype(f32)]
    convert_element_type x16 -> x8, other arithmetic: 8.49 us -> 17.3 us  [line_sums(): groups[n][k] = (piece.astype(f32) + other.astype(f32)).astype(piece.dtype)]
  transfers between devices with their start and end apart: 65 -> 75, of which waited for: 32 -> 27; matrix products, arithmetic and copies ran while one was open for 39% -> 14% of each run, Pallas kernels for 3% -> 39%
where the time goes in v2:
time: 658 us; the launch traced here: 648 us
  Pallas kernels  254 us (39%)
  waiting for transfers between devices  143 us (22%)
  starting transfers between devices  94.3 us (14%)
  local copies, waits for them, and re-layouts  65.5 us (10%)
  other arithmetic  56 us (9%)
  matrix products  19.4 us (3%)
  between operations  15.2 us (2%)
    pallas_call x6, Pallas kernels, product(): pl.pallas_call(body, grid=(cols // 256,), in_specs=[pl.BlockSpec((rows, d...  73.2 us
    pallas_call x8, Pallas kernels, run(): pl.pallas_call(whole, out_shape=outs, in_specs=specs + [pl.BlockSpec(memo...  55.4 us
    pallas_call x2, Pallas kernels, mlp_rows(): pl.pallas_call(rows_kernel, grid_spec=pltpu.PrefetchScalarGridSpec(num_sc...  54.6 us
    unnamed x240, local copies, waits for them, and re-layouts  51 us
    ppermute x15, starting transfers between devices, line_sums(): lax.ppermute(piece, 'z', pairs[stage])  49.7 us
    ppermute x4, waiting for transfers between devices, scatter_row(): got_x = lax.ppermute(to_x, 'x', swap)  35.4 us
    ppermute x15, waiting for transfers between devices, line_sums(): lax.ppermute(piece, 'z', pairs[stage])  28.3 us
    pallas_call x2, Pallas kernels, turned(): pl.pallas_call(turn_kernel, grid_spec=pltpu.PrefetchScalarGridSpec(num_sc...  26.6 us
  transfers between devices with their start and end apart: 75, of which 27 were waited for; matrix products, arithmetic and copies ran while one was open for 14% of the time, Pallas kernels for 39%

profile of v2, /device:TPU:0, one launch (start us, length us, event | category | flops | bytes accessed | tf_op | source)
XLA Modules:
  0.0 647.8 jit_solution(14391031536720704371)
XLA Ops:
  11.1 3.0 collective-permute-start
  17.9 3.4 shard_map.306
  21.4 8.9 %collective-permute-done.1.refs_1_ = bf16[64,2048]{1,0:T(8,128)(2,1)S(1)} collective-permute-done((bf16[64,2048]{1,0:T(8,128)(2,1)S(1)}, bf16[64,2048]{1,0:T(8,128)(2,1)S(1)}, u32[]{:S(2)}, u32[]{:S(2)}) %collective-permute-start.1) | collective-permute-done | bytes 262176 | tf_op jit(solution)/shard_map/ppermute | solution.py:47
  34.0 3.6 collective-permute-done.3.refs_4_
  44.2 19.6 %shard_map.308 = (bf16[512,2048]{1,0:T(8,128)(2,1)}, f32[512,640]{1,0:T(8,128)}, f32[512,640]{1,0:T(8,128)}, bf16[512,640]{1,0:T(8,128)(2,1)S(1)}, f32[512,640]{...) custom-call(s32[1]{0:T(128)} %bitcast.1.refs_0_, ...), custom_call_target="tpu_custom_call" | custom-call | flops 1 | bytes 1 | tf_op jit(solution)/shard_map/pallas_call | solution.py:710
  67.9 22.3 %collective-permute-done.6.got_x.refs_3_ = bf16[256,1024]{1,0:T(8,128)(2,1)S(1)} collective-permute-done((bf16[256,1024]{1,0:T(8,128)(2,1)S(1)}, bf16[256,1024]{1,0:T(8,128)(2,1)S(1)}, u32[]{:S(2)}, u32[]{:S(2)}) %collective-permute-start.6) | collective-permute-done | bytes 524320 | tf_op jit(solution)/shard_map/ppermute | solution.py:61
  91.5 2.2 shard_map.309
  95.9 10.1 %collective-permute-done.8.refs_5_ = bf16[128,1024]{1,0:T(8,128)(2,1)S(1)} collective-permute-done((bf16[128,1024]{1,0:T(8,128)(2,1)}, bf16[128,1024]{1,0:T(8,128)(2,1)S(1)}, u32[]{:S(2)}, u32[]{:S(2)}) %collective-permute-start.8) | collective-permute-done | bytes 262176 | tf_op jit(solution)/shard_map/ppermute | solution.py:70
  116.6 2.0 collective-permute-start.20
  120.6 8.3 %shard_map.311 = (bf16[768,2048]{1,0:T(8,128)(2,1)}, bf16[768,2048]{1,0:T(8,128)(2,1)}) custom-call(s32[1]{0:T(128)} %bitcast.6.core_ref, bf16[2048,1536]{1,0:T(8,128)(2,1)} %refs_9_.4, bf16[2048,1536]{1,0:T(8,128)(2,1)} %refs_10_.4, bf16[512,640]{1,0:T(8,128)(2,1)} %copy-done.45), custom_call_target="tpu_custom_call" | custom-call | flops 1 | bytes 1 | tf_op jit(solution)/shard_map/pallas_call | solution.py:651
  132.2 7.1 %collective-permute-done.18 = bf16[64,2048]{1,0:T(8,128)(2,1)S(1)} collective-permute-done((bf16[64,2048]{1,0:T(8,128)(2,1)S(1)}, bf16[64,2048]{1,0:T(8,128)(2,1)S(1)}, u32[]{:S(2)}, u32[]{:S(2)}) %collective-permute-start.18) | collective-permute-done | bytes 262176 | tf_op jit(solution)/shard_map/ppermute | solution.py:52
  152.2 8.5 %fusion.26.refs_8_ = f32[512,1536]{1,0:T(8,128)} fusion(bf16[512,2048]{1,0:T(8,128)(2,1)} %constant_dynamic-update-slice_fusion, bf16[1536,2048]{1,0:T(8,128)(2,1)} %down_ref.3), kind=kOutput, calls=%fused_computation.96 | convolution fusion | flops 3221225472 | bytes 11534336 | tf_op jit(solution)/shard_map/dot_general | solution.py:816
  162.4 23.8 %shard_map.314 = (bf16[512,2048]{1,0:T(8,128)(2,1)}, bf16[512,1536]{1,0:T(8,128)(2,1)}, bf16[256,1024]{1,0:T(8,128)(2,1)}, bf16[256,1024]{1,0:T(8,128)(2,1)}, bf...) custom-call(bf16[64,2048]{1,0:T(8,128)(2,1)} %copy-done.48, ...), custom_call_target="tpu_custom_call" | custom-call | flops 1 | bytes 1 | tf_op jit(solution)/shard_map/pallas_call | solution.py:835
  190.9 6.2 shard_map.315
  201.1 8.4 %collective-permute-done.22.refs_0_ = bf16[256,1024]{1,0:T(8,128)(2,1)S(1)} collective-permute-done((bf16[256,1024]{1,0:T(8,128)(2,1)}, bf16[256,1024]{1,0:T(8,128)(2,1)S(1)}, u32[]{:S(2)}, u32[]{:S(2)}) %collective-permute-start.22) | collective-permute-done | bytes 524320 | tf_op jit(solution)/shard_map/ppermute | solution.py:61
  211.3 2.3 shard_map.317
  216.3 9.2 %collective-permute-done.24.refs_6_ = bf16[128,1024]{1,0:T(8,128)(2,1)S(1)} collective-permute-done((bf16[128,1024]{1,0:T(8,128)(2,1)}, bf16[128,1024]{1,0:T(8,128)(2,1)S(1)}, u32[]{:S(2)}, u32[]{:S(2)}) %collective-permute-start.24) | collective-permute-done | bytes 262176 | tf_op jit(solution)/shard_map/ppermute | solution.py:70
  235.7 2.3 collective-permute-done.26.refs_2_
  241.7 2.8 collective-permute-done.28.refs_4_
  245.7 23.4 %shard_map.319 = (bf16[512,2048]{1,0:T(8,128)(2,1)}, bf16[512,640]{1,0:T(8,128)(2,1)}, bf16[512,640]{1,0:T(8,128)(2,1)}, f32[2,640,640]{2,1,0:T(8,128)}, f32[8,6...) custom-call(s32[1]{0:T(128)} %bitcast.1.refs_0_, ...), custom_call_target="tpu_custom_call" | custom-call | flops 1 | bytes 1 | tf_op jit(solution)/shard_map/pallas_call | solution.py:710
  274.7 2.6 fusion.4
  277.4 4.7 collective-permute-start.53
  283.3 4.7 collective-permute-done.32.got_x.refs_4_
  287.9 15.9 %collective-permute-done.33.got_y.refs_5_ = bf16[256,1024]{1,0:T(8,128)(2,1)S(1)} collective-permute-done((bf16[256,1024]{1,0:T(8,128)(2,1)S(1)}, bf16[256,1024]{1,0:T(8,128)(2,1)S(1)}, u32[]{:S(2)}, u32[]{:S(2)}) %collective-permute-start.33) | collective-permute-done | bytes 524320 | tf_op jit(solution)/shard_map/ppermute | solution.py:62
  304.7 2.2 shard_map.320
  308.9 4.5 convolution_convert_fusion
  313.4 2.3 collective-permute-start.50
  315.7 3.8 convolution_convert_fusion.1.rest_0_
  321.4 38.5 %shard_map.325 = (bf16[768,3072]{1,0:T(8,128)(2,1)}, bf16[768,3072]{1,0:T(8,128)(2,1)}, bf16[768,3072]{1,0:T(8,128)(2,1)}) custom-call(s32[1]{0:T(128)} %bitcast.6.core_ref, bf16[3072,2048]{1,0:T(8,128)(2,1)} %all-gather.5.cloned.1.call-done.token_ref.right_ref, bf16[3072,2048]{1,0:T(8,128)(2,1)} %all-gather.7.cloned.1.call-done.cot_ref.right_ref, ...), custom_call_target="tpu_custom_call" | custom-call | flops 1 | bytes 1 | tf_op jit(solution)/shard_map/pallas_call | solution.py:597
  359.9 2.9 copy-done.7
  362.8 14.5 %shard_map.326.refs_1_.rest_1_.rest_0_ = f32[768,2048]{1,0:T(8,128)} custom-call(bf16[768,3072]{1,0:T(8,128)(2,1)S(1)} %copy-done.7, bf16[3072,2048]{1,0:T(8,128)(2,1)} %all-gather.7.cloned.1.call-done.cot_ref.right_ref, bf16[1024,640]{1,0:T(8,128)(2,1)S(1)} %convolution_convert_fusion.1.rest_0_), custom_call_target="tpu_custom_call" | custom-call | flops 1 | bytes 1 | tf_op jit(solution)/shard_map/pallas_call | solution.py:625
  377.3 3.6 add_convert_fusion.5
  384.9 3.3 collective-permute-done.40
  388.7 2.7 collective-permute-start.48
  393.6 3.0 fusion.16
  396.6 2.2 slice_bitcast_fusion.3
  398.8 2.3 copy-done.6
  401.1 14.6 %shard_map.328.refs_2_.rest_3_.rest_0_ = f32[768,2048]{1,0:T(8,128)} custom-call(bf16[768,3072]{1,0:T(8,128)(2,1)S(1)} %copy-done.6, bf16[3072,2048]{1,0:T(8,128)(2,1)} %all-gather.5.cloned.1.call-done.token_ref.right_ref, bf16[1024,640]{1,0:T(8,128)(2,1)S(1)} %convolution_convert_fusion.1.rest_0_), custom_call_target="tpu_custom_call" | custom-call | flops 1 | bytes 1 | tf_op jit(solution)/shard_map/pallas_call | solution.py:625
  415.7 14.5 %shard_map.330.rest_2_.rest_0_ = f32[768,2048]{1,0:T(8,128)} custom-call(bf16[768,3072]{1,0:T(8,128)(2,1)S(1)} %bitcast.54, bf16[3072,2048]{1,0:T(8,128)(2,1)} %all-gather.5.cloned.1.call-done.token_ref.right_ref, bf16[1024,640]{1,0:T(8,128)(2,1)S(1)} %convolution_convert_fusion.1.rest_0_), custom_call_target="tpu_custom_call" | custom-call | flops 1 | bytes 1 | tf_op jit(solution)/shard_map/pallas_call | solution.py:625
  430.2 16.1 %shard_map.331 = (bf16[768,1024]{1,0:T(8,128)(2,1)S(1)}, bf16[768,1024]{1,0:T(8,128)(2,1)S(1)}, bf16[768,1024]{1,0:T(8,128)(2,1)S(1)}) custom-call(s32[1]{0:T(128)} %bitcast.6.core_ref, bf16[1024,2048]{1,0:T(8,128)(2,1)} %all-gather.9.cloned.1.call-done.token_ref.right_ref, bf16[1024,2048]{1,0:T(8,128)(2,1)} %all-gather.11.cloned.1.call-done.cot_ref.right_ref, ...), custom_call_target="tpu_custom_call" | custom-call | flops 1 | bytes 1 | tf_op jit(solution)/shard_map/pallas_call | solution.py:597
  448.7 10.3 %shard_map.333.refs_4_ = bf16[768,2048]{1,0:T(8,128)(2,1)} custom-call(bf16[768,1024]{1,0:T(8,128)(2,1)S(1)} %get-tuple-element.184.refs_3_.left_ref, bf16[1024,2048]{1,0:T(8,128)(2,1)} %all-gather.11.cloned.1.call-done.cot_ref.right_ref, f32[768,2048]{1,0:T(8,128)} %shard_map.326.refs_1_.rest_1_.rest_0_), custom_call_target="tpu_custom_call" | custom-call | flops 1 | bytes 1 | tf_op jit(solution)/shard_map/pallas_call | solution.py:625
  461.2 2.2 shard_map.323
  463.4 9.7 %shard_map.335.refs_3_.own_ref = bf16[768,2048]{1,0:T(8,128)(2,1)} custom-call(bf16[768,1024]{1,0:T(8,128)(2,1)S(1)} %copy-done.30, bf16[1024,2048]{1,0:T(8,128)(2,1)} %all-gather.9.cloned.1.call-done.token_ref.right_ref, f32[768,2048]{1,0:T(8,128)} %shard_map.328.refs_2_.rest_3_.rest_0_), custom_call_target="tpu_custom_call" | custom-call | flops 1 | bytes 1 | tf_op jit(solution)/shard_map/pallas_call | solution.py:625
  473.1 9.6 %shard_map.337.own_ref = bf16[768,2048]{1,0:T(8,128)(2,1)} custom-call(bf16[768,1024]{1,0:T(8,128)(2,1)S(1)} %copy-done.28, bf16[1024,2048]{1,0:T(8,128)(2,1)} %all-gather.9.cloned.1.call-done.token_ref.right_ref, f32[768,2048]{1,0:T(8,128)} %shard_map.330.rest_2_.rest_0_), custom_call_target="tpu_custom_call" | custom-call | flops 1 | bytes 1 | tf_op jit(solution)/shard_map/pallas_call | solution.py:625
  484.1 3.1 add_convert_fusion.4
  488.1 3.5 collective-permute-done.38.refs_4_
  492.3 3.4 add_convert_fusion.3
  499.5 2.2 add_convert_fusion.8
  506.0 2.0 shard_map.324
  508.0 21.0 %collective-permute-start.44 = (bf16[4,160,160]{2,1,0:T(8,128)(2,1)}, bf16[4,160,160]{2,1,0:T(8,128)(2,1)S(1)}, u32[]{:S(2)}, u32[]{:S(2)}) collective-permute-start(bf16[4,160,160]{2,1,0:T(8,128)(2,1)} %add_convert_fusion.8), channel_id=1, source_target_pairs={{0,8},{24,16},{1,9},{25,17},{2,10},{26,18},{3,11},{27,19},{4,12},{... | collective-permute-start | bytes 614408 | tf_op jit(solution)/shard_map/ppermute | solution.py:97
  529.0 2.6 collective-permute-done.56.refs_2_
  535.0 2.0 add_convert_fusion.1
  539.8 3.3 broadcast_select_fusion.1
  543.1 5.8 collective-permute-start.45
  549.0 6.4 maximum_convert_fusion
  555.4 13.3 %shard_map.338 = f32[2048,1536]{1,0:T(8,128)} custom-call(s32[1]{0:T(128)} %bitcast.6.core_ref, bf16[768,2048]{1,0:T(8,128)(2,1)} %shard_map.337.own_ref, bf16[768,2048]{1,0:T(8,128)(2,1)} %collective-permute-done.68.other_ref), custom_call_target="tpu_custom_call" | custom-call | flops 1 | bytes 1 | tf_op jit(solution)/shard_map/pallas_call | solution.py:686
  568.7 13.3 %shard_map.339 = f32[2048,1536]{1,0:T(8,128)} custom-call(s32[1]{0:T(128)} %bitcast.6.core_ref, bf16[768,2048]{1,0:T(8,128)(2,1)} %shard_map.335.refs_3_.own_ref, bf16[768,2048]{1,0:T(8,128)(2,1)} %collective-permute-done.69.other_ref), custom_call_target="tpu_custom_call" | custom-call | flops 1 | bytes 1 | tf_op jit(solution)/shard_map/pallas_call | solution.py:686
  582.8 2.1 add_convert_fusion
  588.3 2.5 broadcast_select_fusion.6
  593.6 3.0 maximum_convert_fusion.3
  596.6 21.5 %collective-permute-done.61.refs_2_ = bf16[1024,640]{1,0:T(8,128)(2,1)} collective-permute-done((bf16[1024,640]{1,0:T(8,128)(2,1)S(1)}, bf16[1024,640]{1,0:T(8,128)(2,1)}, u32[]{:S(2)}, u32[]{:S(2)}) %collective-permute-start.61) | collective-permute-done | bytes 1310752 | tf_op jit(solution)/shard_map/ppermute | solution.py:97
  625.2 2.7 maximum_convert_fusion.1
  629.7 4.2 collective-permute-done.65
  638.4 2.7 maximum_convert_fusion.2
  (431 shorter events, 143.6 us)
Async XLA Ops:
  7.2 312.3 %all-gather.7.cloned.1.call-start = ((), (), s32[]{:S(2)}) async-start(), calls=%async_computation.1 | async-start | bytes 12976128 | tf_op jit(solution)/shard_map/all_gather | solution.py:785
  9.1 310.4 %all-gather.5.cloned.1.call-start = ((), (), s32[]{:S(2)}) async-start(), calls=%async_computation | async-start | bytes 12976128 | tf_op jit(solution)/shard_map/all_gather | solution.py:826
  11.1 10.2 %collective-permute-start = (bf16[64,2048]{1,0:T(8,128)(2,1)S(1)}, bf16[64,2048]{1,0:T(8,128)(2,1)S(1)}, u32[]{:S(2)}, u32[]{:S(2)}) collective-permute-start(bf16[64,2048]{1,0:T(8,128)(2,1)S(1)} %get-tuple-element.107.refs_1_), channel_id=1, source_target_pairs={{0,1},{1,0},{2,3},{3,2},{4,5},{5,4},{6,7},{7,6},{8,9},{9,8},{10,11... | collective-permute-start | bytes 786440 | tf_op jit(solution)/shard_map/ppermute | solution.py:46
  14.1 19.1 %collective-permute-start.2 = (bf16[64,2048]{1,0:T(8,128)(2,1)S(1)}, bf16[64,2048]{1,0:T(8,128)(2,1)S(1)}, u32[]{:S(2)}, u32[]{:S(2)}) collective-permute-start(bf16[64,2048]{1,0:T(8,128)(2,1)S(1)} %get-tuple-element.107.refs_1_), channel_id=1, source_target_pairs={{0,2},{2,0},{1,3},{3,1},{4,6},{6,4},{5,7},{7,5},{8,10},{10,8},{9,1... | collective-permute-start | bytes 786440 | tf_op jit(solution)/shard_map/ppermute | solution.py:49
  15.6 14.7 %collective-permute-start.1 = (bf16[64,2048]{1,0:T(8,128)(2,1)S(1)}, bf16[64,2048]{1,0:T(8,128)(2,1)S(1)}, u32[]{:S(2)}, u32[]{:S(2)}) collective-permute-start(bf16[64,2048]{1,0:T(8,128)(2,1)S(1)} %get-tuple-element.108.refs_5_), channel_id=1, source_target_pairs={{0,2},{2,0},{1,3},{3,1},{4,6},{6,4},{5,7},{7,5},{8,10},{10,8},{9,1... | collective-permute-start | bytes 786440 | tf_op jit(solution)/shard_map/ppermute | solution.py:47
  16.1 17.1 %collective-permute-start.4 = (bf16[64,2048]{1,0:T(8,128)(2,1)S(1)}, bf16[64,2048]{1,0:T(8,128)(2,1)S(1)}, u32[]{:S(2)}, u32[]{:S(2)}) collective-permute-start(bf16[64,2048]{1,0:T(8,128)(2,1)S(1)} %get-tuple-element.108.refs_5_), channel_id=1, source_target_pairs={{0,1},{1,0},{2,3},{3,2},{4,5},{5,4},{6,7},{7,6},{8,9},{9,8},{10,11... | collective-permute-start | bytes 786440 | tf_op jit(solution)/shard_map/ppermute | solution.py:48
  31.0 6.6 %collective-permute-start.3 = (bf16[64,2048]{1,0:T(8,128)(2,1)}, bf16[64,2048]{1,0:T(8,128)(2,1)S(1)}, u32[]{:S(2)}, u32[]{:S(2)}) collective-permute-start(bf16[64,2048]{1,0:T(8,128)(2,1)} %get-tuple-element.110.refs_2_), channel_id=1, source_target_pairs={{0,2},{2,0},{1,3},{3,1},{4,6},{6,4},{5,7},{7,5},{8,10},{10,8},{9,1... | collective-permute-start | bytes 786440 | tf_op jit(solution)/shard_map/ppermute | solution.py:52
  32.5 6.6 %collective-permute-start.5 = (bf16[64,2048]{1,0:T(8,128)(2,1)}, bf16[64,2048]{1,0:T(8,128)(2,1)S(1)}, u32[]{:S(2)}, u32[]{:S(2)}) collective-permute-start(bf16[64,2048]{1,0:T(8,128)(2,1)} %get-tuple-element.111.refs_7_), channel_id=1, source_target_pairs={{0,1},{1,0},{2,3},{3,2},{4,5},{5,4},{6,7},{7,6},{8,9},{9,8},{10,11... | collective-permute-start | bytes 786440 | tf_op jit(solution)/shard_map/ppermute | solution.py:53
  67.1 23.1 %collective-permute-start.6 = (bf16[256,1024]{1,0:T(8,128)(2,1)S(1)}, bf16[256,1024]{1,0:T(8,128)(2,1)S(1)}, u32[]{:S(2)}, u32[]{:S(2)}) collective-permute-start(bf16[256,1024]{1,0:T(8,128)(2,1)S(1)} %get-tuple-element.114), channel_id=1, source_target_pairs={{0,1},{1,0},{2,3},{3,2},{4,5},{5,4},{6,7},{7,6},{8,9},{9,8},{10,11... | collective-permute-start | bytes 1572872 | tf_op jit(solution)/shard_map/ppermute | solution.py:61
  67.5 23.2 %collective-permute-start.7 = (bf16[256,1024]{1,0:T(8,128)(2,1)S(1)}, bf16[256,1024]{1,0:T(8,128)(2,1)S(1)}, u32[]{:S(2)}, u32[]{:S(2)}) collective-permute-start(bf16[256,1024]{1,0:T(8,128)(2,1)S(1)} %get-tuple-element.115), channel_id=1, source_target_pairs={{0,2},{2,0},{1,3},{3,1},{4,6},{6,4},{5,7},{7,5},{8,10},{10,8},{9,1... | collective-permute-start | bytes 1572872 | tf_op jit(solution)/shard_map/ppermute | solution.py:62
  93.7 12.3 %collective-permute-start.8 = (bf16[128,1024]{1,0:T(8,128)(2,1)}, bf16[128,1024]{1,0:T(8,128)(2,1)S(1)}, u32[]{:S(2)}, u32[]{:S(2)}) collective-permute-start(bf16[128,1024]{1,0:T(8,128)(2,1)} %get-tuple-element.118), channel_id=1, source_target_pairs={{0,2},{2,0},{1,3},{3,1},{4,6},{6,4},{5,7},{7,5},{8,10},{10,8},{9,1... | collective-permute-start | bytes 786440 | tf_op jit(solution)/shard_map/ppermute | solution.py:70
  94.1 12.8 %collective-permute-start.9 = (bf16[128,1024]{1,0:T(8,128)(2,1)}, bf16[128,1024]{1,0:T(8,128)(2,1)S(1)}, u32[]{:S(2)}, u32[]{:S(2)}) collective-permute-start(bf16[128,1024]{1,0:T(8,128)(2,1)} %get-tuple-element.119), channel_id=1, source_target_pairs={{0,1},{1,0},{2,3},{3,2},{4,5},{5,4},{6,7},{7,6},{8,9},{9,8},{10,11... | collective-permute-start | bytes 786440 | tf_op jit(solution)/shard_map/ppermute | solution.py:71
  112.6 317.6 %all-gather.11.cloned.1.call-start = ((), (), s32[]{:S(2)}) async-start(), calls=%async_computation.3 | async-start | bytes 4325376 | tf_op jit(solution)/shard_map/all_gather | solution.py:785
  113.4 316.8 %all-gather.9.cloned.1.call-start = ((), (), s32[]{:S(2)}) async-start(), calls=%async_computation.2 | async-start | bytes 4325376 | tf_op jit(solution)/shard_map/all_gather | solution.py:826
  114.8 14.1 %collective-permute-start.16 = (bf16[64,2048]{1,0:T(8,128)(2,1)}, bf16[64,2048]{1,0:T(8,128)(2,1)S(1)}, u32[]{:S(2)}, u32[]{:S(2)}) collective-permute-start(bf16[64,2048]{1,0:T(8,128)(2,1)} %get-tuple-element.127), channel_id=1, source_target_pairs={{0,1},{1,0},{2,3},{3,2},{4,5},{5,4},{6,7},{7,6},{8,9},{9,8},{10,11... | collective-permute-start | bytes 786440 | tf_op jit(solution)/shard_map/ppermute | solution.py:46
  116.6 14.9 %collective-permute-start.17 = (bf16[64,2048]{1,0:T(8,128)(2,1)}, bf16[64,2048]{1,0:T(8,128)(2,1)S(1)}, u32[]{:S(2)}, u32[]{:S(2)}) collective-permute-start(bf16[64,2048]{1,0:T(8,128)(2,1)} %get-tuple-element.127), channel_id=1, source_target_pairs={{0,2},{2,0},{1,3},{3,1},{4,6},{6,4},{5,7},{7,5},{8,10},{10,8},{9,1... | collective-permute-start | bytes 786440 | tf_op jit(solution)/shard_map/ppermute | solution.py:49
  116.6 13.6 %collective-permute-start.20 = (bf16[64,2048]{1,0:T(8,128)(2,1)}, bf16[64,2048]{1,0:T(8,128)(2,1)S(1)}, u32[]{:S(2)}, u32[]{:S(2)}) collective-permute-start(bf16[64,2048]{1,0:T(8,128)(2,1)} %get-tuple-element.128), channel_id=1, source_target_pairs={{0,2},{2,0},{1,3},{3,1},{4,6},{6,4},{5,7},{7,5},{8,10},{10,8},{9,1... | collective-permute-start | bytes 786440 | tf_op jit(solution)/shard_map/ppermute | solution.py:47
  120.3 20.4 %collective-permute-start.19 = (bf16[64,2048]{1,0:T(8,128)(2,1)}, bf16[64,2048]{1,0:T(8,128)(2,1)}, u32[]{:S(2)}, u32[]{:S(2)}) collective-permute-start(bf16[64,2048]{1,0:T(8,128)(2,1)} %get-tuple-element.128), channel_id=1, source_target_pairs={{0,1},{1,0},{2,3},{3,2},{4,5},{5,4},{6,7},{7,6},{8,9},{9,8},{10,11... | collective-permute-start | bytes 786440 | tf_op jit(solution)/shard_map/ppermute | solution.py:48
  128.9 10.3 %collective-permute-start.18 = (bf16[64,2048]{1,0:T(8,128)(2,1)S(1)}, bf16[64,2048]{1,0:T(8,128)(2,1)S(1)}, u32[]{:S(2)}, u32[]{:S(2)}) collective-permute-start(bf16[64,2048]{1,0:T(8,128)(2,1)S(1)} %collective-permute-done.16), channel_id=1, source_target_pairs={{0,2},{2,0},{1,3},{3,1},{4,6},{6,4},{5,7},{7,5},{8,10},{10,8},{9,1... | collective-permute-start | bytes 786440 | tf_op jit(solution)/shard_map/ppermute | solution.py:52
  130.1 14.8 %collective-permute-start.21 = (bf16[64,2048]{1,0:T(8,128)(2,1)S(1)}, bf16[64,2048]{1,0:T(8,128)(2,1)S(1)}, u32[]{:S(2)}, u32[]{:S(2)}) collective-permute-start(bf16[64,2048]{1,0:T(8,128)(2,1)S(1)} %collective-permute-done.20), channel_id=1, source_target_pairs={{0,1},{1,0},{2,3},{3,2},{4,5},{5,4},{6,7},{7,6},{8,9},{9,8},{10,11... | collective-permute-start | bytes 786440 | tf_op jit(solution)/shard_map/ppermute | solution.py:53
  145.6 15.1 %collective-permute-start.12 = (bf16[64,2048]{1,0:T(8,128)(2,1)S(1)}, bf16[64,2048]{1,0:T(8,128)(2,1)S(1)}, u32[]{:S(2)}, u32[]{:S(2)}) collective-permute-start(bf16[64,2048]{1,0:T(8,128)(2,1)S(1)} %get-tuple-element.121.refs_0_), channel_id=1, source_target_pairs={{0,2},{2,0},{1,3},{3,1},{4,6},{6,4},{5,7},{7,5},{8,10},{10,8},{9,1... | collective-permute-start | bytes 786440 | tf_op jit(solution)/shard_map/ppermute | solution.py:49
  147.7 13.1 %collective-permute-start.14 = (bf16[64,2048]{1,0:T(8,128)(2,1)S(1)}, bf16[64,2048]{1,0:T(8,128)(2,1)S(1)}, u32[]{:S(2)}, u32[]{:S(2)}) collective-permute-start(bf16[64,2048]{1,0:T(8,128)(2,1)S(1)} %get-tuple-element.122.refs_4_), channel_id=1, source_target_pairs={{0,1},{1,0},{2,3},{3,2},{4,5},{5,4},{6,7},{7,6},{8,9},{9,8},{10,11... | collective-permute-start | bytes 786440 | tf_op jit(solution)/shard_map/ppermute | solution.py:48
  151.3 9.5 %collective-permute-start.13 = (bf16[64,2048]{1,0:T(8,128)(2,1)}, bf16[64,2048]{1,0:T(8,128)(2,1)S(1)}, u32[]{:S(2)}, u32[]{:S(2)}) collective-permute-start(bf16[64,2048]{1,0:T(8,128)(2,1)} %get-tuple-element.125.refs_1_), channel_id=1, source_target_pairs={{0,2},{2,0},{1,3},{3,1},{4,6},{6,4},{5,7},{7,5},{8,10},{10,8},{9,1... | collective-permute-start | bytes 786440 | tf_op jit(solution)/shard_map/ppermute | solution.py:52
  151.3 9.5 %collective-permute-start.15 = (bf16[64,2048]{1,0:T(8,128)(2,1)}, bf16[64,2048]{1,0:T(8,128)(2,1)S(1)}, u32[]{:S(2)}, u32[]{:S(2)}) collective-permute-start(bf16[64,2048]{1,0:T(8,128)(2,1)} %get-tuple-element.126.refs_6_), channel_id=1, source_target_pairs={{0,1},{1,0},{2,3},{3,2},{4,5},{5,4},{6,7},{7,6},{8,9},{9,8},{10,11... | collective-permute-start | bytes 786440 | tf_op jit(solution)/shard_map/ppermute | solution.py:53
  186.1 23.4 %collective-permute-start.22 = (bf16[256,1024]{1,0:T(8,128)(2,1)}, bf16[256,1024]{1,0:T(8,128)(2,1)S(1)}, u32[]{:S(2)}, u32[]{:S(2)}) collective-permute-start(bf16[256,1024]{1,0:T(8,128)(2,1)} %get-tuple-element.136), channel_id=1, source_target_pairs={{0,1},{1,0},{2,3},{3,2},{4,5},{5,4},{6,7},{7,6},{8,9},{9,8},{10,11... | collective-permute-start | bytes 1572872 | tf_op jit(solution)/shard_map/ppermute | solution.py:61
  187.9 22.6 %collective-permute-start.23 = (bf16[256,1024]{1,0:T(8,128)(2,1)}, bf16[256,1024]{1,0:T(8,128)(2,1)S(1)}, u32[]{:S(2)}, u32[]{:S(2)}) collective-permute-start(bf16[256,1024]{1,0:T(8,128)(2,1)} %get-tuple-element.137), channel_id=1, source_target_pairs={{0,2},{2,0},{1,3},{3,1},{4,6},{6,4},{5,7},{7,5},{8,10},{10,8},{9,1... | collective-permute-start | bytes 1572872 | tf_op jit(solution)/shard_map/ppermute | solution.py:62
  213.6 11.9 %collective-permute-start.24 = (bf16[128,1024]{1,0:T(8,128)(2,1)}, bf16[128,1024]{1,0:T(8,128)(2,1)S(1)}, u32[]{:S(2)}, u32[]{:S(2)}) collective-permute-start(bf16[128,1024]{1,0:T(8,128)(2,1)} %get-tuple-element.142), channel_id=1, source_target_pairs={{0,2},{2,0},{1,3},{3,1},{4,6},{6,4},{5,7},{7,5},{8,10},{10,8},{9,1... | collective-permute-start | bytes 786440 | tf_op jit(solution)/shard_map/ppermute | solution.py:70
  215.0 11.4 %collective-permute-start.25 = (bf16[128,1024]{1,0:T(8,128)(2,1)}, bf16[128,1024]{1,0:T(8,128)(2,1)S(1)}, u32[]{:S(2)}, u32[]{:S(2)}) collective-permute-start(bf16[128,1024]{1,0:T(8,128)(2,1)} %get-tuple-element.143), channel_id=1, source_target_pairs={{0,1},{1,0},{2,3},{3,2},{4,5},{5,4},{6,7},{7,6},{8,9},{9,8},{10,11... | collective-permute-start | bytes 786440 | tf_op jit(solution)/shard_map/ppermute | solution.py:71
  232.5 6.8 %collective-permute-start.30 = (bf16[64,2048]{1,0:T(8,128)(2,1)S(1)}, bf16[64,2048]{1,0:T(8,128)(2,1)S(1)}, u32[]{:S(2)}, u32[]{:S(2)}) collective-permute-start(bf16[64,2048]{1,0:T(8,128)(2,1)S(1)} %get-tuple-element.146.refs_5_), channel_id=1, source_target_pairs={{0,2},{2,0},{1,3},{3,1},{4,6},{6,4},{5,7},{7,5},{8,10},{10,8},{9,1... | collective-permute-start | bytes 786440 | tf_op jit(solution)/shard_map/ppermute | solution.py:47
  233.3 8.3 %collective-permute-start.27 = (bf16[64,2048]{1,0:T(8,128)(2,1)S(1)}, bf16[64,2048]{1,0:T(8,128)(2,1)S(1)}, u32[]{:S(2)}, u32[]{:S(2)}) collective-permute-start(bf16[64,2048]{1,0:T(8,128)(2,1)S(1)} %get-tuple-element.145.refs_1_.rest_0_), channel_id=1, source_target_pairs={{0,2},{2,0},{1,3},{3,1},{4,6},{6,4},{5,7},{7,5},{8,10},{10,8},{9,1... | collective-permute-start | bytes 786440 | tf_op jit(solution)/shard_map/ppermute | solution.py:49
  234.5 7.2 %collective-permute-start.29 = (bf16[64,2048]{1,0:T(8,128)(2,1)S(1)}, bf16[64,2048]{1,0:T(8,128)(2,1)S(1)}, u32[]{:S(2)}, u32[]{:S(2)}) collective-permute-start(bf16[64,2048]{1,0:T(8,128)(2,1)S(1)} %get-tuple-element.146.refs_5_), channel_id=1, source_target_pairs={{0,1},{1,0},{2,3},{3,2},{4,5},{5,4},{6,7},{7,6},{8,9},{9,8},{10,11... | collective-permute-start | bytes 786440 | tf_op jit(solution)/shard_map/ppermute | solution.py:48
  238.0 6.5 collective-permute-start.28
  272.8 35.1 %collective-permute-start.46 = (bf16[512,1024]{1,0:T(8,128)(2,1)}, bf16[512,1024]{1,0:T(8,128)(2,1)}, u32[]{:S(2)}, u32[]{:S(2)}) collective-permute-start(bf16[512,1024]{1,0:T(8,128)(2,1)} %get-tuple-element.210), channel_id=1, source_target_pairs={{0,4},{4,0},{1,5},{5,1},{2,6},{6,2},{3,7},{7,3},{8,12},{12,8},{9,1... | collective-permute-start | bytes 3145736 | tf_op jit(solution)/shard_map/ppermute | solution.py:76
  272.9 15.0 %collective-permute-start.32 = (bf16[256,1024]{1,0:T(8,128)(2,1)S(1)}, bf16[256,1024]{1,0:T(8,128)(2,1)S(1)}, u32[]{:S(2)}, u32[]{:S(2)}) collective-permute-start(bf16[256,1024]{1,0:T(8,128)(2,1)S(1)} %get-tuple-element.154), channel_id=1, source_target_pairs={{0,1},{1,0},{2,3},{3,2},{4,5},{5,4},{6,7},{7,6},{8,9},{9,8},{10,11... | collective-permute-start | bytes 1572872 | tf_op jit(solution)/shard_map/ppermute | solution.py:61
  277.4 99.9 %collective-permute-start.53 = (bf16[640,1024]{1,0:T(8,128)(2,1)}, bf16[640,1024]{1,0:T(8,128)(2,1)}, u32[]{:S(2)}, u32[]{:S(2)}) collective-permute-start(bf16[640,1024]{1,0:T(8,128)(2,1)} %fusion.4), channel_id=1, source_target_pairs={{0,8},{24,16},{1,9},{25,17},{2,10},{26,18},{3,11},{27,19},{4,12},{... | collective-permute-start | bytes 3932168 | tf_op jit(solution)/shard_map/ppermute | solution.py:97
  282.1 26.8 %collective-permute-start.49 = (bf16[512,640]{1,0:T(8,128)(2,1)}, bf16[512,640]{1,0:T(8,128)(2,1)}, u32[]{:S(2)}, u32[]{:S(2)}) collective-permute-start(bf16[512,640]{1,0:T(8,128)(2,1)} %get-tuple-element.174), channel_id=1, source_target_pairs={{0,4},{4,0},{1,5},{5,1},{2,6},{6,2},{3,7},{7,3},{8,12},{12,8},{9,1... | collective-permute-start | bytes 1966088 | tf_op jit(solution)/shard_map/ppermute | solution.py:76
  282.2 21.7 %collective-permute-start.33 = (bf16[256,1024]{1,0:T(8,128)(2,1)S(1)}, bf16[256,1024]{1,0:T(8,128)(2,1)S(1)}, u32[]{:S(2)}, u32[]{:S(2)}) collective-permute-start(bf16[256,1024]{1,0:T(8,128)(2,1)S(1)} %get-tuple-element.155), channel_id=1, source_target_pairs={{0,2},{2,0},{1,3},{3,1},{4,6},{6,4},{5,7},{7,5},{8,10},{10,8},{9,1... | collective-permute-start | bytes 1572872 | tf_op jit(solution)/shard_map/ppermute | solution.py:62
  287.9 27.8 %collective-permute-start.47 = (bf16[512,640]{1,0:T(8,128)(2,1)}, bf16[512,640]{1,0:T(8,128)(2,1)}, u32[]{:S(2)}, u32[]{:S(2)}) collective-permute-start(bf16[512,640]{1,0:T(8,128)(2,1)} %get-tuple-element.173), channel_id=1, source_target_pairs={{0,4},{4,0},{1,5},{5,1},{2,6},{6,2},{3,7},{7,3},{8,12},{12,8},{9,1... | collective-permute-start | bytes 1966088 | tf_op jit(solution)/shard_map/ppermute | solution.py:76
  306.9 75.8 %collective-permute-start.34 = (bf16[128,1024]{1,0:T(8,128)(2,1)}, bf16[128,1024]{1,0:T(8,128)(2,1)S(1)}, u32[]{:S(2)}, u32[]{:S(2)}) collective-permute-start(bf16[128,1024]{1,0:T(8,128)(2,1)} %get-tuple-element.158), channel_id=1, source_target_pairs={{0,2},{2,0},{1,3},{3,1},{4,6},{6,4},{5,7},{7,5},{8,10},{10,8},{9,1... | collective-permute-start | bytes 786440 | tf_op jit(solution)/shard_map/ppermute | solution.py:70
  307.9 74.8 %collective-permute-start.35 = (bf16[128,1024]{1,0:T(8,128)(2,1)}, bf16[128,1024]{1,0:T(8,128)(2,1)S(1)}, u32[]{:S(2)}, u32[]{:S(2)}) collective-permute-start(bf16[128,1024]{1,0:T(8,128)(2,1)} %get-tuple-element.159), channel_id=1, source_target_pairs={{0,1},{1,0},{2,3},{3,2},{4,5},{5,4},{6,7},{7,6},{8,9},{9,8},{10,11... | collective-permute-start | bytes 786440 | tf_op jit(solution)/shard_map/ppermute | solution.py:71
  313.4 169.4 %collective-permute-start.50 = (bf16[1024,640]{1,0:T(8,128)(2,1)}, bf16[1024,640]{1,0:T(8,128)(2,1)}, u32[]{:S(2)}, u32[]{:S(2)}) collective-permute-start(bf16[1024,640]{1,0:T(8,128)(2,1)} %convolution_convert_fusion), channel_id=1, source_target_pairs={{0,8},{24,16},{1,9},{25,17},{2,10},{26,18},{3,11},{27,19},{4,12},{... | collective-permute-start | bytes 3932168 | tf_op jit(solution)/shard_map/ppermute | solution.py:97
  380.9 101.9 %collective-permute-start.54 = (bf16[640,1024]{1,0:T(8,128)(2,1)}, bf16[640,1024]{1,0:T(8,128)(2,1)}, u32[]{:S(2)}, u32[]{:S(2)}) collective-permute-start(bf16[640,1024]{1,0:T(8,128)(2,1)} %add_convert_fusion.5), channel_id=1, source_target_pairs={{8,16},{16,8},{9,17},{17,9},{10,18},{18,10},{11,19},{19,11},{12,20... | collective-permute-start | bytes 3932168 | tf_op jit(solution)/shard_map/ppermute | solution.py:97
  388.7 109.5 %collective-permute-start.48 = (bf16[1024,640]{1,0:T(8,128)(2,1)S(1)}, bf16[1024,640]{1,0:T(8,128)(2,1)}, u32[]{:S(2)}, u32[]{:S(2)}) collective-permute-start(bf16[1024,640]{1,0:T(8,128)(2,1)S(1)} %convolution_convert_fusion.1.rest_0_), channel_id=1, source_target_pairs={{0,8},{24,16},{1,9},{25,17},{2,10},{26,18},{3,11},{27,19},{4,12},{... | collective-permute-start | bytes 3932168 | tf_op jit(solution)/shard_map/ppermute | solution.py:97
  391.5 67.5 %collective-permute-start.36 = (bf16[256,1024]{1,0:T(8,128)(2,1)}, bf16[256,1024]{1,0:T(8,128)(2,1)S(1)}, u32[]{:S(2)}, u32[]{:S(2)}) collective-permute-start(bf16[256,1024]{1,0:T(8,128)(2,1)} %get-tuple-element.162), channel_id=1, source_target_pairs={{0,1},{1,0},{2,3},{3,2},{4,5},{5,4},{6,7},{7,6},{8,9},{9,8},{10,11... | collective-permute-start | bytes 1572872 | tf_op jit(solution)/shard_map/ppermute | solution.py:61
  392.7 68.0 %collective-permute-start.37 = (bf16[256,1024]{1,0:T(8,128)(2,1)}, bf16[256,1024]{1,0:T(8,128)(2,1)}, u32[]{:S(2)}, u32[]{:S(2)}) collective-permute-start(bf16[256,1024]{1,0:T(8,128)(2,1)} %get-tuple-element.163), channel_id=1, source_target_pairs={{0,2},{2,0},{1,3},{3,1},{4,6},{6,4},{5,7},{7,5},{8,10},{10,8},{9,1... | collective-permute-start | bytes 1572872 | tf_op jit(solution)/shard_map/ppermute | solution.py:62
  459.0 79.5 %collective-permute-start.70 = (bf16[768,2048]{1,0:T(8,128)(2,1)}, bf16[768,2048]{1,0:T(8,128)(2,1)}, u32[]{:S(2)}, u32[]{:S(2)}) collective-permute-start(bf16[768,2048]{1,0:T(8,128)(2,1)} %shard_map.333.refs_4_), channel_id=1, source_target_pairs={{0,4},{4,0},{1,5},{5,1},{2,6},{6,2},{3,7},{7,3},{8,12},{12,8},{9,1... | collective-permute-start | bytes 9437192 | tf_op jit(solution)/shard_map/ppermute | solution.py:76
  460.7 26.5 %collective-permute-start.43 = (bf16[4,160,160]{2,1,0:T(8,128)(2,1)}, bf16[4,160,160]{2,1,0:T(8,128)(2,1)}, u32[]{:S(2)}, u32[]{:S(2)}) collective-permute-start(bf16[4,160,160]{2,1,0:T(8,128)(2,1)} %broadcast_select_fusion.12), channel_id=1, source_target_pairs={{0,4},{4,0},{1,5},{5,1},{2,6},{6,2},{3,7},{7,3},{8,12},{12,8},{9,1... | collective-permute-start | bytes 614408 | tf_op jit(solution)/shard_map/ppermute | solution.py:76
  482.9 8.7 %collective-permute-start.38 = (bf16[128,1024]{1,0:T(8,128)(2,1)S(1)}, bf16[128,1024]{1,0:T(8,128)(2,1)S(1)}, u32[]{:S(2)}, u32[]{:S(2)}) collective-permute-start(bf16[128,1024]{1,0:T(8,128)(2,1)S(1)} %copy-done.113), channel_id=1, source_target_pairs={{0,2},{2,0},{1,3},{3,1},{4,6},{6,4},{5,7},{7,5},{8,10},{10,8},{9,1... | collective-permute-start | bytes 786440 | tf_op jit(solution)/shard_map/ppermute | solution.py:70
  487.2 8.5 %collective-permute-start.39 = (bf16[128,1024]{1,0:T(8,128)(2,1)S(1)}, bf16[128,1024]{1,0:T(8,128)(2,1)S(1)}, u32[]{:S(2)}, u32[]{:S(2)}) collective-permute-start(bf16[128,1024]{1,0:T(8,128)(2,1)S(1)} %copy-done.112), channel_id=1, source_target_pairs={{0,1},{1,0},{2,3},{3,2},{4,5},{5,4},{6,7},{7,6},{8,9},{9,8},{10,11... | collective-permute-start | bytes 786440 | tf_op jit(solution)/shard_map/ppermute | solution.py:71
  488.1 55.0 %collective-permute-start.68 = (bf16[768,2048]{1,0:T(8,128)(2,1)}, bf16[768,2048]{1,0:T(8,128)(2,1)}, u32[]{:S(2)}, u32[]{:S(2)}) collective-permute-start(bf16[768,2048]{1,0:T(8,128)(2,1)} %shard_map.337.own_ref), channel_id=1, source_target_pairs={{0,4},{4,0},{1,5},{5,1},{2,6},{6,2},{3,7},{7,3},{8,12},{12,8},{9,1... | collective-permute-start | bytes 9437192 | tf_op jit(solution)/shard_map/ppermute | solution.py:76
  492.3 56.6 %collective-permute-start.69 = (bf16[768,2048]{1,0:T(8,128)(2,1)}, bf16[768,2048]{1,0:T(8,128)(2,1)}, u32[]{:S(2)}, u32[]{:S(2)}) collective-permute-start(bf16[768,2048]{1,0:T(8,128)(2,1)} %shard_map.335.refs_3_.own_ref), channel_id=1, source_target_pairs={{0,4},{4,0},{1,5},{5,1},{2,6},{6,2},{3,7},{7,3},{8,12},{12,8},{9,1... | collective-permute-start | bytes 9437192 | tf_op jit(solution)/shard_map/ppermute | solution.py:76
  496.4 11.6 %collective-permute-start.55 = (bf16[1024,640]{1,0:T(8,128)(2,1)}, bf16[1024,640]{1,0:T(8,128)(2,1)}, u32[]{:S(2)}, u32[]{:S(2)}) collective-permute-start(bf16[1024,640]{1,0:T(8,128)(2,1)} %add_convert_fusion.4), channel_id=1, source_target_pairs={{8,16},{16,8},{9,17},{17,9},{10,18},{18,10},{11,19},{19,11},{12,20... | collective-permute-start | bytes 3932168 | tf_op jit(solution)/shard_map/ppermute | solution.py:97
  498.2 33.4 %collective-permute-start.56 = (bf16[640,1024]{1,0:T(8,128)(2,1)}, bf16[640,1024]{1,0:T(8,128)(2,1)}, u32[]{:S(2)}, u32[]{:S(2)}) collective-permute-start(bf16[640,1024]{1,0:T(8,128)(2,1)} %add_convert_fusion.3), channel_id=1, source_target_pairs={{8,0},{16,24},{9,1},{17,25},{10,2},{18,26},{11,3},{19,27},{12,4},{... | collective-permute-start | bytes 3932168 | tf_op jit(solution)/shard_map/ppermute | solution.py:97
  508.0 74.0 %collective-permute-start.44 = (bf16[4,160,160]{2,1,0:T(8,128)(2,1)}, bf16[4,160,160]{2,1,0:T(8,128)(2,1)S(1)}, u32[]{:S(2)}, u32[]{:S(2)}) collective-permute-start(bf16[4,160,160]{2,1,0:T(8,128)(2,1)} %add_convert_fusion.8), channel_id=1, source_target_pairs={{0,8},{24,16},{1,9},{25,17},{2,10},{26,18},{3,11},{27,19},{4,12},{... | collective-permute-start | bytes 614408 | tf_op jit(solution)/shard_map/ppermute | solution.py:97
  533.2 48.8 %collective-permute-start.57 = (bf16[1024,640]{1,0:T(8,128)(2,1)S(1)}, bf16[1024,640]{1,0:T(8,128)(2,1)}, u32[]{:S(2)}, u32[]{:S(2)}) collective-permute-start(bf16[1024,640]{1,0:T(8,128)(2,1)S(1)} %add_convert_fusion.2), channel_id=1, source_target_pairs={{8,16},{16,8},{9,17},{17,9},{10,18},{18,10},{11,19},{19,11},{12,20... | collective-permute-start | bytes 3932168 | tf_op jit(solution)/shard_map/ppermute | solution.py:97
  538.5 43.5 %collective-permute-start.58 = (bf16[1024,640]{1,0:T(8,128)(2,1)S(1)}, bf16[1024,640]{1,0:T(8,128)(2,1)}, u32[]{:S(2)}, u32[]{:S(2)}) collective-permute-start(bf16[1024,640]{1,0:T(8,128)(2,1)S(1)} %add_convert_fusion.1), channel_id=1, source_target_pairs={{8,0},{16,24},{9,1},{17,25},{10,2},{18,26},{11,3},{19,27},{12,4},{... | collective-permute-start | bytes 3932168 | tf_op jit(solution)/shard_map/ppermute | solution.py:97
  543.1 38.9 %collective-permute-start.45 = (f32[72,128]{1,0:T(8,128)S(1)}, f32[72,128]{1,0:T(8,128)S(1)}, u32[]{:S(2)}, u32[]{:S(2)}) collective-permute-start(f32[72,128]{1,0:T(8,128)S(1)} %copy-done.101), channel_id=1, source_target_pairs={{0,8},{24,16},{1,9},{25,17},{2,10},{26,18},{3,11},{27,19},{4,12},{... | collective-permute-start | bytes 110600 | tf_op jit(solution)/shard_map/ppermute | solution.py:97
  548.9 43.2 %collective-permute-start.67 = (bf16[640,1024]{1,0:T(8,128)(2,1)S(1)}, bf16[640,1024]{1,0:T(8,128)(2,1)}, u32[]{:S(2)}, u32[]{:S(2)}) collective-permute-start(bf16[640,1024]{1,0:T(8,128)(2,1)S(1)} %broadcast_select_fusion.2), channel_id=1, source_target_pairs={{0,4},{4,0},{1,5},{5,1},{2,6},{6,2},{3,7},{7,3},{8,12},{12,8},{9,1... | collective-permute-start | bytes 3932168 | tf_op jit(solution)/shard_map/ppermute | solution.py:76
  584.9 33.2 %collective-permute-start.61 = (bf16[1024,640]{1,0:T(8,128)(2,1)S(1)}, bf16[1024,640]{1,0:T(8,128)(2,1)}, u32[]{:S(2)}, u32[]{:S(2)}) collective-permute-start(bf16[1024,640]{1,0:T(8,128)(2,1)S(1)} %add_convert_fusion), channel_id=1, source_target_pairs={{8,0},{16,24},{9,1},{17,25},{10,2},{18,26},{11,3},{19,27},{12,4},{... | collective-permute-start | bytes 3932168 | tf_op jit(solution)/shard_map/ppermute | solution.py:97
  587.5 9.1 %collective-permute-start.59 = (bf16[4,160,160]{2,1,0:T(8,128)(2,1)S(1)}, bf16[4,160,160]{2,1,0:T(8,128)(2,1)S(1)}, u32[]{:S(2)}, u32[]{:S(2)}) collective-permute-start(bf16[4,160,160]{2,1,0:T(8,128)(2,1)S(1)} %add_convert_fusion.7), channel_id=1, source_target_pairs={{8,16},{16,8},{9,17},{17,9},{10,18},{18,10},{11,19},{19,11},{12,20... | collective-permute-start | bytes 614408 | tf_op jit(solution)/shard_map/ppermute | solution.py:97
  590.9 32.4 %collective-permute-start.63 = (bf16[1024,640]{1,0:T(8,128)(2,1)}, bf16[1024,640]{1,0:T(8,128)(2,1)}, u32[]{:S(2)}, u32[]{:S(2)}) collective-permute-start(bf16[1024,640]{1,0:T(8,128)(2,1)} %broadcast_select_fusion.6), channel_id=1, source_target_pairs={{0,4},{4,0},{1,5},{5,1},{2,6},{6,2},{3,7},{7,3},{8,12},{12,8},{9,1... | collective-permute-start | bytes 3932168 | tf_op jit(solution)/shard_map/ppermute | solution.py:76
  619.0 8.9 %collective-permute-start.62 = (f32[72,128]{1,0:T(8,128)S(1)}, f32[72,128]{1,0:T(8,128)S(1)}, u32[]{:S(2)}, u32[]{:S(2)}) collective-permute-start(f32[72,128]{1,0:T(8,128)S(1)} %add.84), channel_id=1, source_target_pairs={{8,0},{16,24},{9,1},{17,25},{10,2},{18,26},{11,3},{19,27},{12,4},{... | collective-permute-start | bytes 110600 | tf_op jit(solution)/shard_map/ppermute | solution.py:97
  621.7 15.1 %collective-permute-start.64 = (bf16[1024,640]{1,0:T(8,128)(2,1)S(1)}, bf16[1024,640]{1,0:T(8,128)(2,1)}, u32[]{:S(2)}, u32[]{:S(2)}) collective-permute-start(bf16[1024,640]{1,0:T(8,128)(2,1)S(1)} %broadcast_select_fusion.5), channel_id=1, source_target_pairs={{0,4},{4,0},{1,5},{5,1},{2,6},{6,2},{3,7},{7,3},{8,12},{12,8},{9,1... | collective-permute-start | bytes 3932168 | tf_op jit(solution)/shard_map/ppermute | solution.py:76
  621.9 12.0 %collective-permute-start.65 = (bf16[4,160,160]{2,1,0:T(8,128)(2,1)S(1)}, bf16[4,160,160]{2,1,0:T(8,128)(2,1)S(1)}, u32[]{:S(2)}, u32[]{:S(2)}) collective-permute-start(bf16[4,160,160]{2,1,0:T(8,128)(2,1)S(1)} %add_convert_fusion.6), channel_id=1, source_target_pairs={{8,0},{16,24},{9,1},{17,25},{10,2},{18,26},{11,3},{19,27},{12,4},{... | collective-permute-start | bytes 614408 | tf_op jit(solution)/shard_map/ppermute | solution.py:97
  (127 other events, 941.7 us)
Sparse Core Ops, SparseCore 0:
  10.9 113.0 all-gather.6
  126.9 112.0 all-gather.4
  241.9 68.3 all-gather.10
  313.0 66.9 all-gather.8

commit v3 on v2

--- a/solution.py
+++ b/solution.py
@@ -15,7 +15,13 @@
 f32 = jnp.float32
 bf16 = jnp.bfloat16
 swap = [(0, 1), (1, 0)]
-brief = pl.CostEstimate(flops=1, bytes_accessed=1, transcendentals=0)
+
+
+def cost(micros):
+    return pl.CostEstimate(flops=0, bytes_accessed=int(micros * 3e6), transcendentals=0)
+
+
+brief = cost(1)
 large = pltpu.CompilerParams(vmem_limit_bytes=48 * 1024 * 1024)
 ALL = ("z", "core", "y", "x")
 STEP = 16
@@ -35,7 +41,7 @@
         out_specs=[anywhere] * len(values),
         out_shape=[jax.ShapeDtypeStruct(value.shape, value.dtype) for value in values],
         input_output_aliases={n: n for n in range(len(values))},
-        cost_estimate=brief,
+        cost_estimate=cost(0.1),
     )(*values, *after)
 
 
@@ -52,6 +58,17 @@
     one_d = lax.ppermute(one_x, "y", swap)
     two_d = lax.ppermute(two_y, "x", swap)
     return [one, one_x, one_y, one_d, two, two_x, two_y, two_d]
+
+
+def gather_blocks(block, square):
+    if not square:
+        return gather_row((block,), square)
+    return [
+        block,
+        lax.ppermute(block, "x", swap),
+        lax.ppermute(block, "y", swap),
+        lax.ppermute(block, ("y", "x"), [(0, 3), (3, 0), (1, 2), (2, 1)]),
+    ]
 
 
 def scatter_row(sends, square, beside=()):
@@ -76,36 +93,32 @@
     return lax.ppermute(value, "core", swap)
 
 
-def half_of(value, which, axis):
-    size = value.shape[axis] // 2
-    return lax.dynamic_slice_in_dim(value, which * size, size, axis=axis)
-
-
-def join(own, other, core, axis):
-    first = jnp.where(core == 0, own, other)
-    second = jnp.where(core == 0, other, own)
-    return jnp.concatenate([first, second], axis=axis).astype(f32)
-
-
-def line_sums(groups, beside):
+def line_move(pieces):
+    pairs = [[(0, 1), (3, 2)], [(1, 2), (2, 1)], [(1, 0), (2, 3)]]
+    return [(piece, stage, lax.ppermute(piece, "z", pairs[stage])) for piece, stage in pieces]
+
+
+def settle_kernel(inner_ref, *refs, stages):
+    count = len(stages)
+    for n, stage in enumerate(stages):
+        piece, other, out = refs[n], refs[count + n], refs[2 * count + n]
+        if stage < 2:
+            out[...] = (piece[...].astype(f32) + other[...].astype(f32)).astype(out.dtype)
+        else:
+            out[...] = jnp.where(inner_ref[0] == 1, piece[...], other[...])
+
+
+def line_settle(moved, after):
     place = lax.axis_index("z")
-    inner = (place == 1) | (place == 2)
-    pairs = [[(0, 1), (3, 2)], [(1, 2), (2, 1)], [(1, 0), (2, 3)]]
-    groups = [list(group) for group in groups]
-    for step in range(len(groups) + 2):
-        moves = [(step - stage, stage) for stage in range(3) if 0 <= step - stage < len(groups)]
-        got = [lax.ppermute(piece, "z", pairs[stage]) for n, stage in moves for piece in groups[n]]
-        if beside[step]:
-            got = held(got, beside[step])
-        got = list(got)
-        for n, stage in moves:
-            for k, piece in enumerate(groups[n]):
-                other = got.pop(0)
-                if stage < 2:
-                    groups[n][k] = (piece.astype(f32) + other.astype(f32)).astype(piece.dtype)
-                else:
-                    groups[n][k] = jnp.where(inner, piece, other)
-    return groups
+    inner = ((place == 1) | (place == 2)).astype(jnp.int32).reshape((1,))
+    pieces, stages, others = zip(*moved, strict=True)
+    return run(
+        functools.partial(settle_kernel, stages=stages),
+        [jax.ShapeDtypeStruct(piece.shape, piece.dtype) for piece in pieces],
+        (inner, *pieces, *others),
+        after=after,
+        scalar=True,
+    )
 
 
 def assemble(pieces, out_ref):
@@ -113,6 +126,44 @@
     for piece in pieces:
         out_ref[at : at + piece.shape[0], :] = piece[...]
         at += piece.shape[0]
+
+
+def split(whole_ref, core, mine_ref, theirs_ref):
+    size = mine_ref.shape[1]
+    for ref, which in ((mine_ref, core), (theirs_ref, 1 - core)):
+        ref[...] = whole_ref[:, pl.ds(pl.multiple_of(which * size, 128), size)]
+
+
+def pairs_kernel(*refs):
+    count = len(refs) // 5
+    for n in range(count):
+        own_left, other_left, own_right, other_right = refs[4 * n : 4 * n + 4]
+        out_ref = refs[4 * count + n]
+        cols = out_ref.shape[1]
+        for first in range(0, cols, 512):
+            span = slice(first, min(first + 512, cols))
+            out_ref[:, span] = (
+                lax.dot_general(
+                    own_left[...], own_right[:, span], contract_rows, preferred_element_type=f32
+                )
+                + lax.dot_general(
+                    other_left[...], other_right[:, span], contract_rows, preferred_element_type=f32
+                )
+            ).astype(bf16)
+
+
+def sum_kernel(one_ref, two_ref, *refs):
+    out_ref, count = refs[-1], one_ref.shape[0]
+    total = one_ref[...] + two_ref[...]
+    if len(refs) > 1:
+        gains = refs[0][...] + refs[1][...]
+        rest = jnp.zeros((gains.shape[0], total.shape[1] - gains.shape[1]), f32)
+        total = jnp.concatenate([total, jnp.concatenate([gains, rest], axis=1)], axis=0)
+    out_ref[...] = total.astype(out_ref.dtype)
+
+
+def add_one_kernel(one_ref, two_ref, out_ref):
+    out_ref[...] = one_ref[...] + two_ref[...]
 
 
 def send_shapes(length, width, plain):
@@ -126,8 +177,16 @@
     )
 
 
-def emit(value, first, width, sends, plain):
+def emit(value, first, width, sends, plain, spot=None):
     last = first + value.shape[1]
+    if spot is not None:
+        half = value.shape[0] // 8
+        for n in range(2):
+            for k in range(4):
+                start = pl.multiple_of((lax.bitwise_xor(k, spot) * 2 + n) * half, half)
+                block = value[(n * 4 + k) * half : (n * 4 + k + 1) * half]
+                sends[0][pl.ds(start, half), first:last] = block.astype(bf16)
+        return
     if plain:
         sends[0][:, first:last] = value.astype(bf16)
         return
@@ -181,32 +240,30 @@
     two_ref[...] = normed[half:]
 
 
-def second_norm_kernel(input_ref, gain_ref, *refs, cuts):
-    hidden_ref, one_ref, two_ref, *parts = refs[-3 - len(cuts) + 1 :]
-    addends = refs[: -3 - len(cuts) + 1]
+def second_norm_kernel(input_ref, gain_ref, *refs):
+    addends, (hidden_ref, one_ref, two_ref, all_ref) = refs[:-4], refs[-4:]
     hidden = input_ref[...].astype(f32) + finish(addends)
     hidden_ref[...] = hidden
     normed = (hidden * lax.rsqrt(mean_of(hidden * hidden) + eps) * gain_ref[...]).astype(bf16)
     half = normed.shape[0] // 2
     one_ref[...] = normed[:half]
     two_ref[...] = normed[half:]
-    for ref, first, last in zip(parts, cuts[:-1], cuts[1:], strict=True):
-        ref[...] = normed[first:last]
+    all_ref[...] = normed
 
 
 def norm_back_kernel(value_ref, before_ref, gain_ref, *refs, final):
-    outs = 2 if final else 4
+    outs = 1 if final else 4
     addends, outs = refs[:-outs], refs[-outs:]
     values = value_ref[...].astype(f32)
     scale = lax.rsqrt(mean_of(values * values) + eps)
     hat = values * scale
     grad = finish(addends)
-    outs[0][...] = jnp.sum(grad * hat, axis=0, keepdims=True)
     scaled = grad * gain_ref[...]
     total = before_ref[...].astype(f32) + scale * (scaled - hat * mean_of(scaled * hat))
     if final:
-        outs[1][...] = total.astype(bf16)
+        outs[0][...] = total.astype(bf16)
         return
+    outs[0][...] = jnp.sum(grad * hat, axis=0, keepdims=True)
     outs[1][...] = total
     low = total.astype(bf16)
     half = low.shape[0] // 2
@@ -263,12 +320,13 @@
             emit(total_ref[:, first : first + 512], first, width, outs, plain)
 
 
-def down_kernel(activ_ref, weight_ref, *sends, plain):
+def down_kernel(spot_ref, activ_ref, weight_ref, *sends, plain):
+    spot = None if plain else spot_ref[0]
     width = weight_ref.shape[1]
     for first in range(0, width, 512):
         cols = slice(first, first + 512)
         value = jnp.dot(activ_ref[...], weight_ref[:, cols], preferred_element_type=f32)
-        emit(value, first, width, sends, plain)
+        emit(value, first, width, sends, plain, spot)
 
 
 def tile_span(first, last, head, width):
@@ -349,12 +407,13 @@
         refs[:10],
         refs[10:],
     )
-    (normed_ref, branch_ref, stream_ref, gated_ref, conv_ref, recur_ref, intake_ref, state_ref), refs = (
-        refs[:8],
-        refs[8:],
-    )
-    *sends, part_high, part_low = refs
+    (mine_ref, theirs_ref, branch_ref, stream_ref, gated_ref, conv_ref, recur_ref, intake_ref, state_ref), refs = (
+        refs[:9],
+        refs[9:],
+    )
+    *sends, part_high, part_low, normed_ref = refs
     assemble(pieces, normed_ref)
+    split(normed_ref, spot_ref[1], mine_ref, theirs_ref)
     for first, last in tiles(branch_ref.shape[1]):
         cols = slice(first, last)
         branch_ref[:, cols] = jnp.dot(normed_ref[...], branch_w[:, cols], preferred_element_type=f32)
@@ -432,31 +491,56 @@
         emit(value, first, output_w.shape[1], sends, plain)
 
 
-def backward_kernel(spot_ref, *refs, count, head, plain):
-    pieces, refs = refs[:count], refs[count:]
-    (
-        output_w,
-        branch_w,
-        stream_w,
-        branch_ref,
-        stream_ref,
-        joined_ref,
-        conv_ref,
-        recur_ref,
-        intake_ref,
-        state_ref,
-        taps_ref,
-        high_ref,
-        soft_ref,
-    ), refs = refs[:13], refs[13:]
-    (cot_ref, branch_grad_ref, stream_grad_ref, gates_ref, sums_ref), refs = refs[:5], refs[5:]
-    *sends, grad_ref, pre_ref, conv_low, conv_grad = refs
+def branch_back_kernel(spot_ref, *refs, count):
+    pieces, (output_w, branch_ref, state_ref), refs = refs[:count], refs[count : count + 3], refs[count + 3 :]
+    mine_ref, theirs_ref, branch_grad_ref, grad_ref, cot_ref = refs
     assemble(pieces, cot_ref)
-    for first, last in tiles(branch_ref.shape[1]):
+    split(cot_ref, spot_ref[1], mine_ref, theirs_ref)
+    length, width = branch_ref.shape
+    for first, last in tiles(width):
         cols = slice(first, last)
         grad_ref[:, cols] = lax.dot_general(
             cot_ref[...], output_w[cols, :], contract_cols, preferred_element_type=f32
         )
+
+    def rows(step, _):
+        at = pl.ds(pl.multiple_of(step * STEP, STEP), STEP)
+        value, slope = gelu_terms(branch_ref[at, :])
+        grad = grad_ref[at, :]
+        branch_grad_ref[at, :] = (grad * state_ref[at, :] * slope).astype(bf16)
+        grad_ref[at, :] = grad * value
+        return _
+
+    lax.fori_loop(0, length // STEP, rows, 0)
+
+
+def backward_kernel(
+    spot_ref,
+    grad_ref,
+    branch_grad_ref,
+    branch_w,
+    stream_w,
+    stream_ref,
+    joined_ref,
+    conv_ref,
+    recur_ref,
+    intake_ref,
+    state_ref,
+    taps_ref,
+    high_ref,
+    soft_ref,
+    normed_mine,
+    normed_theirs,
+    gain_ref,
+    stream_grad_ref,
+    mine_ref,
+    theirs_ref,
+    gains_ref,
+    *refs,
+    head,
+    plain,
+):
+    *sends, gates_ref, sums_ref, pre_ref, conv_low, conv_grad = refs
     length, width = grad_ref.shape
     steps = length // STEP
     offset = token_place(length, spot_ref[0], plain)
@@ -482,9 +566,7 @@
         recur = recur_ref[pl.ds(here, STEP), :]
         intake = intake_ref[pl.ds(here, STEP), :]
         carried, square, root, multiplier = decay_terms(recur, soft, link)
-        value, slope = gelu_terms(branch_ref[pl.ds(at, STEP), :])
-        gated_grad = grad_ref[pl.ds(at, STEP), :]
-        grad = gated_grad * value
+        grad = grad_ref[pl.ds(at, STEP), :]
         found = []
         for part in reversed(range(count)):
             own = carried[8 * part : 8 * part + 8]
@@ -501,7 +583,6 @@
             found.append(adjoint)
         adjoint = jnp.concatenate(found[::-1], axis=0)
         state = state_ref[pl.ds(at, STEP), :]
-        branch_grad_ref[pl.ds(at, STEP), :] = (gated_grad * state * slope).astype(bf16)
         tail = state_ref[pl.ds(at_before + (STEP - 8), 8), :]
         earlier = jnp.concatenate([tail, state], axis=0)[7 : 7 + STEP]
         driven_part = adjoint * intake
@@ -560,6 +641,15 @@
     kept = lax.fori_loop(0, steps, unwind, (eight,) * 5)
     for k in range(5):
         sums_ref[k : k + 1, :] = jnp.sum(kept[k], axis=0, keepdims=True)
+    count = width // head
+    lanes = lax.broadcasted_iota(jnp.int32, (head, width), 1)
+    for out_ref, which in ((mine_ref, spot_ref[1]), (theirs_ref, 1 - spot_ref[1])):
+        blocks = gates_ref[which, 0:head, :]
+        for h in range(1, count):
+            blocks = jnp.where(lanes >= h * head, gates_ref[which, h * head : (h + 1) * head, :], blocks)
+        out_ref[0:head, :] = blocks
+        out_ref[head : head + 8, :] = sums_ref[...]
+
     step_cols = 512
     for first in range(0, branch_w.shape[0], step_cols):
         cols = slice(first, first + step_cols)
@@ -568,74 +658,200 @@
         ) + lax.dot_general(
             stream_grad_ref[...], stream_w[cols, :], contract_cols, preferred_element_type=f32
         )
-        emit(value, first, branch_w.shape[0], sends, plain)
-
-
-def rows_kernel(core_ref, token_ref, cot_ref, gate_ref, up_ref, down_ref, *rest):
+        half = normed_mine.shape[1]
+        inside = slice(first % half, first % half + step_cols)
+        mine = spot_ref[1] == first // half
+        normed = jnp.where(mine, normed_mine[:, inside], normed_theirs[:, inside]).astype(f32)
+        gains_ref[:, cols] = jnp.sum(value * normed, axis=0, keepdims=True) / gain_ref[:, cols]
+        emit(value, first, branch_w.shape[0], sends, plain, None if plain else spot_ref[0])
+
+
+def rows_kernel(token_ref, grad_ref, gate_ref, up_ref, *rest):
     activ_ref, gate_out, up_out = rest[-3:]
-    tokens, cots = token_ref[...], cot_ref[...]
+    tokens = token_ref[...]
     hidden = gate_ref.shape[0]
     part = hidden // 3
     for n in range(3):
         rows = slice(n * part, (n + 1) * part)
         gate_pre = lax.dot_general(gate_ref[rows], tokens, contract_cols, preferred_element_type=f32)
         up_pre = lax.dot_general(up_ref[rows], tokens, contract_cols, preferred_element_type=f32)
-        activ_grad = lax.dot_general(down_ref[rows], cots, contract_cols, preferred_element_type=f32)
+        activ_grad = grad_ref[rows]
         value, slope = gelu_terms(gate_pre)
         activ_ref[rows] = (value * up_pre).astype(bf16)
         gate_out[rows] = (activ_grad * up_pre * slope).astype(bf16)
         up_out[rows] = (activ_grad * value).astype(bf16)
 
 
-def mlp_rows(core, tokens, cots, gate, up, down, after):
+def mlp_rows(tokens, grads, gate, up, part, kept, after):
     count, width = tokens.shape
     hidden = gate.shape[0]
-    tile = 256
-    rows = pl.BlockSpec((tile, width), lambda i, core: (i, 0))
-    tall = pl.BlockSpec((hidden, tile), lambda i, core: (0, i))
-    weight = pl.BlockSpec((hidden, width), lambda i, core: (0, 0))
+    tile = 512
+    steps = count // tile // 2
+    tall = pl.BlockSpec((hidden, tile), lambda i: (0, i + part * steps))
+    weight = pl.BlockSpec((hidden, width), lambda i: (0, 0))
     return pl.pallas_call(
         rows_kernel,
+        grid=(steps,),
+        in_specs=[pl.BlockSpec((tile, width), lambda i: (i + part * steps, 0)), tall, weight, weight]
+        + [pl.BlockSpec(memory_space=pl.ANY)] * (len(kept) + len(after)),
+        out_specs=[tall, tall, tall],
+        out_shape=[jax.ShapeDtypeStruct((hidden, count), bf16)] * 3,
+        input_output_aliases={4 + n: n for n in range(len(kept))},
+        cost_estimate=cost(20),
+        compiler_params=large,
+    )(tokens, grads, gate, up, *kept, *after)
+
+
+def row_back_kernel(*refs, count):
+    pieces, (weight_ref, out_ref, rows_ref) = refs[:count], refs[count:]
+
+    @pl.when(pl.program_id(0) == 0)
+    def _():
+        half = pieces[0].shape[0] // 2
+        at = 0
+        for n in range(2):
+            for piece in pieces:
+                rows_ref[at : at + half, :] = piece[n * half : (n + 1) * half, :]
+                at += half
+
+    out_ref[...] = lax.dot_general(
+        rows_ref[...], weight_ref[...], contract_cols, preferred_element_type=f32
+    )
+
+
+def row_back(pieces, down):
+    hidden, width = down.shape
+    length = sum(piece.shape[0] for piece in pieces)
+    tile = min(512, hidden)
+    return pl.pallas_call(
+        functools.partial(row_back_kernel, count=len(pieces)),
+        grid=(hidden // tile,),
+        in_specs=[pl.BlockSpec(piece.shape, lambda i: (0, 0)) for piece in pieces]
+        + [pl.BlockSpec((tile, width), lambda i: (i, 0))],
+        out_specs=pl.BlockSpec((length, tile), lambda i: (0, i)),
+        out_shape=jax.ShapeDtypeStruct((length, hidden), f32),
+        scratch_shapes=[pltpu.VMEM((length, width), bf16)],
+        cost_estimate=cost(6),
+        compiler_params=large,
+    )(*pieces, down)
+
+
+def product(left, right, core, turn, after=()):
+    rows, depth = left.shape
+    cols = right.shape[1]
+    tile = 256
+
+    def body(core_ref, left_ref, right_ref, *rest):
+        low_ref, whole_ref = rest[-2:]
+        low = jnp.dot(left_ref[...], right_ref[...], preferred_element_type=f32).astype(bf16)
+        low_ref[...] = low
+        wide = low.astype(f32)
+        whole_ref[...] = wide.T if turn else wide
+
+    if turn:
+        place = pl.BlockSpec((tile, rows), lambda n, core: (n, core[0]))
+        shape = (cols, 2 * rows)
+    else:
+        place = pl.BlockSpec((rows, tile), lambda n, core: (core[0], n))
+        shape = (2 * rows, cols)
+    return pl.pallas_call(
+        body,
+        grid_spec=pltpu.PrefetchScalarGridSpec(
+            num_scalar_prefetch=1,
+            grid=(cols // tile,),
+            in_specs=[
+                pl.BlockSpec((rows, depth), lambda n, core: (0, 0)),
+                pl.BlockSpec((depth, tile), lambda n, core: (0, n)),
+            ]
+            + [pl.BlockSpec(memory_space=pl.ANY)] * len(after),
+            out_specs=[pl.BlockSpec((rows, tile), lambda n, core: (0, n)), place],
+        ),
+        out_shape=[jax.ShapeDtypeStruct((rows, cols), bf16), jax.ShapeDtypeStruct(shape, f32)],
+        cost_estimate=cost(20),
+        compiler_params=large,
+    )(core, left, right, *after)
+
+
+def filled(whole, other, core, turn, after=()):
+    rows, cols = other.shape
+    tile = cols // 2
+
+    def body(core_ref, other_ref, *rest):
+        wide = other_ref[...].astype(f32)
+        rest[-1][...] = wide.T if turn else wide
+
+    if turn:
+        place = pl.BlockSpec((tile, rows), lambda n, core: (n, 1 - core[0]))
+    else:
+        place = pl.BlockSpec((rows, tile), lambda n, core: (1 - core[0], n))
+    return pl.pallas_call(
+        body,
+        grid_spec=pltpu.PrefetchScalarGridSpec(
+            num_scalar_prefetch=1,
+            grid=(2,),
+            in_specs=[
+                pl.BlockSpec((rows, tile), lambda n, core: (0, n)),
+            ]
+            + [pl.BlockSpec(memory_space=pl.ANY)] * (1 + len(after)),
+            out_specs=place,
+        ),
+        out_shape=jax.ShapeDtypeStruct(whole.shape, f32),
+        input_output_aliases={2: 0},
+        cost_estimate=cost(4.5),
+        compiler_params=large,
+    )(core, other, whole, *after)
+
+
+def join_kernel(core_ref, own_ref, other_ref, *rest):
+    mine = pl.program_id(0) == core_ref[0]
+    rest[-1][...] = jnp.where(mine, own_ref[...], other_ref[...]).astype(f32)
+
+
+def joined_halves(own, other, core, axis, after):
+    rows, cols = own.shape
+    part = pl.BlockSpec((rows, cols), lambda h, core: (0, 0))
+    place = pl.BlockSpec((rows, cols), (lambda h, core: (h, 0)) if axis == 0 else (lambda h, core: (0, h)))
+    shape = (2 * rows, cols) if axis == 0 else (rows, 2 * cols)
+    return pl.pallas_call(
+        join_kernel,
+        grid_spec=pltpu.PrefetchScalarGridSpec(
+            num_scalar_prefetch=1,
+            grid=(2,),
+            in_specs=[part, part] + [pl.BlockSpec(memory_space=pl.ANY)] * len(after),
+            out_specs=place,
+        ),
+        out_shape=jax.ShapeDtypeStruct(shape, f32),
+        cost_estimate=cost(4),
+        compiler_params=large,
+    )(core, own, other, *after)
+
+
+def back_kernel(core_ref, weight_ref, cot_ref, *rest):
+    rest[-1][...] = lax.dot_general(
+        weight_ref[...], cot_ref[...], contract_cols, preferred_element_type=f32
+    )
+
+
+def down_back(core, cots, down, after):
+    count, width = cots.shape
+    hidden = down.shape[0] // 2
+    tile = 512
+    return pl.pallas_call(
+        back_kernel,
         grid_spec=pltpu.PrefetchScalarGridSpec(
             num_scalar_prefetch=1,
             grid=(count // tile,),
-            in_specs=[rows, rows, weight, weight]
-            + [pl.BlockSpec((hidden, width), lambda i, core: (core[0], 0))]
+            in_specs=[
+                pl.BlockSpec((hidden, width), lambda i, core: (core[0], 0)),
+                pl.BlockSpec((tile, width), lambda i, core: (i, 0)),
+            ]
             + [pl.BlockSpec(memory_space=pl.ANY)] * len(after),
-            out_specs=[tall, tall, tall],
+            out_specs=pl.BlockSpec((hidden, tile), lambda i, core: (0, i)),
         ),
-        out_shape=[jax.ShapeDtypeStruct((hidden, count), bf16)] * 3,
-        cost_estimate=brief,
+        out_shape=jax.ShapeDtypeStruct((hidden, count), f32),
+        cost_estimate=cost(20),
         compiler_params=large,
-    )(core, tokens, cots, gate, up, down, *after)
-
-
-def product(left, right, added=(), after=()):
-    rows, depth = left.shape
-    cols = right.shape[1]
-    kind = bf16 if added else f32
-
-    def body(left_ref, right_ref, *rest):
-        total = jnp.dot(left_ref[...], right_ref[...], preferred_element_type=f32)
-        if added:
-            total = total + rest[0][...]
-        rest[-1][...] = total.astype(kind)
-
-    column = pl.BlockSpec((rows, 256), lambda n: (0, n))
-    return pl.pallas_call(
-        body,
-        grid=(cols // 256,),
-        in_specs=[
-            pl.BlockSpec((rows, depth), lambda n: (0, 0)),
-            pl.BlockSpec((depth, 256), lambda n: (0, n)),
-        ]
-        + [column] * len(added)
-        + [pl.BlockSpec(memory_space=pl.ANY)] * len(after),
-        out_specs=column,
-        out_shape=jax.ShapeDtypeStruct((rows, cols), kind),
-        cost_estimate=brief,
-        compiler_params=pltpu.CompilerParams(vmem_limit_bytes=48 * 1024 * 1024),
-    )(left, right, *added, *after)
+    )(core, down, cots, *after)
 
 
 def flip_kernel(core_ref, one_ref, two_ref, *rest):
@@ -657,47 +873,11 @@
             out_specs=[result, result],
         ),
         out_shape=[jax.ShapeDtypeStruct((hidden, width), bf16)] * 2,
-        cost_estimate=brief,
+        cost_estimate=cost(8),
     )(core.astype(jnp.int32).reshape((1,)), one, two, *after)
 
 
-def turn_kernel(core_ref, own_ref, other_ref, out_ref):
-    mine = pl.program_id(0) == core_ref[0]
-
-    @pl.when(mine)
-    def _():
-        out_ref[...] = own_ref[...].astype(f32).T
-
-    @pl.when(jnp.logical_not(mine))
-    def _():
-        out_ref[...] = other_ref[...].astype(f32).T
-
-
-def turned(own, other, core):
-    hidden, width = own.shape
-    tile = 256
-
-    def chosen(h, n, core):
-        return (0, jnp.where(h == core[0], n, 0))
-
-    def unchosen(h, n, core):
-        return (0, jnp.where(h == core[0], 0, n))
-
-    return pl.pallas_call(
-        turn_kernel,
-        grid_spec=pltpu.PrefetchScalarGridSpec(
-            num_scalar_prefetch=1,
-            grid=(2, width // tile),
-            in_specs=[pl.BlockSpec((hidden, tile), chosen), pl.BlockSpec((hidden, tile), unchosen)],
-            out_specs=pl.BlockSpec((tile, hidden), lambda h, n, core: (n, h)),
-        ),
-        out_shape=jax.ShapeDtypeStruct((width, 2 * hidden), f32),
-        cost_estimate=brief,
-        compiler_params=pltpu.CompilerParams(vmem_limit_bytes=48 * 1024 * 1024),
-    )(core.astype(jnp.int32).reshape((1,)), own, other)
-
-
-def run(body, outs, args, scratch=(), after=(), scalar=False):
+def run(body, outs, args, scratch=(), after=(), scalar=False, micros=1):
     vmem = pl.BlockSpec(memory_space=pltpu.VMEM)
     specs = [vmem] * len(args)
     if scalar:
@@ -713,13 +893,9 @@
         in_specs=specs + [pl.BlockSpec(memory_space=pl.ANY)] * len(after),
         out_specs=[vmem] * len(outs),
         scratch_shapes=scratch,
-        cost_estimate=brief,
+        cost_estimate=cost(micros),
         compiler_params=large,
     )(*args, *after)
-
-
-def take_heads(wide, count, size):
-    return jnp.stack([wide[h * size : (h + 1) * size, h * size : (h + 1) * size] for h in range(count)])
 
 
 def local(
@@ -752,6 +928,7 @@
     spot = jnp.zeros((1,), jnp.int32)
     if square:
         spot = spot + (2 * lax.axis_index("y") + lax.axis_index("x")).astype(jnp.int32)
+    where = jnp.concatenate([spot, core_id])
     heads, head = recur_weight.shape[0], recur_weight.shape[1]
     width = heads * head
     length = segment_ids.shape[1]
@@ -779,21 +956,20 @@
     soft = (-decay_scale * jax.nn.softplus(-decay_param))[None, :]
     taps = conv_weight.astype(f32)
 
-    cuts = (0, block * 3 // 4, block)
-    spans = list(zip(cuts[:-1], cuts[1:], strict=True))
     if line:
-        cots = [lax.all_gather(cotangent[a:b], ALL, axis=0, tiled=True) for a, b in spans]
+        cots = lax.all_gather(cotangent, ALL, axis=0, tiled=True)
 
     normed_pieces = gather_row(normed_own, square, (wide_high,) if square else ())
     token = shape((length, width), f32)
     token_low = shape((length, width), bf16)
     row_low = shape((length, features), bf16)
     row_sends = send_shapes(length, features, plain)
-    normed, branch_pre, stream_pre, gated, convolved, recur_gate, intake_gate, state, *sends = run(
+    half_row = shape((length, features // 2), bf16)
+    normed_mine, normed_theirs, branch_pre, stream_pre, gated, convolved, recur_gate, intake_gate, state, *sends = run(
         functools.partial(forward_kernel, count=len(normed_pieces), head=head, plain=plain),
-        [row_low, token, token, token_low, token, token, token, token, *row_sends],
+        [half_row, half_row, token, token, token_low, token, token, token, token, *row_sends],
         (
-            spot,
+            where,
             *normed_pieces,
             branch_weight,
             stream_weight,
@@ -806,24 +982,26 @@
             gate_bias,
             soft,
         ),
-        [pltpu.VMEM((length, width), bf16)] * 2,
+        [pltpu.VMEM((length, width), bf16)] * 2 + [pltpu.VMEM((length, features), bf16)],
         scalar=True,
-    )
-    cot_own = (cotangent[: block // 2], cotangent[block // 2 :])
+        micros=20,
+    )
+    own_cots = cotangent
     if square:
-        cot_own = held(cot_own, (normed_pieces[-1],))
-    cot_row = jnp.concatenate(gather_row(cot_own, square), axis=0)
-    activ_grad = lax.dot_general(cot_row, down_weight, contract_cols, preferred_element_type=f32)
-    addends = scatter_row(sends, square)
-
-    parts = [shape((b - a, features), bf16) for a, b in spans]
-    hidden, one, two, *token_parts = run(
-        functools.partial(second_norm_kernel, cuts=cuts),
-        [shape((block, features), f32), *halves, *parts],
+        (own_cots,) = held((cotangent,), normed_pieces)
+    own_cots = gather_blocks(own_cots, square)
+    activ_grad = row_back(own_cots, down_weight)
+    if square:
+        sends[:2] = held(sends[:2], own_cots[1:])
+    addends = scatter_row(sends, square, (activ_grad,) if square else ())
+
+    hidden, one, two, normed_two = run(
+        second_norm_kernel,
+        [shape((block, features), f32), *halves, shape((block, features), bf16)],
         (inputs, gain_two, *addends),
     )
     if line:
-        tokens = [lax.all_gather(part, ALL, axis=0, tiled=True) for part in token_parts]
+        tokens = lax.all_gather(normed_two, ALL, axis=0, tiled=True)
         gate_turned, up_turned = flipped(gate_weight, up_weight, core, (gated,))
     mlp_pieces = gather_row((one, two), square, (gate_turned,) if line else ())
     tile = min(512, hidden_units)
@@ -841,32 +1019,60 @@
         + [pl.BlockSpec(send.shape, lambda i: (0, 0)) for send in row_sends],
         out_shape=[row_low, low_units, *kept, *row_sends],
         scratch_shapes=[pltpu.VMEM((length, features), bf16), pltpu.VMEM((length, features), f32)],
-        cost_estimate=brief,
+        cost_estimate=cost(23),
         compiler_params=pltpu.CompilerParams(vmem_limit_bytes=56 * 1024 * 1024),
     )(*mlp_pieces, activ_grad, gate_weight, up_weight)
     kept, sends = sends[: len(kept)], sends[len(kept) :]
-    out_sends = run(functools.partial(down_kernel, plain=plain), row_sends, (activ, down_weight))
-    addends = scatter_row(sends, square, (out_sends[0],) if square else ())
+    beside = ()
+    if line:
+        grads = down_back(core_id, cots, down_weight, (sends[0],))
+        beside = (grads,)
+    addends = scatter_row(sends, square, beside)
 
     mlp_gain_part, resid_grad, one, two = run(
         functools.partial(norm_back_kernel, final=False),
         [shape((1, features), f32), shape((block, features), f32), *halves],
         (hidden, cotangent, gain_two, *addends),
     )
-    if line:
-        kept_a = mlp_rows(core_id, tokens[0], cots[0], gate_turned, up_turned, down_weight, (one,))
-    cot_pieces = gather_row((one, two), square)
-
-    branch_cot, branch_low, stream_low, wide_grad, sums, *sends = run(
-        functools.partial(backward_kernel, count=len(cot_pieces), head=head, plain=plain),
-        [row_low, token_low, token_low, shape((2, width, width), f32), shape((8, width), f32), *row_sends],
+    (out_part,) = run(
+        functools.partial(down_kernel, plain=plain), [row_low], (spot, activ, down_weight), after=(one,), scalar=True, micros=6
+    )
+    mlp_out = lax.psum_scatter(out_part, ("y", "x"), scatter_dimension=0, tiled=True)
+    cot_pieces = gather_row((one, two), square, (out_part,) if square else ())
+
+    cot_mine, cot_theirs, branch_low, state_grad = run(
+        functools.partial(branch_back_kernel, count=len(cot_pieces)),
+        [half_row, half_row, token_low, token],
+        (where, *cot_pieces, output_weight, branch_pre, state),
+        [pltpu.VMEM((length, features), bf16)],
+        scalar=True,
+        micros=6,
+    )
+    normed_other = sibling(normed_theirs)
+    output_half, branch_half = run(
+        pairs_kernel,
+        [shape((width, features // 2), bf16), shape((features // 2, width), bf16)],
         (
-            spot,
-            *cot_pieces,
-            output_weight,
+            gated,
+            sibling(gated),
+            cot_mine,
+            sibling(cot_theirs),
+            normed_mine,
+            normed_other,
+            branch_low,
+            sibling(branch_low),
+        ),
+    )
+    packed = shape((head + 8, width), f32)
+    stream_low, flat_mine, flat_theirs, norm_gain_part, one_part = run(
+        functools.partial(backward_kernel, head=head, plain=plain),
+        [token_low, packed, packed, shape((1, features), f32), row_low],
+        (
+            where,
+            state_grad,
+            branch_low,
             branch_weight,
             stream_weight,
-            branch_pre,
             stream_pre,
             joined,
             convolved,
@@ -876,79 +1082,102 @@
             taps,
             wide_high,
             soft,
+            normed_mine,
+            normed_theirs,
+            gain_one,
         ),
         [
-            pltpu.VMEM((length, width), f32),
+            pltpu.VMEM((2, width, width), f32),
+            pltpu.VMEM((8, width), f32),
             pltpu.VMEM((2, length, width), bf16),
             pltpu.VMEM((length, width), bf16),
             pltpu.VMEM((length + 8, width), f32),
         ],
+        after=(output_half, branch_half),
         scalar=True,
-    )
-    addends = scatter_row(sends, square)
-    norm_gain_part, inputs_grad = run(
+        micros=18,
+    )
+    gains = jnp.concatenate([norm_gain_part, mlp_gain_part], axis=1).reshape(8, -1)
+    if line:
+        moved = line_move([(output_half, 0)])
+        (output_sum,) = line_settle(moved, (stream_low,))
+        branch_half, stream_low, flat_mine, flat_theirs, one_part, gains = held(
+            (branch_half, stream_low, flat_mine, flat_theirs, one_part, gains), (output_sum,)
+        )
+        moved = line_move([(output_sum, 1), (branch_half, 0)])
+        gains_other = lax.ppermute(gains, "x", swap)
+    (stream_half,) = run(
+        pairs_kernel,
+        [shape((features // 2, width), bf16)],
+        (normed_mine, normed_other, stream_low, sibling(stream_low)),
+        micros=3,
+    )
+    one_grad = lax.psum_scatter(one_part, ("y", "x"), scatter_dimension=0, tiled=True)
+
+    gate_low = ()
+    if line:
+        small = [shape(gains.shape, f32)]
+        (gains,) = run(add_one_kernel, small, (gains, gains_other))
+        gains_other = lax.ppermute(gains, "y", swap)
+        (gains,) = run(add_one_kernel, small, (gains, gains_other), after=(stream_half,))
+        flat_other, gains_other = sibling(flat_theirs), sibling(gains)
+        rows_a = mlp_rows(tokens, grads, gate_turned, up_turned, 0, (), (stream_half, gains))
+        output_sum, branch_sum = line_settle(moved, rows_a[:1])
+        (flat,) = run(
+            sum_kernel,
+            [shape((packed.shape[0] + 8, width), bf16)],
+            (flat_mine, flat_other, gains, gains_other),
+            after=rows_a[:1],
+        )
+        moved = line_move([(output_sum, 2), (branch_sum, 1), (stream_half, 0), (flat, 0)])
+        activ_all, gate_all, up_all = mlp_rows(
+            tokens, grads, gate_turned, up_turned, 1, rows_a, (branch_sum, flat)
+        )
+        gate_low, gate_w_grad = product(gate_all, tokens, core_id, True)
+        output_sum, branch_sum, stream_sum, flat_sum = line_settle(moved, (gate_low,))
+        moved = line_move([(branch_sum, 2), (stream_sum, 1), (flat_sum, 1)])
+        (gate_sent,) = held((gate_low,), (stream_sum,))
+        up_low, up_w_grad = product(up_all, tokens, core_id, True, (branch_sum, stream_sum))
+        gate_low = (up_low,)
+    else:
+        (flat,) = run(sum_kernel, [packed], (flat_mine, sibling(flat_theirs)))
+
+    (inputs_grad,) = run(
         functools.partial(norm_back_kernel, final=True),
-        [shape((1, features), f32), shape((block, features), bf16)],
-        (inputs, resid_grad, gain_one, *addends),
-    )
-    if square:
-        out_sends = held(out_sends, (inputs_grad,))
-    addends = scatter_row(out_sends, square)
-    (block_out,) = run(add_kernel, [shape((block, features), bf16)], (hidden, *addends))
-
-    def both(value):
-        return jnp.concatenate([value, sibling(value)], axis=0)
-
-    def both_halves(value):
-        return jnp.concatenate(
-            [half_of(value, core, 1), sibling(half_of(value, 1 - core, 1))], axis=0
+        [shape((block, features), bf16)],
+        (inputs, resid_grad, gain_one, one_grad),
+        after=gate_low,
+    )
+    (block_out,) = run(
+        add_kernel, [shape((block, features), bf16)], (hidden, mlp_out), after=gate_low
+    )
+
+    def whole(own, axis, after=()):
+        return joined_halves(own, sibling(own), core_id, axis, after)
+
+    if line:
+        gate_w_grad = filled(gate_w_grad, sibling(gate_sent), core_id, True, (inputs_grad, block_out))
+        branch_sum, stream_sum, flat_sum = line_settle(moved, (gate_w_grad,))
+        moved = line_move([(stream_sum, 2), (flat_sum, 2)])
+        (up_sent,) = held((up_low,), (stream_sum,))
+        down_low, down_w_grad = product(activ_all, cots, core_id, False, (stream_sum, flat_sum))
+        up_w_grad = filled(up_w_grad, sibling(up_sent), core_id, True, (down_low,))
+        output_w_grad = whole(output_sum, 1, (up_w_grad,))
+        branch_w_grad = whole(branch_sum, 0, (output_w_grad,))
+        stream_sum, flat_sum = line_settle(moved, (branch_w_grad,))
+        (down_sent,) = held((down_low,), (stream_sum,))
+        stream_w_grad = whole(stream_sum, 0)
+        down_w_grad = filled(down_w_grad, sibling(down_sent), core_id, False, (flat_sum,))
+        gains = flat_sum[packed.shape[0] :, : features // 4].astype(f32)
+    else:
+        gains = lax.psum(gains, ALL)
+        output_sum, branch_sum, stream_sum, flat_sum = (
+            lax.psum(part, "z") for part in (output_half, branch_half, stream_half, flat)
         )
-
-    normed_half = both_halves(normed)
-    output_half = lax.dot_general(
-        both(gated), both_halves(branch_cot), contract_rows, preferred_element_type=f32
-    ).astype(bf16)
-    branch_half = lax.dot_general(
-        normed_half, both(branch_low), contract_rows, preferred_element_type=f32
-    ).astype(bf16)
-    stream_half = lax.dot_general(
-        normed_half, both(stream_low), contract_rows, preferred_element_type=f32
-    ).astype(bf16)
-    recur_part = take_heads(wide_grad[0], heads, head).astype(bf16)
-    intake_part = take_heads(wide_grad[1], heads, head).astype(bf16)
-    gate_half = (
-        jnp.where(core == 0, recur_part, intake_part).astype(f32)
-        + sibling(jnp.where(core == 0, intake_part, recur_part)).astype(f32)
-    ).astype(bf16)
-    gains = jnp.concatenate([norm_gain_part, mlp_gain_part], axis=1)
-    if square:
-        gains = gains + lax.ppermute(gains, "x", swap)
-        gains = gains + lax.ppermute(gains, "y", swap)
-    else:
-        gains = lax.psum(gains, ("y", "x"))
-    small = jnp.concatenate([sums.reshape(-1), gains.reshape(-1)]).reshape(-1, 128)
-    small = small + sibling(small)
-
-    if line:
-        first = [product(part, right, (), (stream_half,)) for part, right in zip(kept_a, (cots[0], tokens[0], tokens[0]), strict=True)]
-        kept_b = mlp_rows(
-            core_id, tokens[1], cots[1], gate_turned, up_turned, down_weight, (stream_half, *first)
-        )
-        down_half, gate_half_w, up_half_w = (
-            product(part, right, (before,))
-            for part, right, before in zip(kept_b, (cots[1], tokens[1], tokens[1]), first, strict=True)
-        )
-        groups = line_sums(
-            [(output_half,), (branch_half,), (stream_half,), (gate_half, small)],
-            ((first[0],), (first[2],), (kept_b[0],), (down_half,), (up_half_w,), ()),
-        )
-        (output_sum,), (branch_sum,), (stream_sum,), (gate_sum, small_sum) = groups
-        down_w_grad = join(down_half, sibling(down_half), core, 0)
-        gate_w_grad = turned(gate_half_w, sibling(gate_half_w), core)
-        up_w_grad = turned(up_half_w, sibling(up_half_w), core)
-    else:
-        output_sum, branch_sum, stream_sum, gate_sum, small_sum = (
-            lax.psum(part, "z") for part in (output_half, branch_half, stream_half, gate_half, small)
+        output_w_grad, branch_w_grad, stream_w_grad = (
+            whole(output_sum, 1),
+            whole(branch_sum, 0),
+            whole(stream_sum, 0),
         )
 
         def over_rows(left, right):
@@ -957,29 +1186,30 @@
 
         gate_w_grad = over_rows(mlp_in, kept[0])
         up_w_grad = over_rows(mlp_in, kept[1])
-        down_w_grad = over_rows(activ, cot_row)
-
-    def whole(own, axis):
-        return join(own, sibling(own), core, axis)
-
-    gate_other = sibling(gate_sum)
-    small_flat = small_sum.reshape(-1)
-    sums = small_flat[: 8 * width].reshape(8, width)
-    gains = small_flat[8 * width :].reshape(2, -1)
+        down_w_grad = over_rows(activ, jnp.concatenate(own_cots, axis=0))
+
+    sums = flat_sum[head : head + 8].astype(f32)
+    gates = flat_sum[:head]
+    gates_other = sibling(gates)
+
+    def heads_of(blocks):
+        return blocks.reshape(head, heads, head).transpose(1, 0, 2).astype(f32)
+
+    gains = gains.reshape(2, -1)
     return (
         block_out,
         inputs_grad,
         gains[0],
-        whole(branch_sum, 0),
-        whole(stream_sum, 0),
+        branch_w_grad,
+        stream_w_grad,
         sums[0:4],
         sums[4],
-        jnp.where(core == 0, gate_sum, gate_other).astype(f32),
+        heads_of(jnp.where(core == 0, gates, gates_other)),
         sums[5],
-        jnp.where(core == 0, gate_other, gate_sum).astype(f32),
+        heads_of(jnp.where(core == 0, gates_other, gates)),
         sums[6],
         sums[7] * decay_scale * jax.nn.sigmoid(-decay_param),
-        whole(output_sum, 1),
+        output_w_grad,
         gains[1],
         gate_w_grad,
         up_w_grad,

time: 658 us -> 549 us (0.83)
  other arithmetic: 56 us -> 3.21 us
  waiting for transfers between devices: 143 us -> 113 us
  starting transfers between devices: 94.3 us -> 68.9 us
  matrix products: 19.4 us -> 0 us
  local copies, waits for them, and re-layouts: 65.5 us -> 76 us
  Pallas kernels: 254 us -> 263 us
    ppermute x4 -> x2, waiting for transfers between devices: 35.4 us -> 0.01 us  [scatter_row(): got_x = lax.ppermute(to_x, 'x', swap)]
    convert_element_type x14 -> x3, other arithmetic: 35.4 us -> 0.96 us  [the longest x1 0.95 us: heads_of(): return blocks.reshape(head, heads, head).transpose(1, 0, 2).astype(f32)]
    pallas_call x8 -> x19, Pallas kernels: 55.4 us -> 80.8 us  [run(): pl.pallas_call(whole, out_shape=outs, in_specs=specs + [pl.BlockSpec(memo...]
    dot_general x4 -> x0, matrix products: 19.4 us -> none  [the longest x1 8.53 us: local(): lax.dot_general(cot_row, down_weight, contract_cols, preferred_element_ty...]
    ppermute x4 -> x2, waiting for transfers between devices: 17.5 us -> 0.01 us  [scatter_row(): got_y = lax.ppermute(to_y, 'y', swap)]
    unnamed x240 -> x218, local copies, waits for them, and re-layouts: 51 us -> 68.3 us
    select_n x10 -> x0, other arithmetic: 14.7 us -> none  [the longest x4 8.26 us: join(): first = jnp.where(core == 0, own, other)]
    ppermute x17, waiting for transfers between devices: 31.6 us -> 45.4 us  [the longest x12 34.7 us: line_move(): lax.ppermute(piece, 'z', pairs[stage])]
  transfers between devices with their start and end apart: 75 -> 61, of which waited for: 27 -> 21; matrix products, arithmetic and copies ran while one was open for 14% -> 3% of each run, Pallas kernels for 39% -> 47%
where the time goes in v3:
time: 549 us; the launch traced here: 539 us
  Pallas kernels  263 us (48%)
  waiting for transfers between devices  113 us (21%)
  local copies, waits for them, and re-layouts  76 us (14%)
  starting transfers between devices  68.9 us (13%)
  between operations  14.9 us (3%)
    pallas_call x19, Pallas kernels, run(): pl.pallas_call(whole, out_shape=outs, in_specs=specs + [pl.BlockSpec(memo...  80.8 us
    unnamed x218, local copies, waits for them, and re-layouts  68.3 us
    pallas_call x3, Pallas kernels, product(): pl.pallas_call(body, grid_spec=pltpu.PrefetchScalarGridSpec(num_scalar_pr...  58.4 us
    pallas_call x2, Pallas kernels, mlp_rows(): pl.pallas_call(rows_kernel, grid=(steps,), in_specs=[pl.BlockSpec((tile,...  38.8 us
    ppermute x12, waiting for transfers between devices, line_move(): lax.ppermute(piece, 'z', pairs[stage])  34.7 us
    ppermute x12, starting transfers between devices, line_move(): lax.ppermute(piece, 'z', pairs[stage])  33.5 us
    pallas_call x1, Pallas kernels, local(): pl.pallas_call(functools.partial(mlp_kernel, count=len(mlp_pieces), plain...  23.2 us
    ppermute x2, waiting for transfers between devices, scatter_row(): last_y = lax.ppermute(send_y, 'y', swap)  21.1 us
  transfers between devices with their start and end apart: 61, of which 21 were waited for; matrix products, arithmetic and copies ran while one was open for 3% of the time, Pallas kernels for 47%

profile of v3, /device:TPU:0, one launch (start us, length us, event | category | flops | bytes accessed | tf_op | source)
XLA Modules:
  0.0 538.9 jit_solution(9567091098625132787)
XLA Ops:
  10.0 3.0 collective-permute-start
  15.1 1.9 copy.71.refs_0_
  17.2 3.4 shard_map.306
  20.6 1.7 collective-permute-done.1.refs_1_
  25.2 5.4 %collective-permute-done.2.refs_3_ = bf16[64,2048]{1,0:T(8,128)(2,1)S(1)} collective-permute-done((bf16[64,2048]{1,0:T(8,128)(2,1)S(1)}, bf16[64,2048]{1,0:T(8,128)(2,1)S(1)}, u32[]{:S(2)}, u32[]{:S(2)}) %collective-permute-start.2) | collective-permute-done | bytes 262176 | tf_op jit(solution)/shard_map/ppermute | solution.py:55
  30.7 5.1 collective-permute-done.3.refs_4_
  39.0 1.7 collective-permute-start.6
  46.8 19.6 %shard_map.308 = (bf16[512,1024]{1,0:T(8,128)(2,1)S(1)}, bf16[512,1024]{1,0:T(8,128)(2,1)}, f32[512,640]{1,0:T(8,128)}, f32[512,640]{1,0:T(8,128)}, bf16[512,640...) custom-call(s32[2]{0:T(128)S(1)} %pad_add_fusion.1.refs_0_, ...), custom_call_target="tpu_custom_call" | custom-call | bytes 60000000 | tf_op jit(solution)/shard_map/pallas_call | solution.py:890
  70.3 8.1 %collective-permute-done.6.refs_2_.refs_1_ = bf16[128,2048]{1,0:T(8,128)(2,1)} collective-permute-done((bf16[128,2048]{1,0:T(8,128)(2,1)}, bf16[128,2048]{1,0:T(8,128)(2,1)}, u32[]{:S(2)}, u32[]{:S(2)}) %collective-permute-start.6) | collective-permute-done | bytes 524320 | tf_op jit(solution)/shard_map/ppermute | solution.py:68
  81.5 6.1 %shard_map.311.refs_2_.refs_8_ = f32[512,1536]{1,0:T(8,128)S(1)} custom-call(bf16[128,2048]{1,0:T(8,128)(2,1)S(1)} %copy-done.15, bf16[128,2048]{1,0:T(8,128)(2,1)} %collective-permute-done.6.refs_2_.refs_1_, bf16[128,2048]{1,0:T(8,128)(2,1)S(1)} %copy-done.44, bf16[128,2048]{1,0:T(8,128)(2,1)S(1)} %copy-done.42, bf16[1536,2048]{1,0:T(8,128)(2,1)} %refs_2_.1), custom_call_target="tpu_custom_call" | custom-call | bytes 18000000 | tf_op jit(solution)/shard_map/pallas_call | solution.py:726
  90.9 2.3 shard_map.313
  96.3 9.7 %collective-permute-done.11.refs_5_ = bf16[128,1024]{1,0:T(8,128)(2,1)S(1)} collective-permute-done((bf16[128,1024]{1,0:T(8,128)(2,1)}, bf16[128,1024]{1,0:T(8,128)(2,1)S(1)}, u32[]{:S(2)}, u32[]{:S(2)}) %collective-permute-start.11) | collective-permute-done | bytes 262176 | tf_op jit(solution)/shard_map/ppermute | solution.py:87
  106.0 2.5 collective-permute-done.12.refs_6_
  114.9 1.7 collective-permute-start.13
  117.0 8.2 %shard_map.315 = (bf16[768,2048]{1,0:T(8,128)(2,1)}, bf16[768,2048]{1,0:T(8,128)(2,1)}) custom-call(s32[1]{0:T(128)} %bitcast.2.core_ref, bf16[2048,1536]{1,0:T(8,128)(2,1)} %refs_9_.4, bf16[2048,1536]{1,0:T(8,128)(2,1)} %refs_10_.3, bf16[512,640]{1,0:T(8,128)(2,1)} %copy-done.33), custom_call_target="tpu_custom_call" | custom-call | bytes 24000000 | tf_op jit(solution)/shard_map/pallas_call | solution.py:867
  127.2 2.7 collective-permute-done.13.refs_0_
  132.7 7.4 %collective-permute-done.15.refs_2_ = bf16[64,2048]{1,0:T(8,128)(2,1)S(1)} collective-permute-done((bf16[64,2048]{1,0:T(8,128)(2,1)S(1)}, bf16[64,2048]{1,0:T(8,128)(2,1)S(1)}, u32[]{:S(2)}, u32[]{:S(2)}) %collective-permute-start.15) | collective-permute-done | bytes 262176 | tf_op jit(solution)/shard_map/ppermute | solution.py:55
  140.1 3.9 collective-permute-done.16.refs_3_
  145.4 23.2 %shard_map.317 = (bf16[512,2048]{1,0:T(8,128)(2,1)}, bf16[512,1536]{1,0:T(8,128)(2,1)}, bf16[256,1024]{1,0:T(8,128)(2,1)}, bf16[256,1024]{1,0:T(8,128)(2,1)}, bf...) custom-call(bf16[64,2048]{1,0:T(8,128)(2,1)} %copy-done.80, ...), custom_call_target="tpu_custom_call" | custom-call | bytes 69000000 | tf_op jit(solution)/shard_map/pallas_call | solution.py:1013
  171.8 19.8 %shard_map.318.refs_2_.grad_ref = f32[768,4096]{1,0:T(8,128)} custom-call(s32[1]{0:T(128)} %bitcast.2.core_ref, bf16[1536,2048]{1,0:T(8,128)(2,1)} %refs_2_.1, bf16[4096,2048]{1,0:T(8,128)(2,1)} %all-gather.3.cloned.1.call-done.cot_ref.right_ref, bf16[256,1024]{1,0:T(8,128)(2,1)S(1)} %copy-done.73), custom_call_target="tpu_custom_call" | custom-call | bytes 60000000 | tf_op jit(solution)/shard_map/pallas_call | solution.py:839
  193.2 2.3 shard_map.320
  197.3 11.4 %collective-permute-done.21.refs_6_ = bf16[128,1024]{1,0:T(8,128)(2,1)S(1)} collective-permute-done((bf16[128,1024]{1,0:T(8,128)(2,1)}, bf16[128,1024]{1,0:T(8,128)(2,1)S(1)}, u32[]{:S(2)}, u32[]{:S(2)}) %collective-permute-start.21) | collective-permute-done | bytes 262176 | tf_op jit(solution)/shard_map/ppermute | solution.py:87
  208.7 2.0 collective-permute-done.22.refs_7_
  214.0 1.7 shard_map.321
  219.0 1.7 collective-permute-start.27
  220.7 7.7 %shard_map.322.refs_2_ = bf16[512,2048]{1,0:T(8,128)(2,1)} custom-call(s32[1]{0:T(128)} %bitcast.1.refs_0_, bf16[512,1536]{1,0:T(8,128)(2,1)S(1)} %copy-done.47, bf16[1536,2048]{1,0:T(8,128)(2,1)} %refs_2_.1, bf16[64,2048]{1,0:T(8,128)(2,1)} %get-tuple-element.141.refs_3_.refs_1_), custom_call_target="tpu_custom_call" | custom-call | bytes 18000000 | tf_op jit(solution)/shard_map/pallas_call | solution.py:890
  232.0 4.5 collective-permute-done.28.refs_4_
  240.7 6.0 %shard_map.324 = (bf16[512,1024]{1,0:T(8,128)(2,1)S(1)}, bf16[512,1024]{1,0:T(8,128)(2,1)S(1)}, bf16[512,640]{1,0:T(8,128)(2,1)S(1)}, f32[512,640]{1,0:T(8,128)S(1)}) custom-call(s32[2]{0:T(128)S(1)} %pad_add_fusion.1.refs_0_, bf16[64,2048]{1,0:T(8,128)(2,1)} %get-tuple-element.141.refs_3_.refs_1_, bf16[64,2048]{1,0:T(8,128)(2,1)S(1)} %copy-done.72, ...), custom_call_target="tpu_custom_call" | custom-call | bytes 18000000 | tf_op jit(solution)/shard_map/pallas_call | solution.py:890
  248.4 3.1 collective-permute-done.24.refs_1_
  252.4 5.6 %shard_map.325 = (bf16[640,1024]{1,0:T(8,128)(2,1)}, bf16[1024,640]{1,0:T(8,128)(2,1)}) custom-call(bf16[512,640]{1,0:T(8,128)(2,1)S(1)} %copy-done.34, bf16[512,640]{1,0:T(8,128)(2,1)S(1)} %collective-permute-done.24.refs_1_, bf16[512,1024]{1,0:T(8,128)(2,1)S(1)} %get-tuple-element.151.refs_2_, bf16[512,1024]{1,0:T(8,128)(2,1)S(1)} %collective-permute-done.31.refs_3_, ...), custom_call_target="tpu_custom_call" | custom-call | bytes 3000000 | tf_op jit(solution)/shard_map/pallas_call | solution.py:890
  258.1 4.8 collective-permute-start.33
  262.9 19.3 %shard_map.326 = (bf16[512,640]{1,0:T(8,128)(2,1)S(1)}, f32[168,640]{1,0:T(8,128)S(1)}, f32[168,640]{1,0:T(8,128)S(1)}, f32[1,2048]{1,0:T(1,128)S(1)}, bf16[512,2048]{1,0:T(8,128)(2,1)}) custom-call(s32[2]{0:T(128)S(1)} %pad_add_fusion.1.refs_0_, f32[512,640]{1,0:T(8,128)} %copy-done.52, bf16[512,640]{1,0:T(8,128)(2,1)S(1)} %get-tuple-element.153.refs_6_.refs_2_, ...), custom_call_target="tpu_custom_call" | custom-call | bytes 54000000 | tf_op jit(solution)/shard_map/pallas_call | solution.py:890
  284.5 25.1 %collective-permute-done.33.refs_2_ = bf16[640,1024]{1,0:T(8,128)(2,1)} collective-permute-done((bf16[640,1024]{1,0:T(8,128)(2,1)}, bf16[640,1024]{1,0:T(8,128)(2,1)}, u32[]{:S(2)}, u32[]{:S(2)}) %collective-permute-start.33) | collective-permute-done | bytes 1310752 | tf_op jit(solution)/shard_map/ppermute | solution.py:98
  310.9 2.7 shard_map.327.refs_6_.refs_1_
  313.6 5.5 %collective-permute-start.38 = (bf16[1024,640]{1,0:T(8,128)(2,1)}, bf16[1024,640]{1,0:T(8,128)(2,1)}, u32[]{:S(2)}, u32[]{:S(2)}) collective-permute-start(bf16[1024,640]{1,0:T(8,128)(2,1)} %get-tuple-element.172.refs_2_), channel_id=1, source_target_pairs={{0,8},{24,16},{1,9},{25,17},{2,10},{26,18},{3,11},{27,19},{4,12},{... | collective-permute-start | bytes 3932168 | tf_op jit(solution)/shard_map/ppermute | solution.py:98
  319.0 1.8 collective-permute-start.37
  320.8 1.7 collective-permute-start.35
  322.5 2.6 collective-permute-done.35.refs_1_
  325.8 1.7 collective-permute-start.36
  331.2 2.9 shard_map.329.refs_2_.rest_0_.refs_3_
  334.1 4.1 collective-permute-start.43
  338.3 19.7 %shard_map.332 = (bf16[768,4096]{1,0:T(8,128)(2,1)}, bf16[768,4096]{1,0:T(8,128)(2,1)}, bf16[768,4096]{1,0:T(8,128)(2,1)}) custom-call(bf16[4096,2048]{1,0:T(8,128)(2,1)} %all-gather.5.cloned.1.call-done.token_ref.right_ref, f32[768,4096]{1,0:T(8,128)} %shard_map.318.refs_2_.grad_ref, bf16[768,2048]{1,0:T(8,128)(2,1)S(1)} %copy-done, ...), custom_call_target="tpu_custom_call" | custom-call | bytes 60000000 | tf_op jit(solution)/shard_map/pallas_call | solution.py:692
  358.0 3.9 shard_map.333
  363.3 1.8 collective-permute-start.42
  368.2 7.1 %collective-permute-start.44 = (bf16[176,640]{1,0:T(8,128)(2,1)S(1)}, bf16[176,640]{1,0:T(8,128)(2,1)S(1)}, u32[]{:S(2)}, u32[]{:S(2)}) collective-permute-start(bf16[176,640]{1,0:T(8,128)(2,1)S(1)} %shard_map.334.rest_4_.refs_4_), channel_id=1, source_target_pairs={{0,8},{24,16},{1,9},{25,17},{2,10},{26,18},{3,11},{27,19},{4,12},{... | collective-permute-start | bytes 675848 | tf_op jit(solution)/shard_map/ppermute | solution.py:98
  375.3 19.1 %shard_map.335 = (bf16[768,4096]{1,0:T(8,128)(2,1)}, bf16[768,4096]{1,0:T(8,128)(2,1)}, bf16[768,4096]{1,0:T(8,128)(2,1)}) custom-call(bf16[4096,2048]{1,0:T(8,128)(2,1)} %all-gather.5.cloned.1.call-done.token_ref.right_ref, f32[768,4096]{1,0:T(8,128)} %shard_map.318.refs_2_.grad_ref, ...), custom_call_target="tpu_custom_call", output_to_operand_aliasing={{0}: (4, {}), {1}: (5, {}), {2}: (6, {})} | custom-call | bytes 60000000 | tf_op jit(solution)/shard_map/pallas_call | solution.py:692
  394.3 19.6 %shard_map.336 = (bf16[768,2048]{1,0:T(8,128)(2,1)S(1)}, f32[2048,1536]{1,0:T(8,128)}) custom-call(s32[1]{0:T(128)} %bitcast.2.core_ref, bf16[768,4096]{1,0:T(8,128)(2,1)} %get-tuple-element.178.left_ref, bf16[4096,2048]{1,0:T(8,128)(2,1)} %all-gather.5.cloned.1.call-done.token_ref.right_ref), custom_call_target="tpu_custom_call" | custom-call | bytes 60000000 | tf_op jit(solution)/shard_map/pallas_call | solution.py:757
  415.6 5.1 shard_map.337
  423.1 1.8 collective-permute-start.46
  426.4 19.6 %shard_map.338 = (bf16[768,2048]{1,0:T(8,128)(2,1)S(1)}, f32[2048,1536]{1,0:T(8,128)}) custom-call(s32[1]{0:T(128)} %bitcast.2.core_ref, bf16[768,4096]{1,0:T(8,128)(2,1)} %get-tuple-element.176.left_ref, bf16[4096,2048]{1,0:T(8,128)(2,1)} %all-gather.5.cloned.1.call-done.token_ref.right_ref, bf16[1024,640]{1,0:T(8,128)(2,1)} %get-tuple-element.180.rest_0_.refs_1_, ...), custom_call_target="tpu_custom_call" | custom-call | bytes 60000000 | tf_op jit(solution)/shard_map/pallas_call | solution.py:757
  446.0 2.0 copy-done.30
  455.6 4.6 shard_map.342.refs_7_
  460.2 3.0 shard_map.343
  469.8 19.2 %shard_map.345 = (bf16[768,2048]{1,0:T(8,128)(2,1)S(1)}, f32[1536,2048]{1,0:T(8,128)}) custom-call(s32[1]{0:T(128)} %bitcast.2.core_ref, bf16[768,4096]{1,0:T(8,128)(2,1)} %get-tuple-element.192.left_ref, bf16[4096,2048]{1,0:T(8,128)(2,1)} %all-gather.3.cloned.1.call-done.cot_ref.right_ref, bf16[1024,640]{1,0:T(8,128)(2,1)S(1)} %copy-done.6, ...), custom_call_target="tpu_custom_call" | custom-call | bytes 60000000 | tf_op jit(solution)/shard_map/pallas_call | solution.py:757
  489.1 1.7 copy-done.3
  490.8 3.4 shard_map.346.rest_0_
  494.2 2.5 shard_map.347.rest_0_
  496.7 2.5 shard_map.348.refs_5_
  499.2 9.6 %collective-permute-done.50.refs_4_ = bf16[176,640]{1,0:T(8,128)(2,1)S(1)} collective-permute-done((bf16[176,640]{1,0:T(8,128)(2,1)S(1)}, bf16[176,640]{1,0:T(8,128)(2,1)S(1)}, u32[]{:S(2)}, u32[]{:S(2)}) %collective-permute-start.50) | collective-permute-done | bytes 225312 | tf_op jit(solution)/shard_map/ppermute | solution.py:98
  515.0 2.9 collective-permute-done.55
  520.3 2.3 reshape.79
  522.6 2.4 copy_bitcast_fusion
  525.0 2.5 shard_map.350
  527.6 4.3 shard_map.352
  (357 shorter events, 107.7 us)
Async XLA Ops:
  7.2 163.5 %all-gather.3.cloned.1.call-start = ((), (), s32[]{:S(2)}) async-start(), calls=%async_computation.2 | async-start | bytes 17301504 | tf_op jit(solution)/shard_map/all_gather | solution.py:960
  8.0 330.3 %all-gather.5.cloned.1.call-start = ((), (), s32[]{:S(2)}) async-start(), calls=%async_computation.4 | async-start | bytes 17301504 | tf_op jit(solution)/shard_map/all_gather | solution.py:1004
  10.0 10.6 %collective-permute-start = (bf16[64,2048]{1,0:T(8,128)(2,1)S(1)}, bf16[64,2048]{1,0:T(8,128)(2,1)S(1)}, u32[]{:S(2)}, u32[]{:S(2)}) collective-permute-start(bf16[64,2048]{1,0:T(8,128)(2,1)S(1)} %get-tuple-element.107.refs_1_), channel_id=1, source_target_pairs={{0,1},{1,0},{2,3},{3,2},{4,5},{5,4},{6,7},{7,6},{8,9},{9,8},{10,11... | collective-permute-start | bytes 786440 | tf_op jit(solution)/shard_map/ppermute | solution.py:52
  13.0 9.2 %collective-permute-start.1 = (bf16[64,2048]{1,0:T(8,128)(2,1)S(1)}, bf16[64,2048]{1,0:T(8,128)(2,1)S(1)}, u32[]{:S(2)}, u32[]{:S(2)}) collective-permute-start(bf16[64,2048]{1,0:T(8,128)(2,1)S(1)} %get-tuple-element.108.refs_5_), channel_id=1, source_target_pairs={{0,2},{2,0},{1,3},{3,1},{4,6},{6,4},{5,7},{7,5},{8,10},{10,8},{9,1... | collective-permute-start | bytes 786440 | tf_op jit(solution)/shard_map/ppermute | solution.py:53
  14.5 16.1 %collective-permute-start.2 = (bf16[64,2048]{1,0:T(8,128)(2,1)S(1)}, bf16[64,2048]{1,0:T(8,128)(2,1)S(1)}, u32[]{:S(2)}, u32[]{:S(2)}) collective-permute-start(bf16[64,2048]{1,0:T(8,128)(2,1)S(1)} %get-tuple-element.107.refs_1_), channel_id=1, source_target_pairs={{0,2},{2,0},{1,3},{3,1},{4,6},{6,4},{5,7},{7,5},{8,10},{10,8},{9,1... | collective-permute-start | bytes 786440 | tf_op jit(solution)/shard_map/ppermute | solution.py:55
  15.0 15.6 %collective-permute-start.4 = (bf16[64,2048]{1,0:T(8,128)(2,1)S(1)}, bf16[64,2048]{1,0:T(8,128)(2,1)S(1)}, u32[]{:S(2)}, u32[]{:S(2)}) collective-permute-start(bf16[64,2048]{1,0:T(8,128)(2,1)S(1)} %get-tuple-element.108.refs_5_), channel_id=1, source_target_pairs={{0,1},{1,0},{2,3},{3,2},{4,5},{5,4},{6,7},{7,6},{8,9},{9,8},{10,11... | collective-permute-start | bytes 786440 | tf_op jit(solution)/shard_map/ppermute | solution.py:54
  23.0 12.8 %collective-permute-start.3 = (bf16[64,2048]{1,0:T(8,128)(2,1)}, bf16[64,2048]{1,0:T(8,128)(2,1)S(1)}, u32[]{:S(2)}, u32[]{:S(2)}) collective-permute-start(bf16[64,2048]{1,0:T(8,128)(2,1)} %get-tuple-element.110.refs_2_), channel_id=1, source_target_pairs={{0,2},{2,0},{1,3},{3,1},{4,6},{6,4},{5,7},{7,5},{8,10},{10,8},{9,1... | collective-permute-start | bytes 786440 | tf_op jit(solution)/shard_map/ppermute | solution.py:58
  24.5 11.2 %collective-permute-start.5 = (bf16[64,2048]{1,0:T(8,128)(2,1)}, bf16[64,2048]{1,0:T(8,128)(2,1)S(1)}, u32[]{:S(2)}, u32[]{:S(2)}) collective-permute-start(bf16[64,2048]{1,0:T(8,128)(2,1)} %get-tuple-element.111.refs_7_), channel_id=1, source_target_pairs={{0,1},{1,0},{2,3},{3,2},{4,5},{5,4},{6,7},{7,6},{8,9},{9,8},{10,11... | collective-permute-start | bytes 786440 | tf_op jit(solution)/shard_map/ppermute | solution.py:59
  37.2 33.1 %collective-permute-start.8 = (bf16[128,2048]{1,0:T(8,128)(2,1)}, bf16[128,2048]{1,0:T(8,128)(2,1)S(1)}, u32[]{:S(2)}, u32[]{:S(2)}) collective-permute-start(bf16[128,2048]{1,0:T(8,128)(2,1)} %shard_map.309.refs_0_), channel_id=1, source_target_pairs={{0,3},{3,0},{1,2},{2,1},{4,7},{7,4},{5,6},{6,5},{8,11},{11,8},{9,1... | collective-permute-start | bytes 1572872 | tf_op jit(solution)/shard_map/ppermute | solution.py:70
  38.7 31.6 %collective-permute-start.7 = (bf16[128,2048]{1,0:T(8,128)(2,1)}, bf16[128,2048]{1,0:T(8,128)(2,1)S(1)}, u32[]{:S(2)}, u32[]{:S(2)}) collective-permute-start(bf16[128,2048]{1,0:T(8,128)(2,1)} %shard_map.309.refs_0_), channel_id=1, source_target_pairs={{0,2},{2,0},{1,3},{3,1},{4,6},{6,4},{5,7},{7,5},{8,10},{10,8},{9,1... | collective-permute-start | bytes 1572872 | tf_op jit(solution)/shard_map/ppermute | solution.py:69
  39.0 39.5 %collective-permute-start.6 = (bf16[128,2048]{1,0:T(8,128)(2,1)}, bf16[128,2048]{1,0:T(8,128)(2,1)}, u32[]{:S(2)}, u32[]{:S(2)}) collective-permute-start(bf16[128,2048]{1,0:T(8,128)(2,1)} %shard_map.309.refs_0_), channel_id=1, source_target_pairs={{0,1},{1,0},{2,3},{3,2},{4,5},{5,4},{6,7},{7,6},{8,9},{9,8},{10,11... | collective-permute-start | bytes 1572872 | tf_op jit(solution)/shard_map/ppermute | solution.py:68
  70.3 192.6 %copy-start.8 = (bf16[512,1024]{1,0:T(8,128)(2,1)}, bf16[512,1024]{1,0:T(8,128)(2,1)S(1)}, u32[]{:S(2)}) copy-start(bf16[512,1024]{1,0:T(8,128)(2,1)S(1)} %get-tuple-element.144.refs_4_.refs_14_.refs_0_) | copy-start | bytes 3145732
  78.5 10.8 %collective-permute-start.9 = (bf16[256,1024]{1,0:T(8,128)(2,1)}, bf16[256,1024]{1,0:T(8,128)(2,1)S(1)}, u32[]{:S(2)}, u32[]{:S(2)}) collective-permute-start(bf16[256,1024]{1,0:T(8,128)(2,1)} %get-tuple-element.116), channel_id=1, source_target_pairs={{0,1},{1,0},{2,3},{3,2},{4,5},{5,4},{6,7},{7,6},{8,9},{9,8},{10,11... | collective-permute-start | bytes 1572872 | tf_op jit(solution)/shard_map/ppermute | solution.py:78
  79.0 10.3 %collective-permute-start.10 = (bf16[256,1024]{1,0:T(8,128)(2,1)}, bf16[256,1024]{1,0:T(8,128)(2,1)S(1)}, u32[]{:S(2)}, u32[]{:S(2)}) collective-permute-start(bf16[256,1024]{1,0:T(8,128)(2,1)} %get-tuple-element.117), channel_id=1, source_target_pairs={{0,2},{2,0},{1,3},{3,1},{4,6},{6,4},{5,7},{7,5},{8,10},{10,8},{9,1... | collective-permute-start | bytes 1572872 | tf_op jit(solution)/shard_map/ppermute | solution.py:79
  93.1 12.9 %collective-permute-start.11 = (bf16[128,1024]{1,0:T(8,128)(2,1)}, bf16[128,1024]{1,0:T(8,128)(2,1)S(1)}, u32[]{:S(2)}, u32[]{:S(2)}) collective-permute-start(bf16[128,1024]{1,0:T(8,128)(2,1)} %get-tuple-element.122), channel_id=1, source_target_pairs={{0,2},{2,0},{1,3},{3,1},{4,6},{6,4},{5,7},{7,5},{8,10},{10,8},{9,1... | collective-permute-start | bytes 786440 | tf_op jit(solution)/shard_map/ppermute | solution.py:87
  94.8 13.7 %collective-permute-start.12 = (bf16[128,1024]{1,0:T(8,128)(2,1)}, bf16[128,1024]{1,0:T(8,128)(2,1)S(1)}, u32[]{:S(2)}, u32[]{:S(2)}) collective-permute-start(bf16[128,1024]{1,0:T(8,128)(2,1)} %get-tuple-element.123), channel_id=1, source_target_pairs={{0,1},{1,0},{2,3},{3,2},{4,5},{5,4},{6,7},{7,6},{8,9},{9,8},{10,11... | collective-permute-start | bytes 786440 | tf_op jit(solution)/shard_map/ppermute | solution.py:88
  114.3 331.7 %reduce-scatter.3.cloned.1.call-start = ((), (), s32[]{:S(2)}) async-start(), calls=%async_computation.3 | async-start | bytes 2621440 | tf_op jit(solution)/shard_map/reduce_scatter | solution.py:1040
  114.9 15.0 %collective-permute-start.13 = (bf16[64,2048]{1,0:T(8,128)(2,1)}, bf16[64,2048]{1,0:T(8,128)(2,1)S(1)}, u32[]{:S(2)}, u32[]{:S(2)}) collective-permute-start(bf16[64,2048]{1,0:T(8,128)(2,1)} %copy-done.80), channel_id=1, source_target_pairs={{0,1},{1,0},{2,3},{3,2},{4,5},{5,4},{6,7},{7,6},{8,9},{9,8},{10,11... | collective-permute-start | bytes 786440 | tf_op jit(solution)/shard_map/ppermute | solution.py:52
  116.5 15.0 %collective-permute-start.14 = (bf16[64,2048]{1,0:T(8,128)(2,1)}, bf16[64,2048]{1,0:T(8,128)(2,1)S(1)}, u32[]{:S(2)}, u32[]{:S(2)}) collective-permute-start(bf16[64,2048]{1,0:T(8,128)(2,1)} %copy-done.82), channel_id=1, source_target_pairs={{0,2},{2,0},{1,3},{3,1},{4,6},{6,4},{5,7},{7,5},{8,10},{10,8},{9,1... | collective-permute-start | bytes 786440 | tf_op jit(solution)/shard_map/ppermute | solution.py:53
  125.2 14.9 %collective-permute-start.15 = (bf16[64,2048]{1,0:T(8,128)(2,1)S(1)}, bf16[64,2048]{1,0:T(8,128)(2,1)S(1)}, u32[]{:S(2)}, u32[]{:S(2)}) collective-permute-start(bf16[64,2048]{1,0:T(8,128)(2,1)S(1)} %copy-done.81), channel_id=1, source_target_pairs={{0,2},{2,0},{1,3},{3,1},{4,6},{6,4},{5,7},{7,5},{8,10},{10,8},{9,1... | collective-permute-start | bytes 786440 | tf_op jit(solution)/shard_map/ppermute | solution.py:55
  126.8 13.3 %collective-permute-start.17 = (bf16[64,2048]{1,0:T(8,128)(2,1)S(1)}, bf16[64,2048]{1,0:T(8,128)(2,1)S(1)}, u32[]{:S(2)}, u32[]{:S(2)}) collective-permute-start(bf16[64,2048]{1,0:T(8,128)(2,1)S(1)} %copy-done.83), channel_id=1, source_target_pairs={{0,1},{1,0},{2,3},{3,2},{4,5},{5,4},{6,7},{7,6},{8,9},{9,8},{10,11... | collective-permute-start | bytes 786440 | tf_op jit(solution)/shard_map/ppermute | solution.py:54
  132.2 11.8 %collective-permute-start.16 = (bf16[64,2048]{1,0:T(8,128)(2,1)}, bf16[64,2048]{1,0:T(8,128)(2,1)S(1)}, u32[]{:S(2)}, u32[]{:S(2)}) collective-permute-start(bf16[64,2048]{1,0:T(8,128)(2,1)} %get-tuple-element.129.refs_1_), channel_id=1, source_target_pairs={{0,2},{2,0},{1,3},{3,1},{4,6},{6,4},{5,7},{7,5},{8,10},{10,8},{9,1... | collective-permute-start | bytes 786440 | tf_op jit(solution)/shard_map/ppermute | solution.py:58
  132.6 11.5 %collective-permute-start.18 = (bf16[64,2048]{1,0:T(8,128)(2,1)}, bf16[64,2048]{1,0:T(8,128)(2,1)S(1)}, u32[]{:S(2)}, u32[]{:S(2)}) collective-permute-start(bf16[64,2048]{1,0:T(8,128)(2,1)} %get-tuple-element.130.refs_6_), channel_id=1, source_target_pairs={{0,1},{1,0},{2,3},{3,2},{4,5},{5,4},{6,7},{7,6},{8,9},{9,8},{10,11... | collective-permute-start | bytes 786440 | tf_op jit(solution)/shard_map/ppermute | solution.py:59
  168.6 23.0 %collective-permute-start.20 = (bf16[256,1024]{1,0:T(8,128)(2,1)}, bf16[256,1024]{1,0:T(8,128)(2,1)S(1)}, u32[]{:S(2)}, u32[]{:S(2)}) collective-permute-start(bf16[256,1024]{1,0:T(8,128)(2,1)} %get-tuple-element.134), channel_id=1, source_target_pairs={{0,2},{2,0},{1,3},{3,1},{4,6},{6,4},{5,7},{7,5},{8,10},{10,8},{9,1... | collective-permute-start | bytes 1572872 | tf_op jit(solution)/shard_map/ppermute | solution.py:79
  169.6 22.0 %collective-permute-start.19 = (bf16[256,1024]{1,0:T(8,128)(2,1)}, bf16[256,1024]{1,0:T(8,128)(2,1)S(1)}, u32[]{:S(2)}, u32[]{:S(2)}) collective-permute-start(bf16[256,1024]{1,0:T(8,128)(2,1)} %get-tuple-element.133.rest_0_), channel_id=1, source_target_pairs={{0,1},{1,0},{2,3},{3,2},{4,5},{5,4},{6,7},{7,6},{8,9},{9,8},{10,11... | collective-permute-start | bytes 1572872 | tf_op jit(solution)/shard_map/ppermute | solution.py:78
  195.5 13.2 %collective-permute-start.21 = (bf16[128,1024]{1,0:T(8,128)(2,1)}, bf16[128,1024]{1,0:T(8,128)(2,1)S(1)}, u32[]{:S(2)}, u32[]{:S(2)}) collective-permute-start(bf16[128,1024]{1,0:T(8,128)(2,1)} %get-tuple-element.139), channel_id=1, source_target_pairs={{0,2},{2,0},{1,3},{3,1},{4,6},{6,4},{5,7},{7,5},{8,10},{10,8},{9,1... | collective-permute-start | bytes 786440 | tf_op jit(solution)/shard_map/ppermute | solution.py:87
  196.9 13.8 %collective-permute-start.22 = (bf16[128,1024]{1,0:T(8,128)(2,1)}, bf16[128,1024]{1,0:T(8,128)(2,1)S(1)}, u32[]{:S(2)}, u32[]{:S(2)}) collective-permute-start(bf16[128,1024]{1,0:T(8,128)(2,1)} %get-tuple-element.140), channel_id=1, source_target_pairs={{0,1},{1,0},{2,3},{3,2},{4,5},{5,4},{6,7},{7,6},{8,9},{9,8},{10,11... | collective-permute-start | bytes 786440 | tf_op jit(solution)/shard_map/ppermute | solution.py:88
  216.7 11.7 %collective-permute-start.26 = (bf16[64,2048]{1,0:T(8,128)(2,1)}, bf16[64,2048]{1,0:T(8,128)(2,1)S(1)}, u32[]{:S(2)}, u32[]{:S(2)}) collective-permute-start(bf16[64,2048]{1,0:T(8,128)(2,1)} %get-tuple-element.146.refs_5_), channel_id=1, source_target_pairs={{0,2},{2,0},{1,3},{3,1},{4,6},{6,4},{5,7},{7,5},{8,10},{10,8},{9,1... | collective-permute-start | bytes 786440 | tf_op jit(solution)/shard_map/ppermute | solution.py:53
  217.0 11.4 %collective-permute-start.25 = (bf16[64,2048]{1,0:T(8,128)(2,1)}, bf16[64,2048]{1,0:T(8,128)(2,1)S(1)}, u32[]{:S(2)}, u32[]{:S(2)}) collective-permute-start(bf16[64,2048]{1,0:T(8,128)(2,1)} %get-tuple-element.141.refs_3_.refs_1_), channel_id=1, source_target_pairs={{0,1},{1,0},{2,3},{3,2},{4,5},{5,4},{6,7},{7,6},{8,9},{9,8},{10,11... | collective-permute-start | bytes 786440 | tf_op jit(solution)/shard_map/ppermute | solution.py:52
  217.8 13.4 %collective-permute-start.29 = (bf16[64,2048]{1,0:T(8,128)(2,1)}, bf16[64,2048]{1,0:T(8,128)(2,1)S(1)}, u32[]{:S(2)}, u32[]{:S(2)}) collective-permute-start(bf16[64,2048]{1,0:T(8,128)(2,1)} %get-tuple-element.146.refs_5_), channel_id=1, source_target_pairs={{0,1},{1,0},{2,3},{3,2},{4,5},{5,4},{6,7},{7,6},{8,9},{9,8},{10,11... | collective-permute-start | bytes 786440 | tf_op jit(solution)/shard_map/ppermute | solution.py:54
  219.0 12.2 %collective-permute-start.27 = (bf16[64,2048]{1,0:T(8,128)(2,1)}, bf16[64,2048]{1,0:T(8,128)(2,1)S(1)}, u32[]{:S(2)}, u32[]{:S(2)}) collective-permute-start(bf16[64,2048]{1,0:T(8,128)(2,1)} %get-tuple-element.141.refs_3_.refs_1_), channel_id=1, source_target_pairs={{0,2},{2,0},{1,3},{3,1},{4,6},{6,4},{5,7},{7,5},{8,10},{10,8},{9,1... | collective-permute-start | bytes 786440 | tf_op jit(solution)/shard_map/ppermute | solution.py:55
  229.8 6.6 %collective-permute-start.28 = (bf16[64,2048]{1,0:T(8,128)(2,1)}, bf16[64,2048]{1,0:T(8,128)(2,1)S(1)}, u32[]{:S(2)}, u32[]{:S(2)}) collective-permute-start(bf16[64,2048]{1,0:T(8,128)(2,1)} %get-tuple-element.147.refs_2_), channel_id=1, source_target_pairs={{0,2},{2,0},{1,3},{3,1},{4,6},{6,4},{5,7},{7,5},{8,10},{10,8},{9,1... | collective-permute-start | bytes 786440 | tf_op jit(solution)/shard_map/ppermute | solution.py:58
  230.0 7.1 %collective-permute-start.30 = (bf16[64,2048]{1,0:T(8,128)(2,1)}, bf16[64,2048]{1,0:T(8,128)(2,1)S(1)}, u32[]{:S(2)}, u32[]{:S(2)}) collective-permute-start(bf16[64,2048]{1,0:T(8,128)(2,1)} %get-tuple-element.148.refs_7_), channel_id=1, source_target_pairs={{0,1},{1,0},{2,3},{3,2},{4,5},{5,4},{6,7},{7,6},{8,9},{9,8},{10,11... | collective-permute-start | bytes 786440 | tf_op jit(solution)/shard_map/ppermute | solution.py:59
  230.9 219.0 %reduce-scatter.5.cloned.1.call-start = ((), (), s32[]{:S(2)}) async-start(), calls=%async_computation.5 | async-start | bytes 2621440 | tf_op jit(solution)/shard_map/reduce_scatter | solution.py:1115
  231.2 20.3 %collective-permute-start.23 = (bf16[512,1024]{1,0:T(8,128)(2,1)}, bf16[512,1024]{1,0:T(8,128)(2,1)S(1)}, u32[]{:S(2)}, u32[]{:S(2)}) collective-permute-start(bf16[512,1024]{1,0:T(8,128)(2,1)} %get-tuple-element.145.refs_15_), channel_id=1, source_target_pairs={{0,4},{4,0},{1,5},{5,1},{2,6},{6,2},{3,7},{7,3},{8,12},{12,8},{9,1... | collective-permute-start | bytes 3145736 | tf_op jit(solution)/shard_map/ppermute | solution.py:93
  247.8 4.5 collective-permute-start.31
  247.8 3.6 collective-permute-start.24
  248.4 4.0 collective-permute-start.32
  258.1 51.5 %collective-permute-start.33 = (bf16[640,1024]{1,0:T(8,128)(2,1)}, bf16[640,1024]{1,0:T(8,128)(2,1)}, u32[]{:S(2)}, u32[]{:S(2)}) collective-permute-start(bf16[640,1024]{1,0:T(8,128)(2,1)} %get-tuple-element.160.refs_17_.refs_1_), channel_id=1, source_target_pairs={{0,8},{24,16},{1,9},{25,17},{2,10},{26,18},{3,11},{27,19},{4,12},{... | collective-permute-start | bytes 3932168 | tf_op jit(solution)/shard_map/ppermute | solution.py:98
  283.7 29.8 %copy-start.10 = (bf16[512,640]{1,0:T(8,128)(2,1)}, bf16[512,640]{1,0:T(8,128)(2,1)S(1)}, u32[]{:S(2)}) copy-start(bf16[512,640]{1,0:T(8,128)(2,1)S(1)} %get-tuple-element.161.refs_3_.refs_1_) | copy-start | bytes 1966084
  313.6 44.5 %collective-permute-start.38 = (bf16[1024,640]{1,0:T(8,128)(2,1)}, bf16[1024,640]{1,0:T(8,128)(2,1)}, u32[]{:S(2)}, u32[]{:S(2)}) collective-permute-start(bf16[1024,640]{1,0:T(8,128)(2,1)} %get-tuple-element.172.refs_2_), channel_id=1, source_target_pairs={{0,8},{24,16},{1,9},{25,17},{2,10},{26,18},{3,11},{27,19},{4,12},{... | collective-permute-start | bytes 3932168 | tf_op jit(solution)/shard_map/ppermute | solution.py:98
  319.0 39.0 %collective-permute-start.37 = (bf16[640,1024]{1,0:T(8,128)(2,1)}, bf16[640,1024]{1,0:T(8,128)(2,1)}, u32[]{:S(2)}, u32[]{:S(2)}) collective-permute-start(bf16[640,1024]{1,0:T(8,128)(2,1)} %shard_map.327.refs_6_.refs_1_), channel_id=1, source_target_pairs={{8,16},{16,8},{9,17},{17,9},{10,18},{18,10},{11,19},{19,11},{12,20... | collective-permute-start | bytes 3932168 | tf_op jit(solution)/shard_map/ppermute | solution.py:98
  320.8 6.7 %collective-permute-start.34 = (bf16[512,640]{1,0:T(8,128)(2,1)}, bf16[512,640]{1,0:T(8,128)(2,1)S(1)}, u32[]{:S(2)}, u32[]{:S(2)}) collective-permute-start(bf16[512,640]{1,0:T(8,128)(2,1)} %get-tuple-element.167.refs_2_), channel_id=1, source_target_pairs={{0,4},{4,0},{1,5},{5,1},{2,6},{6,2},{3,7},{7,3},{8,12},{12,8},{9,1... | collective-permute-start | bytes 1966088 | tf_op jit(solution)/shard_map/ppermute | solution.py:93
  320.8 4.3 collective-permute-start.35
  325.8 12.4 %collective-permute-start.36 = (f32[8,512]{1,0:T(8,128)S(1)}, f32[8,512]{1,0:T(8,128)S(1)}, u32[]{:S(2)}, u32[]{:S(2)}) collective-permute-start(f32[8,512]{1,0:T(8,128)S(1)} %shard_map.330.refs_0_), channel_id=1, source_target_pairs={{0,2},{2,0},{1,3},{3,1},{4,6},{6,4},{5,7},{7,5},{8,10},{10,8},{9,1... | collective-permute-start | bytes 49160 | tf_op jit(solution)/shard_map/ppermute | solution.py:1121
  334.1 81.5 %collective-permute-start.43 = (bf16[1024,640]{1,0:T(8,128)(2,1)}, bf16[1024,640]{1,0:T(8,128)(2,1)}, u32[]{:S(2)}, u32[]{:S(2)}) collective-permute-start(bf16[1024,640]{1,0:T(8,128)(2,1)} %shard_map.329.refs_2_.rest_0_.refs_3_), channel_id=1, source_target_pairs={{0,8},{24,16},{1,9},{25,17},{2,10},{26,18},{3,11},{27,19},{4,12},{... | collective-permute-start | bytes 3932168 | tf_op jit(solution)/shard_map/ppermute | solution.py:98
  338.3 19.8 %copy-start.7 = (bf16[1024,640]{1,0:T(8,128)(2,1)S(1)}, bf16[1024,640]{1,0:T(8,128)(2,1)}, u32[]{:S(2)}) copy-start(bf16[1024,640]{1,0:T(8,128)(2,1)} %get-tuple-element.172.refs_2_) | copy-start | bytes 3932164
  362.0 53.6 %collective-permute-start.41 = (bf16[640,1024]{1,0:T(8,128)(2,1)}, bf16[640,1024]{1,0:T(8,128)(2,1)}, u32[]{:S(2)}, u32[]{:S(2)}) collective-permute-start(bf16[640,1024]{1,0:T(8,128)(2,1)} %get-tuple-element.177.refs_1_), channel_id=1, source_target_pairs={{8,0},{16,24},{9,1},{17,25},{10,2},{18,26},{11,3},{19,27},{12,4},{... | collective-permute-start | bytes 3932168 | tf_op jit(solution)/shard_map/ppermute | solution.py:98
  363.3 52.3 %collective-permute-start.42 = (bf16[1024,640]{1,0:T(8,128)(2,1)}, bf16[1024,640]{1,0:T(8,128)(2,1)}, u32[]{:S(2)}, u32[]{:S(2)}) collective-permute-start(bf16[1024,640]{1,0:T(8,128)(2,1)} %get-tuple-element.173.rest_3_.refs_2_), channel_id=1, source_target_pairs={{8,16},{16,8},{9,17},{17,9},{10,18},{18,10},{11,19},{19,11},{12,20... | collective-permute-start | bytes 3932168 | tf_op jit(solution)/shard_map/ppermute | solution.py:98
  365.0 2.1 collective-permute-start.39
  365.1 2.0 collective-permute-start.40
  368.2 47.4 %collective-permute-start.44 = (bf16[176,640]{1,0:T(8,128)(2,1)S(1)}, bf16[176,640]{1,0:T(8,128)(2,1)S(1)}, u32[]{:S(2)}, u32[]{:S(2)}) collective-permute-start(bf16[176,640]{1,0:T(8,128)(2,1)S(1)} %shard_map.334.rest_4_.refs_4_), channel_id=1, source_target_pairs={{0,8},{24,16},{1,9},{25,17},{2,10},{26,18},{3,11},{27,19},{4,12},{... | collective-permute-start | bytes 675848 | tf_op jit(solution)/shard_map/ppermute | solution.py:98
  421.8 32.8 %collective-permute-start.48 = (bf16[768,2048]{1,0:T(8,128)(2,1)}, bf16[768,2048]{1,0:T(8,128)(2,1)}, u32[]{:S(2)}, u32[]{:S(2)}) collective-permute-start(bf16[768,2048]{1,0:T(8,128)(2,1)} %shard_map.341), channel_id=1, source_target_pairs={{0,4},{4,0},{1,5},{5,1},{2,6},{6,2},{3,7},{7,3},{8,12},{12,8},{9,1... | collective-permute-start | bytes 9437192 | tf_op jit(solution)/shard_map/ppermute | solution.py:93
  421.8 38.4 %collective-permute-start.45 = (bf16[1024,640]{1,0:T(8,128)(2,1)}, bf16[1024,640]{1,0:T(8,128)(2,1)}, u32[]{:S(2)}, u32[]{:S(2)}) collective-permute-start(bf16[1024,640]{1,0:T(8,128)(2,1)} %get-tuple-element.180.rest_0_.refs_1_), channel_id=1, source_target_pairs={{8,0},{16,24},{9,1},{17,25},{10,2},{18,26},{11,3},{19,27},{12,4},{... | collective-permute-start | bytes 3932168 | tf_op jit(solution)/shard_map/ppermute | solution.py:98
  423.1 37.1 %collective-permute-start.46 = (bf16[1024,640]{1,0:T(8,128)(2,1)}, bf16[1024,640]{1,0:T(8,128)(2,1)}, u32[]{:S(2)}, u32[]{:S(2)}) collective-permute-start(bf16[1024,640]{1,0:T(8,128)(2,1)} %get-tuple-element.181.rest_1_.refs_1_.refs_2_), channel_id=1, source_target_pairs={{8,16},{16,8},{9,17},{17,9},{10,18},{18,10},{11,19},{19,11},{12,20... | collective-permute-start | bytes 3932168 | tf_op jit(solution)/shard_map/ppermute | solution.py:98
  424.8 35.3 %collective-permute-start.47 = (bf16[176,640]{1,0:T(8,128)(2,1)S(1)}, bf16[176,640]{1,0:T(8,128)(2,1)}, u32[]{:S(2)}, u32[]{:S(2)}) collective-permute-start(bf16[176,640]{1,0:T(8,128)(2,1)S(1)} %get-tuple-element.185.refs_3_), channel_id=1, source_target_pairs={{8,16},{16,8},{9,17},{17,9},{10,18},{18,10},{11,19},{19,11},{12,20... | collective-permute-start | bytes 675848 | tf_op jit(solution)/shard_map/ppermute | solution.py:98
  465.4 25.3 %collective-permute-start.53 = (bf16[768,2048]{1,0:T(8,128)(2,1)}, bf16[768,2048]{1,0:T(8,128)(2,1)S(1)}, u32[]{:S(2)}, u32[]{:S(2)}) collective-permute-start(bf16[768,2048]{1,0:T(8,128)(2,1)} %shard_map.344), channel_id=1, source_target_pairs={{0,4},{4,0},{1,5},{5,1},{2,6},{6,2},{3,7},{7,3},{8,12},{12,8},{9,1... | collective-permute-start | bytes 9437192 | tf_op jit(solution)/shard_map/ppermute | solution.py:93
  466.7 27.4 %collective-permute-start.52 = (bf16[640,1024]{1,0:T(8,128)(2,1)S(1)}, bf16[640,1024]{1,0:T(8,128)(2,1)S(1)}, u32[]{:S(2)}, u32[]{:S(2)}) collective-permute-start(bf16[640,1024]{1,0:T(8,128)(2,1)S(1)} %copy-done.49), channel_id=1, source_target_pairs={{0,4},{4,0},{1,5},{5,1},{2,6},{6,2},{3,7},{7,3},{8,12},{12,8},{9,1... | collective-permute-start | bytes 3932168 | tf_op jit(solution)/shard_map/ppermute | solution.py:93
  467.2 29.5 %collective-permute-start.51 = (bf16[1024,640]{1,0:T(8,128)(2,1)}, bf16[1024,640]{1,0:T(8,128)(2,1)S(1)}, u32[]{:S(2)}, u32[]{:S(2)}) collective-permute-start(bf16[1024,640]{1,0:T(8,128)(2,1)} %copy-done.50), channel_id=1, source_target_pairs={{0,4},{4,0},{1,5},{5,1},{2,6},{6,2},{3,7},{7,3},{8,12},{12,8},{9,1... | collective-permute-start | bytes 3932168 | tf_op jit(solution)/shard_map/ppermute | solution.py:93
  467.2 41.6 %collective-permute-start.49 = (bf16[1024,640]{1,0:T(8,128)(2,1)S(1)}, bf16[1024,640]{1,0:T(8,128)(2,1)S(1)}, u32[]{:S(2)}, u32[]{:S(2)}) collective-permute-start(bf16[1024,640]{1,0:T(8,128)(2,1)S(1)} %copy-done.6), channel_id=1, source_target_pairs={{8,0},{16,24},{9,1},{17,25},{10,2},{18,26},{11,3},{19,27},{12,4},{... | collective-permute-start | bytes 3932168 | tf_op jit(solution)/shard_map/ppermute | solution.py:98
  468.5 40.3 %collective-permute-start.50 = (bf16[176,640]{1,0:T(8,128)(2,1)S(1)}, bf16[176,640]{1,0:T(8,128)(2,1)S(1)}, u32[]{:S(2)}, u32[]{:S(2)}) collective-permute-start(bf16[176,640]{1,0:T(8,128)(2,1)S(1)} %get-tuple-element.188.rest_1_.refs_2_), channel_id=1, source_target_pairs={{8,0},{16,24},{9,1},{17,25},{10,2},{18,26},{11,3},{19,27},{12,4},{... | collective-permute-start | bytes 675848 | tf_op jit(solution)/shard_map/ppermute | solution.py:98
  510.1 17.5 %collective-permute-start.56 = (bf16[768,2048]{1,0:T(8,128)(2,1)}, bf16[768,2048]{1,0:T(8,128)(2,1)}, u32[]{:S(2)}, u32[]{:S(2)}) collective-permute-start(bf16[768,2048]{1,0:T(8,128)(2,1)} %shard_map.351), channel_id=1, source_target_pairs={{0,4},{4,0},{1,5},{5,1},{2,6},{6,2},{3,7},{7,3},{8,12},{12,8},{9,1... | collective-permute-start | bytes 9437192 | tf_op jit(solution)/shard_map/ppermute | solution.py:93
  511.4 13.6 %collective-permute-start.54 = (bf16[1024,640]{1,0:T(8,128)(2,1)S(1)}, bf16[1024,640]{1,0:T(8,128)(2,1)S(1)}, u32[]{:S(2)}, u32[]{:S(2)}) collective-permute-start(bf16[1024,640]{1,0:T(8,128)(2,1)S(1)} %copy-done.14), channel_id=1, source_target_pairs={{0,4},{4,0},{1,5},{5,1},{2,6},{6,2},{3,7},{7,3},{8,12},{12,8},{9,1... | collective-permute-start | bytes 3932168 | tf_op jit(solution)/shard_map/ppermute | solution.py:93
  513.3 4.7 collective-permute-start.55
  (104 other events, 390.3 us)
Sparse Core Ops, SparseCore 0:
  10.9 152.4 all-gather.2
  166.8 133.5 all-gather.4
  303.4 42.8 reduce-scatter.2
  365.2 37.5 reduce-scatter.4
